TPU v7x, 32 devices: a whole 2x2x4 slice. The times are simulated.
32 devices in a mesh: alpha: 2 (over y), beta: 16 (over z, x, core).
Axes of the slice: x: 2, y: 2, z: 4, core: 2. Of those that a mesh axis runs over, the one named last changes fastest.
Arguments:
- ci_vectors: bfloat16 [8, 4096, 4096], P(None, 'alpha', 'beta'), may hold values from -6 to 6
- alpha_blocks: bfloat16 [32, 16, 128, 128], P('alpha'), may hold values from -0.125 to 0.125
- alpha_cols: int32 [32, 16], P('alpha'), may hold values from 0 to 31, all different within a row
- beta_blocks: bfloat16 [32, 16, 128, 128], P('beta'), may hold values from -0.125 to 0.125
- beta_cols: int32 [32, 16], P('beta'), may hold values from 0 to 31, all different within a row
- diagonal: float32 [4096, 4096], P('alpha', 'beta'), may hold values from -1 to 3
Outputs:
- sigma_vectors: bfloat16 [8, 4096, 4096], P(None, 'alpha', 'beta')
Inputs may be any that keep to these rules, and one draw needn't show every extreme that they name: `alpha_cols`: each block-row names 16 different block-columns. `beta_cols`: each block-row names 16 different block-columns.
All inputs are finite; a program needn't handle non-finite values.
Results may differ from a plain program's by a relative error of at most 0.001.
Values may be sent and summed in bfloat16 or wider, within the bound.
No kernel may reach another device: no remote copies, remote signals or barrier semaphores. Data moves between devices by JAX's collectives and lax.ppermute only.
A program may use at most 320 MiB of HBM per device.

v0:
```python
import jax
import jax.numpy as jnp
from jax import lax
from jax.sharding import PartitionSpec as P


def alpha_pass(ci_vectors, alpha_blocks, alpha_cols):
    vectors, rows_local, cols_local = ci_vectors.shape
    block = alpha_blocks.shape[-1]
    owned = alpha_blocks.shape[0]
    whole = lax.all_gather(ci_vectors, "alpha", axis=1, tiled=True)
    grid = whole.reshape(vectors, whole.shape[1] // block, block, cols_local)
    picked = grid[:, alpha_cols]
    term = jnp.einsum("rkij,vrkjb->vrib", alpha_blocks, picked, preferred_element_type=jnp.float32)
    return term.reshape(vectors, owned * block, cols_local)


def beta_pass(ci_vectors, beta_blocks, beta_cols):
    vectors, rows_local, cols_local = ci_vectors.shape
    block = beta_blocks.shape[-1]
    turned = lax.all_to_all(ci_vectors, "beta", split_axis=1, concat_axis=2, tiled=True)
    few_rows = turned.shape[1]
    all_cols = turned.shape[2]
    grid = turned.reshape(vectors, few_rows, all_cols // block, block)
    hb_piece = lax.all_gather(beta_blocks, "beta", axis=0, tiled=True)
    col_piece = lax.all_gather(beta_cols.astype(jnp.bfloat16), "beta", axis=0, tiled=True)
    columns = col_piece.astype(jnp.int32)
    count = hb_piece.shape[0]
    picked = grid[:, :, columns]
    term = jnp.einsum("vtnkj,nkij->vtni", picked, hb_piece, preferred_element_type=jnp.float32)
    updated = term.reshape(vectors, few_rows, count * block)
    return lax.all_to_all(updated, "beta", split_axis=2, concat_axis=1, tiled=True)


def shards(ci_vectors, alpha_blocks, alpha_cols, beta_blocks, beta_cols, diagonal):
    alpha_part = alpha_pass(ci_vectors, alpha_blocks, alpha_cols)
    beta_part = beta_pass(ci_vectors, beta_blocks, beta_cols)
    total = alpha_part + beta_part + diagonal[None, :, :] * ci_vectors.astype(jnp.float32)
    return total.astype(jnp.bfloat16)


def solution(mesh):
    placed = (
        P(None, "alpha", "beta"),
        P("alpha", None, None, None),
        P("alpha", None),
        P("beta", None, None, None),
        P("beta", None),
        P("alpha", "beta"),
    )
    return jax.shard_map(
        shards, mesh=mesh, in_specs=placed, out_specs=P(None, "alpha", "beta"), check_vma=False
    )
```

profile of v0, /device:TPU:11, one launch (start us, length us, event | category | flops | bytes accessed | tf_op | source)
XLA Modules:
  0.0 942.2 jit_solution(8841448934641731492)
XLA Ops:
  7.4 0.7 all-gather.6.cloned.1.call-update
  8.1 10.0 %copy.21 = bf16[8,2048,256]{2,0,1:T(8,128)(2,1)} copy(bf16[8,2048,256]{2,1,0:T(8,128)(2,1)} %param.6) | data formatting | bytes 16777216 | tf_op args[0]
  18.1 6.6 all-to-all-start
  24.7 0.0 copy-done.2
  24.7 288.7 %all-gather = bf16[16,2,16]{2,1,0:T(2,128)(2,1)S(1)} all-gather(bf16[1,2,16]{2,1,0:T(2,128)(2,1)S(1)} %convert_bitcast_fusion), channel_id=1, replica_groups=mesh['alpha'=2,'beta'=16] {'beta'}, dimensions={0}, use_global_device_ids=true | all-gather | bytes 1088 | tf_op jit(solution)/shard_map/all_gather | solution.py:26
  313.4 0.1 reshape.28
  313.5 0.0 all-to-all-done
  313.5 12.8 %copy.23 = bf16[8,128,16,256]{1,3,2,0:T(8,128)(2,1)} copy(bf16[8,128,16,256]{3,0,1,2:T(8,128)(2,1)} %bitcast.10) | data formatting | bytes 16777216 | tf_op jit(solution)/shard_map/all_to_all | solution.py:21
  326.3 12.0 %copy.24 = bf16[8,128,32,128]{3,1,2,0:T(8,128)(2,1)} copy(bf16[8,128,32,128]{1,3,2,0:T(8,128)(2,1)} %bitcast.57) | data formatting | bytes 16777216 | tf_op jit(solution)/shard_map/reshape | solution.py:24
  338.3 48.1 %gather_fusion.1 = bf16[512,8,128,128]{3,2,1,0:T(8,128)(2,1)} fusion(bf16[8,128,32,128]{3,1,2,0:T(8,128)(2,1)} %copy.24, s32[1024]{0:T(1024)S(1)} %pad_clamp_fusion), kind=kCustom, calls=%fused_computation.1 | custom fusion | bytes 268437504 | tf_op jit(solution)/shard_map/gather | solution.py:29
  386.4 61.1 %fusion.3 = f32[8,128,32,128]{1,3,0,2:T(8,128)} fusion(bf16[8,128,32,16,128]{4,1,0,3,2:T(8,128)(2,1)} %bitcast.16, bf16[32,16,128,128]{3,2,1,0:T(8,128)(2,1)} %all-gather.6.cloned.1.call-done), kind=kOutput, calls=%fused_computation.7 | convolution fusion | flops 17179869184 | bytes 167772160 | tf_op jit(solution)/shard_map/vtnkj,nkij->vtni/dot_general | solution.py:30
  447.4 6.5 copy.26
  454.0 23.6 %copy.27 = f32[8,128,4096]{1,0,2:T(8,128)} copy(f32[8,128,4096]{1,2,0:T(8,128)S(1)} %bitcast.56) | data formatting | bytes 33554432 | tf_op jit(solution)/shard_map/reshape | solution.py:31
  477.5 5.4 all-to-all-start.1
  482.9 0.3 all-gather.4.cloned.1.call-start
  483.2 0.3 all-gather.4.cloned.1.call-update
  483.5 0.1 reshape.20
  483.6 200.5 %all-gather.4.cloned.1.call-done = bf16[8,4096,256]{2,1,0:T(8,128)(2,1)} async-done(((bf16[8,2048,256]{2,1,0:T(8,128)(2,1)}), bf16[8,4096,256]{2,1,0:T(8,128)(2,1)}) %all-gather.4.cloned.1.call-update) | async-done | bytes 16777232 | tf_op jit(solution)/shard_map/all_gather | solution.py:11
  684.1 49.3 %gather_fusion = bf16[256,8,128,256]{3,2,1,0:T(8,128)(2,1)} fusion(bf16[8,32,128,256]{3,2,1,0:T(8,128)(2,1)} %bitcast.55, s32[1024]{0:T(1024)S(1)} %pad_clamp_fusion.1), kind=kCustom, calls=%fused_computation | custom fusion | bytes 268436480 | tf_op jit(solution)/shard_map/gather | solution.py:13
  733.4 112.6 %all-to-all-done.1 = f32[8,128,4096]{1,0,2:T(8,128)} async-done(((f32[8,128,4096]{1,0,2:T(8,128)}), f32[8,128,4096]{1,0,2:T(8,128)}, u32[]{:S(2)}, u32[]{:S(2)}) %all-to-all-start.1) | async-done | bytes 16777248 | tf_op jit(solution)/shard_map/all_to_all | solution.py:32
  846.0 17.6 %copy.29 = f32[8,128,16,256]{3,1,0,2:T(8,128)} copy(f32[8,128,16,256]{1,0,3,2:T(8,128)} %bitcast.23) | data formatting | bytes 33554432 | tf_op jit(solution)/shard_map/all_to_all | solution.py:32
  863.6 55.9 %bitcast_add_fusion = f32[8,16,128,256]{3,2,0,1:T(8,128)} fusion(f32[8,128,16,256]{3,1,0,2:T(8,128)} %copy.29, bf16[8,16,16,128,256]{4,3,0,2,1:T(8,128)(2,1)} %bitcast.2, bf16[16,16,128,128]{3,2,1,0:T(8,128)(2,1)} %param.7), kind=kOutput, calls=%fused_computation.4 | convolution fusion | flops 17184063488 | bytes 176160768 | tf_op jit(solution)/shard_map/rkij,vrkjb->vrib/dot_general | solution.py:14
  919.5 7.1 copy.30
  926.6 8.2 fusion.2
  (12 shorter events, 0.0 us)
Async XLA Ops:
  7.4 379.0 %all-gather.6.cloned.1.call-start = ((), (), s32[]{:S(2)}) async-start(), calls=%async_computation.3 | async-start | bytes 17825792 | tf_op jit(solution)/shard_map/all_gather | solution.py:25
  8.1 16.6 %copy-start.2 = (s32[2,16]{1,0:T(2,128)S(1)}, s32[2,16]{1,0:T(2,128)}, u32[]{:S(2)}) copy-start(s32[2,16]{1,0:T(2,128)} %param.10) | copy-start | bytes 388
  18.1 295.4 %all-to-all-start = ((bf16[8,2048,256]{2,0,1:T(8,128)(2,1)}), bf16[8,2048,256]{2,0,1:T(8,128)(2,1)}, u32[]{:S(2)}, u32[]{:S(2)}) async-start(bf16[8,2048,256]{2,0,1:T(8,128)(2,1)} %copy.21), calls=%async_computation | async-start | bytes 16777216 | tf_op jit(solution)/shard_map/all_to_all | solution.py:21
  477.5 5.9 copy-start.1
  477.5 368.4 %all-to-all-start.1 = ((f32[8,128,4096]{1,0,2:T(8,128)}), f32[8,128,4096]{1,0,2:T(8,128)}, u32[]{:S(2)}, u32[]{:S(2)}) async-start(f32[8,128,4096]{1,0,2:T(8,128)} %copy.27), calls=%async_computation.1 | async-start | bytes 33554432 | tf_op jit(solution)/shard_map/all_to_all | solution.py:32
  482.9 201.2 %all-gather.4.cloned.1.call-start = ((), (), s32[]{:S(2)}) async-start(), calls=%async_computation.2 | async-start | bytes 25165824 | tf_op jit(solution)/shard_map/all_gather | solution.py:11
  919.5 7.1 copy-start
Sparse Core Ops, SparseCore 0:
  10.4 259.1 all-gather.5
Sparse Core Ops, SparseCore 1:
  484.9 199.1 all-gather.3
where the time goes:
time: 943 us; the launch traced here: 942 us
  waiting for transfers between devices  314 us (33%)
  blocking collectives  289 us (31%)
  local copies, waits for them, and re-layouts  187 us (20%)
  matrix products  117 us (12%)
  between operations  14.9 us (2%)
  starting transfers between devices  12.2 us (1%)
    all_gather x1, blocking collectives, beta_pass(): lax.all_gather(beta_cols.astype(jnp.bfloat16), 'beta', axis=0, tiled=True)  289 us
    all_gather x1, waiting for transfers between devices, alpha_pass(): whole = lax.all_gather(ci_vectors, 'alpha', axis=1, tiled=True)  201 us
    all_to_all x1, waiting for transfers between devices, beta_pass(): lax.all_to_all(updated, 'beta', split_axis=2, concat_axis=1, tiled=True)  113 us
    dot_general x1, matrix products, beta_pass(): jnp.einsum('vtnkj,nkij->vtni', picked, hb_piece, preferred_element_type=j...  61.1 us
    dot_general x1, matrix products, alpha_pass(): jnp.einsum('rkij,vrkjb->vrib', alpha_blocks, picked, preferred_element_ty...  55.9 us
    gather x1, local copies, waits for them, and re-layouts, alpha_pass(): picked = grid[:, alpha_cols]  49.3 us
    gather x1, local copies, waits for them, and re-layouts, beta_pass(): picked = grid[:, :, columns]  48.1 us
    reshape x1, local copies, waits for them, and re-layouts, beta_pass(): updated = term.reshape(vectors, few_rows, count * block)  23.6 us
  transfers between devices with their start and end apart: 4, of which 2 were waited for; matrix products, arithmetic and copies ran while one was open for 14% of the time, Pallas kernels for 0%

commit v1 on v0

v1 whole, which is shorter than its diff:
```python
import functools

import jax
import jax.numpy as jnp
from jax import lax
from jax.experimental import pallas as pl
from jax.experimental.pallas import tpu as pltpu
from jax.sharding import PartitionSpec as P

MIB = 1 << 20
STEPS_PER_OCTAVE = 8
SHIFT = 1000
CODE_BITS = 11
LARGEST = 32767.0


def row_scale(code):
    return jnp.exp2((code - SHIFT).astype(jnp.float32) * (1.0 / STEPS_PER_OCTAVE))


def to_words(values):
    top = jnp.maximum(jnp.max(jnp.abs(values), axis=1, keepdims=True), 2.0 ** -100)
    code = jnp.ceil(jnp.log2(top) * STEPS_PER_OCTAVE + 0.01).astype(jnp.int32) + SHIFT
    words = jnp.round(values * (LARGEST / row_scale(code)))
    words = jnp.clip(words, -LARGEST, LARGEST).astype(jnp.int32)
    lane = lax.broadcasted_iota(jnp.int32, words.shape, 1)
    bit = lax.shift_right_logical(jnp.broadcast_to(code, words.shape), jnp.minimum(lane, CODE_BITS)) & 1
    return jnp.where(lane < CODE_BITS, (words & -2) | bit, words).astype(jnp.int16)


def from_words(words):
    words = words.astype(jnp.int32)
    head = words[:, :128]
    lane = lax.broadcasted_iota(jnp.int32, head.shape, 1)
    bits = jnp.where(lane < CODE_BITS, lax.shift_left(head & 1, jnp.minimum(lane, CODE_BITS)), 0)
    code = jnp.sum(bits.astype(jnp.float32), axis=1, keepdims=True).astype(jnp.int32)
    return words.astype(jnp.float32) * (row_scale(code) * (1.0 / LARGEST))


def beta_kernel(slots, cols_ref, turned_ref, blocks_ref, out_ref):
    dest = pl.program_id(0)
    sources, vectors, few_rows, strip = turned_ref.shape
    block = blocks_ref.shape[-1]
    per_strip = strip // block
    owned = per_strip
    parts = []
    for n in range(owned):
        picked = []
        for k in range(slots):
            c = cols_ref[(dest * owned + n) * slots + k]
            src = c // per_strip
            at = pl.multiple_of((c % per_strip) * block, block)
            tile = turned_ref[src, :, :, pl.ds(at, block)]
            picked.append(tile.reshape(vectors * few_rows, block))
        wide = jnp.concatenate(picked, axis=1)
        tall = blocks_ref[0, 0, n * slots * block : (n + 1) * slots * block, :]
        parts.append(jnp.dot(wide, tall, preferred_element_type=jnp.float32))
    term = jnp.concatenate(parts, axis=1) if owned > 1 else parts[0]
    out_ref[0] = to_words(term).reshape(vectors, few_rows, strip)


def beta_chunk(slots, columns, turned, blocks, first, count):
    sources, _, few_rows, strip = turned.shape
    inner, outer, depth, block = blocks.shape
    dests = inner * outer
    rows = count * few_rows
    return pl.pallas_call(
        functools.partial(beta_kernel, slots),
        grid_spec=pltpu.PrefetchScalarGridSpec(
            num_scalar_prefetch=1,
            grid=(dests,),
            in_specs=[
                pl.BlockSpec((sources, count, few_rows, strip), lambda p, _: (0, first // count, 0, 0)),
                pl.BlockSpec((1, 1, depth, block), lambda p, _: (p % inner, p // inner, 0, 0)),
            ],
            out_specs=pl.BlockSpec((1, count, few_rows, strip), lambda p, _: (p, 0, 0, 0)),
        ),
        out_shape=jax.ShapeDtypeStruct((dests, count, few_rows, strip), jnp.int16),
        compiler_params=pltpu.CompilerParams(vmem_limit_bytes=40 * MIB),
        cost_estimate=pl.CostEstimate(
            flops=4 * dests * rows * strip * slots * block,
            bytes_accessed=blocks.size * 2 + 2 * dests * rows * strip * 2,
            transcendentals=0,
        ),
        name="beta_term",
    )(columns, turned, blocks)


def alpha_kernel(cols_ref, whole_ref, own_ref, blocks_ref, diag_ref, out_ref):
    owned, slots, block, _ = blocks_ref.shape

    @pl.loop(0, owned)
    def _(r):
        picked = []
        for k in range(slots):
            at = pl.multiple_of(cols_ref[r * slots + k] * block, block)
            picked.append(whole_ref[0, pl.ds(at, block), :])
        tall = jnp.concatenate(picked, axis=0)
        wide = jnp.concatenate([blocks_ref[r, k] for k in range(slots)], axis=1)
        term = jnp.dot(wide, tall, preferred_element_type=jnp.float32)
        here = pl.ds(pl.multiple_of(r * block, block), block)
        out_ref[0, here, :] = term + diag_ref[here, :] * own_ref[0, here, :].astype(jnp.float32)


def alpha_term(columns, whole, own, blocks, diagonal):
    vectors, rows, strip = own.shape
    owned, slots, block, _ = blocks.shape
    once = pl.Buffered(1)
    return pl.pallas_call(
        alpha_kernel,
        grid_spec=pltpu.PrefetchScalarGridSpec(
            num_scalar_prefetch=1,
            grid=(vectors,),
            in_specs=[
                pl.BlockSpec((1, whole.shape[1], strip), lambda v, _: (v, 0, 0)),
                pl.BlockSpec((1, rows, strip), lambda v, _: (v, 0, 0)),
                pl.BlockSpec(blocks.shape, lambda v, _: (0, 0, 0, 0), pipeline_mode=once),
                pl.BlockSpec(diagonal.shape, lambda v, _: (0, 0), pipeline_mode=once),
            ],
            out_specs=pl.BlockSpec((1, rows, strip), lambda v, _: (v, 0, 0)),
        ),
        out_shape=jax.ShapeDtypeStruct((vectors, rows, strip), jnp.float32),
        compiler_params=pltpu.CompilerParams(vmem_limit_bytes=44 * MIB),
        cost_estimate=pl.CostEstimate(
            flops=6 * vectors * rows * strip * slots * block,
            bytes_accessed=whole.size * 2 + own.size * 6 + blocks.size * 2 + diagonal.size * 4,
            transcendentals=0,
        ),
        name="alpha_term",
    )(columns, whole, own, blocks, diagonal)


def join_kernel(acc_ref, words_ref, *rest):
    out_ref = rest[-1]
    sources, _, few_rows, strip = words_ref.shape
    for p in range(sources):
        here = pl.ds(p * few_rows, few_rows)
        out_ref[0, here, :] = (acc_ref[0, here, :] + from_words(words_ref[p, 0])).astype(jnp.bfloat16)


def join(acc, words, first, before):
    vectors, rows, strip = acc.shape
    sources, count, few_rows, _ = words.shape
    in_specs = [
        pl.BlockSpec((1, rows, strip), lambda v: (first + v, 0, 0)),
        pl.BlockSpec((sources, 1, few_rows, strip), lambda v: (0, v, 0, 0)),
    ]
    args = [acc, words]
    aliases = {}
    if before is not None:
        in_specs.append(pl.BlockSpec(memory_space=pl.ANY))
        args.append(before)
        aliases = {2: 0}
    return pl.pallas_call(
        join_kernel,
        grid=(count,),
        in_specs=in_specs,
        out_specs=pl.BlockSpec((1, rows, strip), lambda v: (first + v, 0, 0)),
        out_shape=jax.ShapeDtypeStruct((vectors, rows, strip), jnp.bfloat16),
        input_output_aliases=aliases,
        compiler_params=pltpu.CompilerParams(vmem_limit_bytes=32 * MIB),
        cost_estimate=pl.CostEstimate(
            flops=8 * count * rows * strip, bytes_accessed=8 * count * rows * strip, transcendentals=0
        ),
        name="join_terms",
    )(*args)


def gather_beta(beta_blocks, beta_cols, ring):
    owned, slots, block, _ = beta_blocks.shape
    outer = 4 if ring % 4 == 0 else 1
    inner = ring // outer
    turned = beta_blocks.transpose(0, 1, 3, 2).reshape(owned * slots * block, block)
    heads = jnp.pad(beta_cols.reshape(1, owned * slots).astype(jnp.bfloat16), ((0, 15), (0, block - owned * slots)))
    message = jnp.concatenate([turned, heads], axis=0)
    far = [[o * inner + i for o in range(outer)] for i in range(inner)]
    near = [[o * inner + i for i in range(inner)] for o in range(outer)]
    message = lax.all_gather(message, "beta", axis=0, tiled=False, axis_index_groups=far)
    message = lax.all_gather(message, "beta", axis=0, tiled=False, axis_index_groups=near)
    return message, inner, outer


def shards(ring, ci_vectors, alpha_blocks, alpha_cols, beta_blocks, beta_cols, diagonal):
    vectors, rows, strip = ci_vectors.shape
    few_rows = rows // ring
    owned, slots, block, _ = beta_blocks.shape
    count = 2
    half = vectors // 2

    message, inner, outer = gather_beta(beta_blocks, beta_cols, ring)
    body = owned * slots * block
    columns = message[:, :, body, : owned * slots].transpose(1, 0, 2).reshape(-1).astype(jnp.int32)

    turned = []
    for h in range(0, vectors, half):
        piece = ci_vectors[h : h + half].reshape(half, ring, few_rows, strip).transpose(1, 0, 2, 3)
        turned.append(lax.all_to_all(piece, "beta", split_axis=0, concat_axis=0, tiled=True))

    whole = lax.all_gather(ci_vectors, "alpha", axis=1, tiled=True)

    words = []
    for first in range(0, vectors, count):
        term = beta_chunk(slots, columns, turned[first // half], message, first % half, count)
        words.append(lax.all_to_all(term, "beta", split_axis=0, concat_axis=0, tiled=True))

    acc = alpha_term(alpha_cols.reshape(-1), whole, ci_vectors, alpha_blocks, diagonal)
    total = None
    for i, first in enumerate(range(0, vectors, count)):
        total = join(acc, words[i], first, total)
    return total


def solution(mesh):
    placed = (
        P(None, "alpha", "beta"),
        P("alpha", None, None, None),
        P("alpha", None),
        P("beta", None, None, None),
        P("beta", None),
        P("alpha", "beta"),
    )
    return jax.shard_map(
        functools.partial(shards, mesh.shape["beta"]),
        mesh=mesh,
        in_specs=placed,
        out_specs=P(None, "alpha", "beta"),
        check_vma=False,
    )
```

time: 943 us -> 573 us (0.61)
  blocking collectives: 289 us -> 0 us
  local copies, waits for them, and re-layouts: 187 us -> 33 us
  Pallas kernels: 0 us -> 139 us
  matrix products: 117 us -> 0 us
  waiting for transfers between devices: 314 us -> 344 us
  starting transfers between devices: 12.2 us -> 38.4 us
    all_gather x1 -> x0, blocking collectives: 289 us -> none  [beta_pass(): lax.all_gather(beta_cols.astype(jnp.bfloat16), 'beta', axis=0, tiled=True)]
    pallas_call x0 -> x9, Pallas kernels: none -> 139 us  [the longest x4 78.8 us: beta_chunk(): pl.pallas_call(functools.partial(beta_kernel, slots), grid_spec=pltpu.Pre...]
    dot_general x2 -> x0, matrix products: 117 us -> none  [the longest x1 61.1 us: beta_pass(): jnp.einsum('vtnkj,nkij->vtni', picked, hb_piece, preferred_element_type=j...]
    gather x2 -> x0, local copies, waits for them, and re-layouts: 97.3 us -> none  [the longest x1 49.3 us: alpha_pass(): picked = grid[:, alpha_cols]]
    all_to_all x2 -> x6, waiting for transfers between devices: 113 us -> 168 us  [the longest x2 87.6 us: shards(): lax.all_to_all(piece, 'beta', split_axis=0, concat_axis=0, tiled=True)]
    all_to_all x2 -> x0, local copies, waits for them, and re-layouts: 30.4 us -> none  [the longest x1 17.6 us: beta_pass(): lax.all_to_all(updated, 'beta', split_axis=2, concat_axis=1, tiled=True)]
    reshape x2 -> x3, local copies, waits for them, and re-layouts: 35.5 us -> 7.72 us  [the longest x2 7.64 us: shards(): ci_vectors[h:h + half].reshape(half, ring, few_rows, strip)]
    all_to_all x2 -> x6, starting transfers between devices: 11.9 us -> 38.3 us  [the longest x4 25.9 us: shards(): lax.all_to_all(term, 'beta', split_axis=0, concat_axis=0, tiled=True)]
  transfers between devices with their start and end apart: 4 -> 9, of which waited for: 2 -> 7; matrix products, arithmetic and copies ran while one was open for 14% -> 2% of each run, Pallas kernels for 0% -> 24%
where the time goes in v1:
time: 573 us; the launch traced here: 570 us
  waiting for transfers between devices  344 us (60%)
  Pallas kernels  139 us (24%)
  starting transfers between devices  38.4 us (7%)
  local copies, waits for them, and re-layouts  33 us (6%)
  between operations  13.2 us (2%)
    all_to_all x2, waiting for transfers between devices, shards(): lax.all_to_all(piece, 'beta', split_axis=0, concat_axis=0, tiled=True)  87.6 us
    all_to_all x4, waiting for transfers between devices, shards(): lax.all_to_all(term, 'beta', split_axis=0, concat_axis=0, tiled=True)  80.9 us
    all_gather x1, waiting for transfers between devices, gather_beta(): lax.all_gather(message, 'beta', axis=0, tiled=False, axis_index_groups=near)  80.2 us
    all_gather x1, waiting for transfers between devices, gather_beta(): lax.all_gather(message, 'beta', axis=0, tiled=False, axis_index_groups=far)  79.8 us
    pallas_call x4, Pallas kernels, beta_chunk(): pl.pallas_call(functools.partial(beta_kernel, slots), grid_spec=pltpu.Pre...  78.8 us
    pallas_call x1, Pallas kernels, alpha_term(): pl.pallas_call(alpha_kernel, grid_spec=pltpu.PrefetchScalarGridSpec(num_s...  46.3 us
    all_to_all x4, starting transfers between devices, shards(): lax.all_to_all(term, 'beta', split_axis=0, concat_axis=0, tiled=True)  25.9 us
    unnamed x17, local copies, waits for them, and re-layouts  20.1 us
  transfers between devices with their start and end apart: 9, of which 7 were waited for; matrix products, arithmetic and copies ran while one was open for 2% of the time, Pallas kernels for 24%

profile of v1, /device:TPU:11, one launch (start us, length us, event | category | flops | bytes accessed | tf_op | source)
XLA Modules:
  0.0 569.5 jit_solution(12142110612564267755)
XLA Ops:
  10.0 79.8 %all-gather.8.cloned.1.call-done = bf16[16448,128]{1,0:T(8,128)(2,1)} async-done(((bf16[4112,128]{1,0:T(8,128)(2,1)}), bf16[16448,128]{1,0:T(8,128)(2,1)}) %all-gather.8.cloned.1.call-update) | async-done | bytes 4210704 | tf_op jit(solution)/shard_map/all_gather | solution.py:178
  89.9 5.1 fusion.2
  97.2 7.8 %all-to-all-start.3 = ((bf16[16,4,128,256]{3,2,1,0:T(8,128)(2,1)}), bf16[16,4,128,256]{3,2,1,0:T(8,128)(2,1)}, u32[]{:S(2)}, u32[]{:S(2)}) async-start(bf16[16,4,128,256]{3,2,1,0:T(8,128)(2,1)} %bitcast.17), calls=%async_computation.3 | async-start | bytes 8388608 | tf_op jit(solution)/shard_map/all_to_all | solution.py:197
  105.0 5.4 copy.21
  110.4 87.6 %all-to-all-done.3.turned_ref = bf16[16,4,128,256]{3,2,1,0:T(8,128)(2,1)} async-done(((bf16[16,4,128,256]{3,2,1,0:T(8,128)(2,1)}), bf16[16,4,128,256]{3,2,1,0:T(8,128)(2,1)}, u32[]{:S(2)}, u32[]{:S(2)}) %all-to-all-start.3) | async-done | bytes 4194336 | tf_op jit(solution)/shard_map/all_to_all | solution.py:197
  198.0 4.6 all-to-all-start
  203.3 80.2 %all-gather.10.cloned.1.call-done = bf16[16,4112,128]{2,1,0:T(8,128)(2,1)} async-done(((bf16[4,4112,128]{2,1,0:T(8,128)(2,1)}), bf16[16,4112,128]{2,1,0:T(8,128)(2,1)}) %all-gather.10.cloned.1.call-update) | async-done | bytes 16842768 | tf_op jit(solution)/shard_map/all_gather | solution.py:179
  284.4 20.4 %beta_term.6 = s16[16,2,128,256]{3,2,1,0:T(8,128)(2,1)S(1)} custom-call(s32[512]{0:T(512)S(1)} %reshape.35.cols_ref, bf16[16,4,128,256]{3,2,1,0:T(8,128)(2,1)} %all-to-all-done.3.turned_ref, bf16[4,4,4112,128]{3,2,1,0:T(8,128)(2,1)} %bitcast.24), custom_call_target="tpu_custom_call" | custom-call | flops 8589934592 | bytes 21037056 | tf_op jit(solution)/shard_map/beta_term/pallas_call | solution.py:67
  306.1 12.2 %all-to-all-start.4 = ((s16[16,2,128,256]{3,2,1,0:T(8,128)(2,1)}), s16[16,2,128,256]{3,2,1,0:T(8,128)(2,1)S(1)}, u32[]{:S(2)}, u32[]{:S(2)}) async-start(s16[16,2,128,256]{3,2,1,0:T(8,128)(2,1)} %copy-done.4), calls=%async_computation.4 | async-start | bytes 4194304 | tf_op jit(solution)/shard_map/all_to_all | solution.py:204
  318.3 19.6 %beta_term.7 = s16[16,2,128,256]{3,2,1,0:T(8,128)(2,1)S(1)} custom-call(s32[512]{0:T(512)S(1)} %reshape.35.cols_ref, bf16[16,4,128,256]{3,2,1,0:T(8,128)(2,1)} %all-to-all-done.3.turned_ref, bf16[4,4,4112,128]{3,2,1,0:T(8,128)(2,1)} %bitcast.25), custom_call_target="tpu_custom_call" | custom-call | flops 8589934592 | bytes 21037056 | tf_op jit(solution)/shard_map/beta_term/pallas_call | solution.py:67
  339.3 26.8 %all-to-all-done.4.words_ref = s16[16,2,128,256]{3,2,1,0:T(8,128)(2,1)S(1)} async-done(((s16[16,2,128,256]{3,2,1,0:T(8,128)(2,1)}), s16[16,2,128,256]{3,2,1,0:T(8,128)(2,1)S(1)}, u32[]{:S(2)}, u32[]{:S(2)}) %all-to-all-start.4) | async-done | bytes 2097184 | tf_op jit(solution)/shard_map/all_to_all | solution.py:204
  366.1 4.5 all-to-all-start.5
  370.6 19.4 %beta_term.5 = s16[16,2,128,256]{3,2,1,0:T(8,128)(2,1)S(1)} custom-call(s32[512]{0:T(512)S(1)} %reshape.35.cols_ref, bf16[16,4,128,256]{3,2,1,0:T(8,128)(2,1)} %all-to-all-done.turned_ref, bf16[4,4,4112,128]{3,2,1,0:T(8,128)(2,1)} %bitcast.26), custom_call_target="tpu_custom_call" | custom-call | flops 8589934592 | bytes 21037056 | tf_op jit(solution)/shard_map/beta_term/pallas_call | solution.py:67
  391.3 27.1 %all-to-all-done.5.words_ref = s16[16,2,128,256]{3,2,1,0:T(8,128)(2,1)} async-done(((s16[16,2,128,256]{3,2,1,0:T(8,128)(2,1)}), s16[16,2,128,256]{3,2,1,0:T(8,128)(2,1)}, u32[]{:S(2)}, u32[]{:S(2)}) %all-to-all-start.5) | async-done | bytes 2097184 | tf_op jit(solution)/shard_map/all_to_all | solution.py:204
  418.5 4.6 all-to-all-start.2
  423.2 19.4 %beta_term.4 = s16[16,2,128,256]{3,2,1,0:T(8,128)(2,1)S(1)} custom-call(s32[512]{0:T(512)S(1)} %reshape.35.cols_ref, bf16[16,4,128,256]{3,2,1,0:T(8,128)(2,1)} %all-to-all-done.turned_ref, bf16[4,4,4112,128]{3,2,1,0:T(8,128)(2,1)} %bitcast.27), custom_call_target="tpu_custom_call" | custom-call | flops 8589934592 | bytes 21037056 | tf_op jit(solution)/shard_map/beta_term/pallas_call | solution.py:67
  443.9 27.0 %all-to-all-done.2.words_ref = s16[16,2,128,256]{3,2,1,0:T(8,128)(2,1)} async-done(((s16[16,2,128,256]{3,2,1,0:T(8,128)(2,1)}), s16[16,2,128,256]{3,2,1,0:T(8,128)(2,1)}, u32[]{:S(2)}, u32[]{:S(2)}) %all-to-all-start.2) | async-done | bytes 2097184 | tf_op jit(solution)/shard_map/all_to_all | solution.py:204
  470.9 4.6 all-to-all-start.1
  475.5 14.7 %all-gather.6.cloned.1.call-done.whole_ref = bf16[8,4096,256]{2,1,0:T(8,128)(2,1)} async-done(((bf16[8,2048,256]{2,1,0:T(8,128)(2,1)}), bf16[8,4096,256]{2,1,0:T(8,128)(2,1)}) %all-gather.6.cloned.1.call-update) | async-done | bytes 16777232 | tf_op jit(solution)/shard_map/all_gather | solution.py:199
  491.8 46.3 %alpha_term.1.acc_ref = f32[8,2048,256]{2,1,0:T(8,128)} custom-call(s32[256]{0:T(256)S(1)} %reshape.31.cols_ref, bf16[8,4096,256]{2,1,0:T(8,128)(2,1)} %all-gather.6.cloned.1.call-done.whole_ref, bf16[8,2048,256]{2,1,0:T(8,128)(2,1)} %own_ref.1, bf16[16,16,128,128]{3,2,1,0:T(8,128)(2,1)} %blocks_ref.1, f32[2048,256]{1,0:T(8,128)S(1)} %copy-done.6), custom_call_target="tpu_custom_call" | custom-call | flops 51539607552 | bytes 52428800 | tf_op jit(solution)/shard_map/alpha_term/pallas_call | solution.py:109
  538.0 5.8 %copy-done = f32[8,2048,256]{2,1,0:T(8,128)S(1)} copy-done((f32[8,2048,256]{2,1,0:T(8,128)S(1)}, f32[8,2048,256]{2,1,0:T(8,128)}, u32[]{:S(2)}) %copy-start) | copy-done | bytes 16777240
  550.0 3.6 join_terms.6.rest_0_
  553.6 5.8 %copy-done.1 = f32[8,2048,256]{2,1,0:T(8,128)S(1)} copy-done((f32[8,2048,256]{2,1,0:T(8,128)S(1)}, f32[8,2048,256]{2,1,0:T(8,128)}, u32[]{:S(2)}) %copy-start.1) | copy-done | bytes 16777240
  559.4 3.6 join_terms.7
  (33 shorter events, 20.5 us)
Async XLA Ops:
  6.5 83.3 %all-gather.8.cloned.1.call-start = ((), (), s32[]{:S(2)}) async-start(), calls=%async_computation.7 | async-start | bytes 5263360 | tf_op jit(solution)/shard_map/all_gather | solution.py:178
  10.0 273.5 %all-gather.10.cloned.1.call-start = ((), (), s32[]{:S(2)}) async-start(), calls=%async_computation.8 | async-start | bytes 21053440 | tf_op jit(solution)/shard_map/all_gather | solution.py:179
  97.2 100.7 %all-to-all-start.3 = ((bf16[16,4,128,256]{3,2,1,0:T(8,128)(2,1)}), bf16[16,4,128,256]{3,2,1,0:T(8,128)(2,1)}, u32[]{:S(2)}, u32[]{:S(2)}) async-start(bf16[16,4,128,256]{3,2,1,0:T(8,128)(2,1)} %bitcast.17), calls=%async_computation.3 | async-start | bytes 8388608 | tf_op jit(solution)/shard_map/all_to_all | solution.py:197
  198.0 108.2 %all-to-all-start = ((bf16[16,4,128,256]{3,2,1,0:T(8,128)(2,1)}), bf16[16,4,128,256]{3,2,1,0:T(8,128)(2,1)}, u32[]{:S(2)}, u32[]{:S(2)}) async-start(bf16[16,4,128,256]{3,2,1,0:T(8,128)(2,1)} %bitcast.16), calls=%async_computation | async-start | bytes 8388608 | tf_op jit(solution)/shard_map/all_to_all | solution.py:197
  202.6 287.6 %all-gather.6.cloned.1.call-start = ((), (), s32[]{:S(2)}) async-start(), calls=%async_computation.6 | async-start | bytes 25165824 | tf_op jit(solution)/shard_map/all_gather | solution.py:199
  304.8 1.3 copy-start.4
  306.1 60.0 %all-to-all-start.4 = ((s16[16,2,128,256]{3,2,1,0:T(8,128)(2,1)}), s16[16,2,128,256]{3,2,1,0:T(8,128)(2,1)S(1)}, u32[]{:S(2)}, u32[]{:S(2)}) async-start(s16[16,2,128,256]{3,2,1,0:T(8,128)(2,1)} %copy-done.4), calls=%async_computation.4 | async-start | bytes 4194304 | tf_op jit(solution)/shard_map/all_to_all | solution.py:204
  338.0 1.3 copy-start.5
  366.1 52.3 %all-to-all-start.5 = ((s16[16,2,128,256]{3,2,1,0:T(8,128)(2,1)}), s16[16,2,128,256]{3,2,1,0:T(8,128)(2,1)}, u32[]{:S(2)}, u32[]{:S(2)}) async-start(s16[16,2,128,256]{3,2,1,0:T(8,128)(2,1)} %copy-done.5), calls=%async_computation.5 | async-start | bytes 4194304 | tf_op jit(solution)/shard_map/all_to_all | solution.py:204
  390.0 1.3 copy-start.3
  391.3 31.7 %copy-start.7 = (s32[16,16]{1,0:T(8,128)S(1)}, s32[16,16]{1,0:T(8,128)}, u32[]{:S(2)}) copy-start(s32[16,16]{1,0:T(8,128)} %param.8) | copy-start | bytes 3076
  418.5 52.4 %all-to-all-start.2 = ((s16[16,2,128,256]{3,2,1,0:T(8,128)(2,1)}), s16[16,2,128,256]{3,2,1,0:T(8,128)(2,1)}, u32[]{:S(2)}, u32[]{:S(2)}) async-start(s16[16,2,128,256]{3,2,1,0:T(8,128)(2,1)} %copy-done.3), calls=%async_computation.2 | async-start | bytes 4194304 | tf_op jit(solution)/shard_map/all_to_all | solution.py:204
  442.6 1.4 copy-start.2
  470.9 82.7 %all-to-all-start.1 = ((s16[16,2,128,256]{3,2,1,0:T(8,128)(2,1)}), s16[16,2,128,256]{3,2,1,0:T(8,128)(2,1)}, u32[]{:S(2)}, u32[]{:S(2)}) async-start(s16[16,2,128,256]{3,2,1,0:T(8,128)(2,1)} %copy-done.2), calls=%async_computation.1 | async-start | bytes 4194304 | tf_op jit(solution)/shard_map/all_to_all | solution.py:204
  490.2 1.6 copy-start.6
  538.0 5.8 %copy-start = (f32[8,2048,256]{2,1,0:T(8,128)S(1)}, f32[8,2048,256]{2,1,0:T(8,128)}, u32[]{:S(2)}) copy-start(f32[8,2048,256]{2,1,0:T(8,128)} %alpha_term.1.acc_ref) | copy-start | bytes 50331652
  553.6 5.8 %copy-start.1 = (f32[8,2048,256]{2,1,0:T(8,128)S(1)}, f32[8,2048,256]{2,1,0:T(8,128)}, u32[]{:S(2)}) copy-start(f32[8,2048,256]{2,1,0:T(8,128)} %alpha_term.1.acc_ref) | copy-start | bytes 50331652
Sparse Core Ops, SparseCore 0:
  10.1 79.7 all-gather.7
  91.4 192.0 all-gather.9
  285.1 205.0 all-gather.5

commit v2 on v1

v2 whole, which is shorter than its diff:
```python
import functools
import math

import jax
import jax.numpy as jnp
from jax import lax
from jax.experimental import pallas as pl
from jax.experimental.pallas import tpu as pltpu
from jax.sharding import PartitionSpec as P

MIB = 1 << 20
STEPS_PER_OCTAVE = 8
SHIFT = 1000
CODE_BITS = 11
LARGEST = 32767.0
TILE = 16
CORES = 2
ANYWHERE = pl.BlockSpec(memory_space=pl.ANY)


def row_scale(code):
    return jnp.exp2((code - SHIFT).astype(jnp.float32) * (1.0 / STEPS_PER_OCTAVE))


def to_words(values):
    top = jnp.maximum(jnp.max(jnp.abs(values), axis=1, keepdims=True), 2.0 ** -100)
    code = jnp.ceil(jnp.log2(top) * STEPS_PER_OCTAVE + 0.01).astype(jnp.int32) + SHIFT
    words = jnp.round(values * (LARGEST / row_scale(code))).astype(jnp.int32)
    head = words[:, :128]
    lane = lax.broadcasted_iota(jnp.int32, head.shape, 1)
    bit = lax.shift_right_logical(jnp.broadcast_to(code, head.shape), jnp.minimum(lane, CODE_BITS)) & 1
    head = jnp.where(lane < CODE_BITS, (head & -2) | bit, head)
    if words.shape[1] > 128:
        head = jnp.concatenate([head, words[:, 128:]], axis=1)
    return head.astype(jnp.int16)


def from_words(words):
    words = words.astype(jnp.int32)
    head = words[:, :128]
    lane = lax.broadcasted_iota(jnp.int32, head.shape, 1)
    bits = jnp.where(lane < CODE_BITS, lax.shift_left(head & 1, jnp.minimum(lane, CODE_BITS)), 0)
    code = jnp.sum(bits.astype(jnp.float32), axis=1, keepdims=True).astype(jnp.int32)
    return words.astype(jnp.float32) * (row_scale(code) * (1.0 / LARGEST))


def pack_kernel(first, count, few_rows, *refs):
    source_ref, out_ref, sem = refs[0], refs[-2], refs[-1]
    dests = out_ref.shape[0]

    def copy(d, v):
        return pltpu.make_async_copy(
            source_ref.at[first + v, pl.ds(d * few_rows, few_rows)],
            out_ref.at[d, pl.ds(v * few_rows, few_rows)],
            sem.at[d, v],
        )

    def head(d):
        return pltpu.make_async_copy(refs[1], out_ref.at[d, pl.ds(count * few_rows, TILE)], sem.at[d, count])

    def all_of(act):
        for d in range(dests):
            for v in range(count):
                act(copy(d, v))
            if len(refs) == 4:
                act(head(d))

    all_of(lambda c: c.start())
    all_of(lambda c: c.wait())


def pack(ci_vectors, heads, first, count, ring):
    _, rows, strip = ci_vectors.shape
    few_rows = rows // ring
    depth = count * few_rows + (0 if heads is None else TILE)
    args = (ci_vectors,) if heads is None else (ci_vectors, heads)
    return pl.pallas_call(
        functools.partial(pack_kernel, first, count, few_rows),
        in_specs=[ANYWHERE] * len(args),
        out_specs=ANYWHERE,
        out_shape=jax.ShapeDtypeStruct((ring, depth, strip), jnp.bfloat16),
        scratch_shapes=[pltpu.SemaphoreType.DMA((ring, count + 1))],
        cost_estimate=pl.CostEstimate(flops=0, bytes_accessed=4 * ring * depth * strip, transcendentals=0),
        name="pack_pieces",
    )(*args)


def beta_kernel(slots, xs, cols_ref, place_ref, *refs):
    own_ref, twin_ref = refs[:2]
    message_refs = refs[2:-5]
    out_ref, picked_ref, blocks_ref, picked_sem, blocks_sem = refs[-5:]
    block = blocks_ref.shape[-1]
    sources = own_ref.shape[0]
    per_strip = own_ref.shape[2] // block
    _, both_rows, _ = picked_ref.shape
    rows = both_rows // CORES
    half = blocks_ref.shape[1] // 2
    outer = message_refs[0].shape[0]
    dest, tile = pl.program_id(0), pl.program_id(1)
    core, x_here, parity = place_ref[0], place_ref[1], place_ref[2]

    @pl.when((dest == 0) & (tile == 0))
    def _():
        for which, ref in enumerate((own_ref, twin_ref)):
            at = pl.multiple_of((core ^ which) * rows, rows)
            for src in range(sources):
                for s in range(per_strip):
                    pltpu.make_async_copy(
                        ref.at[src, pl.ds(0, rows), pl.ds(s * block, block)],
                        picked_ref.at[src * per_strip + s, pl.ds(at, rows)],
                        picked_sem,
                    ).start()
        for z in range(outer):
            for q in range(xs):
                for r in range(2):
                    d = z * xs + (x_here ^ q)
                    at = pl.multiple_of((parity ^ r) * half, half)
                    pltpu.make_async_copy(
                        message_refs[q * 2 + r].at[z], blocks_ref.at[d, pl.ds(at, half)], blocks_sem.at[d]
                    ).start()
        pltpu.make_async_copy(picked_ref, picked_ref, picked_sem).wait()

    @pl.when(tile == 0)
    def _():
        pltpu.make_async_copy(blocks_ref.at[dest], blocks_ref.at[dest], blocks_sem.at[dest]).wait()

    size = out_ref.shape[1]
    here = pl.ds(pl.multiple_of(tile * size, size), size)
    strip = dest * CORES + core
    parts = []
    for n in range(per_strip):
        wide = jnp.concatenate(
            [picked_ref[cols_ref[(strip * per_strip + n) * slots + k], here, :] for k in range(slots)], axis=1
        )
        tall = blocks_ref[dest, n * slots * block : (n + 1) * slots * block, :]
        parts.append(jnp.dot(wide, tall, preferred_element_type=jnp.float32))
    term = jnp.concatenate(parts, axis=1) if per_strip > 1 else parts[0]
    out_ref[0] = to_words(term)


def beta_term(slots, xs, columns, place, own, twin, messages, rows):
    sources, _, strip = own.shape
    outer, half, block = messages[0].shape
    dests = outer * xs
    both = rows * CORES
    size = math.gcd(both, 512)
    count = sources * strip // block
    return pl.pallas_call(
        functools.partial(beta_kernel, slots, xs),
        grid_spec=pltpu.PrefetchScalarGridSpec(
            num_scalar_prefetch=2,
            grid=(dests, both // size),
            in_specs=[ANYWHERE] * (2 + len(messages)),
            out_specs=pl.BlockSpec((1, size, strip), lambda d, m, *_: (d, m, 0)),
            scratch_shapes=[
                pltpu.VMEM((count, both, block), jnp.bfloat16),
                pltpu.VMEM((dests, 2 * half, block), jnp.bfloat16),
                pltpu.SemaphoreType.DMA,
                pltpu.SemaphoreType.DMA((dests,)),
            ],
        ),
        out_shape=jax.ShapeDtypeStruct((dests, both, strip), jnp.int16),
        compiler_params=pltpu.CompilerParams(vmem_limit_bytes=44 * MIB),
        cost_estimate=pl.CostEstimate(
            flops=4 * dests * both * strip * slots * block,
            bytes_accessed=8 * half * block * dests + 4 * count * both * block,
            transcendentals=0,
        ),
        name="beta_term",
    )(columns, place, own, twin, *messages)


def alpha_kernel(pieces, cols_ref, place_ref, *refs):
    blocks_ref, diag_ref, out_ref, whole_ref = refs[pieces:]
    own_ref = refs[0]
    owned, slots, block, _ = blocks_ref.shape
    rows = own_ref.shape[1]
    for s in range(pieces):
        at = pl.multiple_of(lax.rem(place_ref[3] + s, pieces) * rows, rows)
        whole_ref[pl.ds(at, rows), :] = refs[s][0]

    @pl.loop(0, owned)
    def _(r):
        picked = []
        for k in range(slots):
            at = pl.multiple_of(cols_ref[r * slots + k] * block, block)
            picked.append(whole_ref[pl.ds(at, block), :])
        tall = jnp.concatenate(picked, axis=0)
        wide = jnp.concatenate([blocks_ref[r, k] for k in range(slots)], axis=1)
        term = jnp.dot(wide, tall, preferred_element_type=jnp.float32)
        here = pl.ds(pl.multiple_of(r * block, block), block)
        out_ref[0, here, :] = term + diag_ref[here, :] * own_ref[0, here, :].astype(jnp.float32)


def alpha_term(columns, place, own, others, blocks, diagonal, first):
    count, rows, strip = others[0].shape if others else own.shape
    owned, slots, block, _ = blocks.shape
    pieces = 1 + len(others)
    once = pl.Buffered(1)
    return pl.pallas_call(
        functools.partial(alpha_kernel, pieces),
        grid_spec=pltpu.PrefetchScalarGridSpec(
            num_scalar_prefetch=2,
            grid=(count,),
            in_specs=[pl.BlockSpec((1, rows, strip), lambda v, *_: (first + v, 0, 0))]
            + [pl.BlockSpec((1, rows, strip), lambda v, *_: (v, 0, 0))] * len(others)
            + [
                pl.BlockSpec(blocks.shape, lambda v, *_: (0, 0, 0, 0), pipeline_mode=once),
                pl.BlockSpec(diagonal.shape, lambda v, *_: (0, 0), pipeline_mode=once),
            ],
            out_specs=pl.BlockSpec((1, rows, strip), lambda v, *_: (v, 0, 0)),
            scratch_shapes=[pltpu.VMEM((pieces * rows, strip), jnp.bfloat16)],
        ),
        out_shape=jax.ShapeDtypeStruct((count, rows, strip), jnp.float32),
        compiler_params=pltpu.CompilerParams(vmem_limit_bytes=44 * MIB),
        cost_estimate=pl.CostEstimate(
            flops=6 * count * rows * strip * slots * block,
            bytes_accessed=count * rows * strip * (2 * pieces + 4) + blocks.size * 2 + diagonal.size * 4,
            transcendentals=0,
        ),
        name="alpha_term",
    )(columns, place, own, *others, blocks, diagonal)


def join_kernel(few_rows, acc_ref, words_ref, *rest):
    out_ref = rest[-1]
    for j in range(words_ref.shape[0]):
        for c in range(CORES):
            here = pl.ds((j * CORES + c) * few_rows, few_rows)
            out_ref[0, here, :] = (acc_ref[0, here, :] + from_words(words_ref[j, c, 0])).astype(jnp.bfloat16)


def join(acc, words, first, vectors, before):
    count, rows, strip = acc.shape
    sources = words.shape[0]
    few_rows = rows // (sources * CORES)
    words = words.reshape(sources, CORES, count, few_rows, strip)
    in_specs = [
        pl.BlockSpec((1, rows, strip), lambda v: (v, 0, 0)),
        pl.BlockSpec((sources, CORES, 1, few_rows, strip), lambda v: (0, 0, v, 0, 0)),
    ]
    args = [acc, words]
    aliases = {}
    if before is not None:
        in_specs.append(ANYWHERE)
        args.append(before)
        aliases = {2: 0}
    return pl.pallas_call(
        functools.partial(join_kernel, few_rows),
        grid=(count,),
        in_specs=in_specs,
        out_specs=pl.BlockSpec((1, rows, strip), lambda v: (first + v, 0, 0)),
        out_shape=jax.ShapeDtypeStruct((vectors, rows, strip), jnp.bfloat16),
        input_output_aliases=aliases,
        compiler_params=pltpu.CompilerParams(vmem_limit_bytes=32 * MIB),
        cost_estimate=pl.CostEstimate(
            flops=8 * count * rows * strip, bytes_accessed=8 * count * rows * strip, transcendentals=0
        ),
        name="join_terms",
    )(*args)


def after(value, earlier):
    return lax.optimization_barrier((value, earlier))[0]


def shards(ring, ring_a, ci_vectors, alpha_blocks, alpha_cols, beta_blocks, beta_cols, diagonal):
    vectors, rows, strip = ci_vectors.shape
    few_rows = rows // ring
    owned, slots, block, _ = beta_blocks.shape
    outer = 4
    inner = ring // outer
    xs = inner // CORES
    at_a, at_b = lax.axis_index("alpha"), lax.axis_index("beta")
    parity = lax.rem(at_a, 2)
    place = jnp.stack([lax.rem(at_b, CORES), lax.rem(lax.div(at_b, CORES), xs), parity, at_a]).astype(jnp.int32)
    cuts = [(0, 6), (6, 2)]

    def swap(value, bit):
        return lax.ppermute(value, "beta", [(i, i ^ bit) for i in range(ring)])

    def across(value):
        return lax.ppermute(value, "alpha", [(i, i ^ 1) for i in range(ring_a)])

    def exchange(value):
        return [
            lax.ppermute(value, "alpha", [((i + s) % ring_a, i) for i in range(ring_a)]) for s in range(1, ring_a)
        ]

    stored = beta_blocks.reshape(2, owned * slots // 2, block, block)
    mine = lax.dynamic_index_in_dim(stored, parity, 0, keepdims=False)
    mine = mine.transpose(0, 2, 1).reshape(-1, block)
    far = [[o * inner + i for o in range(outer)] for i in range(inner)]
    carried = [lax.all_gather(mine, "beta", axis=0, tiled=False, axis_index_groups=far)]
    bit = CORES
    while bit < inner:
        carried = carried + [swap(m, bit) for m in carried]
        bit *= 2
    messages = []
    for m in carried:
        messages += [m, across(m)]

    heads = jnp.pad(beta_cols.reshape(1, -1).astype(jnp.bfloat16), ((0, TILE - 1), (0, strip - owned * slots)))
    turned = []
    for i, (first, count) in enumerate(cuts):
        piece = pack(ci_vectors, heads if i == 0 else None, first, count, ring)
        if i > 0:
            piece = after(piece, turned[i - 1])
        turned.append(lax.all_to_all(piece, "beta", split_axis=0, concat_axis=0, tiled=True))
    columns = turned[0][:, cuts[0][1] * few_rows, : owned * slots].reshape(-1).astype(jnp.int32)

    twins = [swap(t, 1) for t in turned]

    own_late = ci_vectors[cuts[0][0] : cuts[0][0] + cuts[0][1]]
    own_early = ci_vectors[cuts[1][0] : cuts[1][0] + cuts[1][1]]
    acc_late = alpha_term(
        alpha_cols.reshape(-1), place, ci_vectors, exchange(after(own_late, messages[-1])), alpha_blocks, diagonal, 0
    )
    acc_early = alpha_term(
        alpha_cols.reshape(-1), place, ci_vectors, exchange(own_early), alpha_blocks, diagonal, cuts[1][0]
    )

    near = [[j * CORES + c for j in range(ring // CORES)] for c in range(CORES)]
    total = None
    last = turned[-1]
    for i, (first, count) in enumerate(cuts):
        term = beta_term(slots, xs, columns, place, turned[i], twins[i], messages, count * few_rows)
        term = after(term, last)
        words = lax.all_to_all(term, "beta", split_axis=0, concat_axis=0, tiled=True, axis_index_groups=near)
        last = words
        total = join((acc_late, acc_early)[i], words, first, vectors, total)
    return total


def solution(mesh):
    placed = (
        P(None, "alpha", "beta"),
        P("alpha", None, None, None),
        P("alpha", None),
        P("beta", None, None, None),
        P("beta", None),
        P("alpha", "beta"),
    )
    return jax.shard_map(
        functools.partial(shards, mesh.shape["beta"], mesh.shape["alpha"]),
        mesh=mesh,
        in_specs=placed,
        out_specs=P(None, "alpha", "beta"),
        check_vma=False,
    )
```

time: 573 us -> 827 us (1.44)
  Pallas kernels: 139 us -> 380 us
  waiting for transfers between devices: 344 us -> 375 us
  starting transfers between devices: 38.4 us -> 28.8 us
    pallas_call x9 -> x8, Pallas kernels: 139 us -> 380 us  [the longest x2 262 us: pack(): pl.pallas_call(functools.partial(pack_kernel, first, count, few_rows), in...]
    all_gather x3 -> x1, waiting for transfers between devices: 175 us -> 0.01 us  [shards(): lax.all_gather(mine, 'beta', axis=0, tiled=False, axis_index_groups=far)]
    ppermute x0 -> x7, waiting for transfers between devices: none -> 91.9 us  [the longest x3 46 us: swap(): return lax.ppermute(value, 'beta', [(i, i ^ bit) for i in range(ring)])]
    all_to_all x2, waiting for transfers between devices: 87.6 us -> 176 us  [shards(): lax.all_to_all(piece, 'beta', split_axis=0, concat_axis=0, tiled=True)]
    all_to_all x4 -> x2, waiting for transfers between devices: 80.9 us -> 106 us  [shards(): lax.all_to_all(term, 'beta', split_axis=0, concat_axis=0, tiled=True, axi...]
    all_to_all x4 -> x2, starting transfers between devices: 25.9 us -> 11.2 us  [shards(): lax.all_to_all(term, 'beta', split_axis=0, concat_axis=0, tiled=True, axi...]
    unnamed x17 -> x20, local copies, waits for them, and re-layouts: 20.1 us -> 14.9 us
  transfers between devices with their start and end apart: 9 -> 12, of which waited for: 7 -> 5; matrix products, arithmetic and copies ran while one was open for 2% -> 1% of each run, Pallas kernels for 24% -> 22%
where the time goes in v2:
time: 827 us; the launch traced here: 825 us
  Pallas kernels  380 us (46%)
  waiting for transfers between devices  375 us (45%)
  starting transfers between devices  28.8 us (3%)
  local copies, waits for them, and re-layouts  25.8 us (3%)
  between operations  13.5 us (2%)
    pallas_call x2, Pallas kernels, pack(): pl.pallas_call(functools.partial(pack_kernel, first, count, few_rows), in...  262 us
    all_to_all x2, waiting for transfers between devices, shards(): lax.all_to_all(piece, 'beta', split_axis=0, concat_axis=0, tiled=True)  176 us
    all_to_all x2, waiting for transfers between devices, shards(): lax.all_to_all(term, 'beta', split_axis=0, concat_axis=0, tiled=True, axi...  106 us
    pallas_call x2, Pallas kernels, beta_term(): pl.pallas_call(functools.partial(beta_kernel, slots, xs), grid_spec=pltpu...  55.7 us
    pallas_call x2, Pallas kernels, alpha_term(): pl.pallas_call(functools.partial(alpha_kernel, pieces), grid_spec=pltpu.P...  51.7 us
    ppermute x3, waiting for transfers between devices, swap(): return lax.ppermute(value, 'beta', [(i, i ^ bit) for i in range(ring)])  46 us
    ppermute x2, waiting for transfers between devices, exchange(): lax.ppermute(value, 'alpha', [((i + s) % ring_a, i) for i in range(ring_a)])  45.9 us
  transfers between devices with their start and end apart: 12, of which 5 were waited for; matrix products, arithmetic and copies ran while one was open for 1% of the time, Pallas kernels for 22%

profile of v2, /device:TPU:11, one launch (start us, length us, event | category | flops | bytes accessed | tf_op | source)
XLA Modules:
  0.0 824.9 jit_solution(14132250528824626731)
XLA Ops:
  8.0 196.7 %pack_pieces.2 = bf16[16,784,256]{2,1,0:T(8,128)(2,1)} custom-call(bf16[8,2048,256]{2,1,0:T(8,128)(2,1)} %refs_0_.7, bf16[16,256]{1,0:T(8,128)(2,1)} %pad.4.refs_1_), custom_call_target="tpu_custom_call" | custom-call | bytes 12845056 | tf_op jit(solution)/shard_map/pack_pieces/pallas_call | solution.py:77
  204.7 6.6 all-to-all-start
  212.4 172.7 %all-to-all-done.refs_0_ = bf16[16,784,256]{2,1,0:T(8,128)(2,1)} async-done(((bf16[16,784,256]{2,1,0:T(8,128)(2,1)}), bf16[16,784,256]{2,1,0:T(8,128)(2,1)}, u32[]{:S(2)}, u32[]{:S(2)}) %all-to-all-start) | async-done | bytes 6422560 | tf_op jit(solution)/shard_map/all_to_all | solution.py:309
  386.6 46.0 %collective-permute-done.3.refs_4_ = bf16[4,2048,128]{2,1,0:T(8,128)(2,1)} collective-permute-done((bf16[4,2048,128]{2,1,0:T(8,128)(2,1)}, bf16[4,2048,128]{2,1,0:T(8,128)(2,1)}, u32[]{:S(2)}, u32[]{:S(2)}) %collective-permute-start.3) | collective-permute-done | bytes 2097184 | tf_op jit(solution)/shard_map/ppermute | solution.py:280
  433.8 65.1 %pack_pieces.3 = bf16[16,256,256]{2,1,0:T(8,128)(2,1)} custom-call(bf16[8,2048,256]{2,1,0:T(8,128)(2,1)} %refs_0_.7), custom_call_target="tpu_custom_call" | custom-call | bytes 4194304 | tf_op jit(solution)/shard_map/pack_pieces/pallas_call | solution.py:77
  498.9 6.1 all-to-all-start.1
  507.5 41.1 %beta_term.3 = s16[8,1536,256]{2,1,0:T(8,128)(2,1)} custom-call(s32[512]{0:T(512)S(1)} %reshape.29.cols_ref, s32[4]{0:T(128)S(1)} %pad_add_fusion.place_ref, bf16[16,784,256]{2,1,0:T(8,128)(2,1)} %all-to-all-done.refs_0_, bf16[16,784,256]{2,1,0:T(8,128)(2,1)} %collective-permute-done.5.refs_1_, bf16[4,2048,128]{2,1,0:T(8,128)(2,1)S(1)} %copy-done.7, ...), custom_call_target="tpu_custom_call" | custom-call | flops 25769803776 | bytes 41943040 | tf_op jit(solution)/shard_map/beta_term/pallas_call | solution.py:148
  548.6 3.8 all-to-all-done.1.refs_0_
  552.4 4.7 all-to-all-start.2
  557.2 5.9 slice.11
  564.1 3.1 slice.9
  568.5 1.6 copy-done.8
  570.1 14.6 %beta_term.2 = s16[8,512,256]{2,1,0:T(8,128)(2,1)S(1)} custom-call(s32[512]{0:T(512)S(1)} %reshape.29.cols_ref, s32[4]{0:T(128)S(1)} %pad_add_fusion.place_ref, bf16[16,256,256]{2,1,0:T(8,128)(2,1)S(1)} %all-to-all-done.1.refs_0_, bf16[16,256,256]{2,1,0:T(8,128)(2,1)} %collective-permute-done.1.refs_1_, bf16[4,2048,128]{2,1,0:T(8,128)(2,1)S(1)} %copy-done.8, ...), custom_call_target="tpu_custom_call" | custom-call | flops 8589934592 | bytes 25165824 | tf_op jit(solution)/shard_map/beta_term/pallas_call | solution.py:148
  586.0 106.5 %all-to-all-done.2 = s16[8,1536,256]{2,1,0:T(8,128)(2,1)} async-done(((s16[8,1536,256]{2,1,0:T(8,128)(2,1)}), s16[8,1536,256]{2,1,0:T(8,128)(2,1)}, u32[]{:S(2)}, u32[]{:S(2)}) %all-to-all-start.2) | async-done | bytes 6291488 | tf_op jit(solution)/shard_map/all_to_all | solution.py:329
  692.5 6.5 all-to-all-start.3
  699.0 45.9 %collective-permute-done.refs_1_ = bf16[2,2048,256]{2,1,0:T(8,128)(2,1)} collective-permute-done((bf16[2,2048,256]{2,1,0:T(8,128)(2,1)}, bf16[2,2048,256]{2,1,0:T(8,128)(2,1)}, u32[]{:S(2)}, u32[]{:S(2)}) %collective-permute-start) | collective-permute-done | bytes 2097184 | tf_op jit(solution)/shard_map/ppermute | solution.py:287
  744.9 1.6 copy-done.6
  746.5 14.9 %alpha_term.2.acc_ref = f32[2,2048,256]{2,1,0:T(8,128)S(1)} custom-call(s32[256]{0:T(256)S(1)} %reshape.26.cols_ref, s32[4]{0:T(128)S(1)} %pad_add_fusion.place_ref, bf16[8,2048,256]{2,1,0:T(8,128)(2,1)} %refs_0_.7, bf16[2,2048,256]{2,1,0:T(8,128)(2,1)} %collective-permute-done.refs_1_, bf16[16,16,128,128]{3,2,1,0:T(8,128)(2,1)} %refs_2_.3, ...), custom_call_target="tpu_custom_call" | custom-call | flops 12884901888 | bytes 18874368 | tf_op jit(solution)/shard_map/alpha_term/pallas_call | solution.py:200
  761.4 2.0 copy-done.3
  763.4 36.8 %alpha_term.3.acc_ref = f32[6,2048,256]{2,1,0:T(8,128)} custom-call(s32[256]{0:T(256)S(1)} %reshape.26.cols_ref, s32[4]{0:T(128)S(1)} %pad_add_fusion.place_ref, bf16[8,2048,256]{2,1,0:T(8,128)(2,1)} %refs_0_.7, bf16[6,2048,256]{2,1,0:T(8,128)(2,1)} %collective-permute-done.6.refs_1_, bf16[16,16,128,128]{3,2,1,0:T(8,128)(2,1)} %refs_2_.3, ...), custom_call_target="tpu_custom_call" | custom-call | flops 38654705664 | bytes 35651584 | tf_op jit(solution)/shard_map/alpha_term/pallas_call | solution.py:200
  800.2 4.6 copy-done.2
  804.8 8.4 %join_terms.2.rest_0_ = bf16[8,2048,256]{2,1,0:T(8,128)(2,1)} custom-call(f32[6,2048,256]{2,1,0:T(8,128)S(1)} %copy-done.2, s16[8,2,6,128,256]{4,3,2,1,0:T(8,128)(2,1)} %bitcast.8.words_ref), custom_call_target="tpu_custom_call" | custom-call | flops 25165824 | bytes 25165824 | tf_op jit(solution)/shard_map/join_terms/pallas_call | solution.py:248
  813.2 2.3 copy-done.4
  815.5 2.6 join_terms.3
  (40 shorter events, 11.5 us)
Async XLA Ops:
  6.5 204.8 %copy-start = (bf16[2,16,128,128]{3,2,1,0:T(8,128)(2,1)S(1)}, bf16[2,16,128,128]{3,2,1,0:T(8,128)(2,1)}, u32[]{:S(2)}) copy-start(bf16[2,16,128,128]{3,2,1,0:T(8,128)(2,1)} %param.9) | copy-start | bytes 3145732
  204.7 180.4 %all-to-all-start = ((bf16[16,784,256]{2,1,0:T(8,128)(2,1)}), bf16[16,784,256]{2,1,0:T(8,128)(2,1)}, u32[]{:S(2)}, u32[]{:S(2)}) async-start(bf16[16,784,256]{2,1,0:T(8,128)(2,1)} %pack_pieces.2), calls=%async_computation | async-start | bytes 12845056 | tf_op jit(solution)/shard_map/all_to_all | solution.py:309
  211.2 174.1 %all-gather.2.cloned.1.call-start = ((), (), s32[]{:S(2)}) async-start(), calls=%async_computation.4 | async-start | bytes 2621440 | tf_op jit(solution)/shard_map/all_gather | solution.py:294
  385.1 120.8 %collective-permute-start.5 = (bf16[16,784,256]{2,1,0:T(8,128)(2,1)}, bf16[16,784,256]{2,1,0:T(8,128)(2,1)}, u32[]{:S(2)}, u32[]{:S(2)}) collective-permute-start(bf16[16,784,256]{2,1,0:T(8,128)(2,1)} %all-to-all-done.refs_0_), channel_id=1, source_target_pairs={{0,1},{1,0},{2,3},{3,2},{4,5},{5,4},{6,7},{7,6},{8,9},{9,8},{10,11... | collective-permute-start | bytes 19267592 | tf_op jit(solution)/shard_map/ppermute | solution.py:280
  385.3 47.2 %collective-permute-start.3 = (bf16[4,2048,128]{2,1,0:T(8,128)(2,1)}, bf16[4,2048,128]{2,1,0:T(8,128)(2,1)}, u32[]{:S(2)}, u32[]{:S(2)}) collective-permute-start(bf16[4,2048,128]{2,1,0:T(8,128)(2,1)} %all-gather.2.cloned.1.call-done.refs_2_), channel_id=1, source_target_pairs={{0,2},{1,3},{2,0},{3,1},{4,6},{5,7},{6,4},{7,5},{8,10},{9,11},{10,... | collective-permute-start | bytes 6291464 | tf_op jit(solution)/shard_map/ppermute | solution.py:280
  385.3 120.6 %collective-permute-start.2 = (bf16[4,2048,128]{2,1,0:T(8,128)(2,1)}, bf16[4,2048,128]{2,1,0:T(8,128)(2,1)}, u32[]{:S(2)}, u32[]{:S(2)}) collective-permute-start(bf16[4,2048,128]{2,1,0:T(8,128)(2,1)} %all-gather.2.cloned.1.call-done.refs_2_), channel_id=1, source_target_pairs={{0,16},{16,0},{1,17},{17,1},{2,18},{18,2},{3,19},{19,3},{4,20},{20... | collective-permute-start | bytes 6291464 | tf_op jit(solution)/shard_map/ppermute | solution.py:283
  432.6 73.4 %collective-permute-start.4 = (bf16[4,2048,128]{2,1,0:T(8,128)(2,1)}, bf16[4,2048,128]{2,1,0:T(8,128)(2,1)}, u32[]{:S(2)}, u32[]{:S(2)}) collective-permute-start(bf16[4,2048,128]{2,1,0:T(8,128)(2,1)} %collective-permute-done.3.refs_4_), channel_id=1, source_target_pairs={{0,16},{16,0},{1,17},{17,1},{2,18},{18,2},{3,19},{19,3},{4,20},{20... | collective-permute-start | bytes 6291464 | tf_op jit(solution)/shard_map/ppermute | solution.py:283
  498.9 53.5 %all-to-all-start.1 = ((bf16[16,256,256]{2,1,0:T(8,128)(2,1)}), bf16[16,256,256]{2,1,0:T(8,128)(2,1)S(1)}, u32[]{:S(2)}, u32[]{:S(2)}) async-start(bf16[16,256,256]{2,1,0:T(8,128)(2,1)} %pack_pieces.3), calls=%async_computation.1 | async-start | bytes 4194304 | tf_op jit(solution)/shard_map/all_to_all | solution.py:309
  506.0 1.6 copy-start.7
  552.4 140.1 %all-to-all-start.2 = ((s16[8,1536,256]{2,1,0:T(8,128)(2,1)}), s16[8,1536,256]{2,1,0:T(8,128)(2,1)}, u32[]{:S(2)}, u32[]{:S(2)}) async-start(s16[8,1536,256]{2,1,0:T(8,128)(2,1)} %beta_term.3), calls=%async_computation.2 | async-start | bytes 12582912 | tf_op jit(solution)/shard_map/all_to_all | solution.py:329
  557.2 11.3 %copy-start.9 = (s32[16,16]{1,0:T(8,128)S(1)}, s32[16,16]{1,0:T(8,128)}, u32[]{:S(2)}) copy-start(s32[16,16]{1,0:T(8,128)} %param.8) | copy-start | bytes 3076
  563.1 200.3 %collective-permute-start.6 = (bf16[6,2048,256]{2,1,0:T(8,128)(2,1)}, bf16[6,2048,256]{2,1,0:T(8,128)(2,1)}, u32[]{:S(2)}, u32[]{:S(2)}) collective-permute-start(bf16[6,2048,256]{2,1,0:T(8,128)(2,1)} %slice.11), channel_id=1, source_target_pairs={{16,0},{0,16},{17,1},{1,17},{18,2},{2,18},{19,3},{3,19},{20,4},{4,... | collective-permute-start | bytes 18874376 | tf_op jit(solution)/shard_map/ppermute | solution.py:287
  563.3 5.2 collective-permute-start.1
  567.2 177.7 %collective-permute-start = (bf16[2,2048,256]{2,1,0:T(8,128)(2,1)}, bf16[2,2048,256]{2,1,0:T(8,128)(2,1)}, u32[]{:S(2)}, u32[]{:S(2)}) collective-permute-start(bf16[2,2048,256]{2,1,0:T(8,128)(2,1)} %slice.9), channel_id=1, source_target_pairs={{16,0},{0,16},{17,1},{1,17},{18,2},{2,18},{19,3},{3,19},{20,4},{4,... | collective-permute-start | bytes 6291464 | tf_op jit(solution)/shard_map/ppermute | solution.py:287
  568.5 1.6 copy-start.8
  584.7 1.3 copy-start.5
  692.5 120.7 %all-to-all-start.3 = ((s16[8,512,256]{2,1,0:T(8,128)(2,1)}), s16[8,512,256]{2,1,0:T(8,128)(2,1)S(1)}, u32[]{:S(2)}, u32[]{:S(2)}) async-start(s16[8,512,256]{2,1,0:T(8,128)(2,1)} %copy-done.5), calls=%async_computation.3 | async-start | bytes 4194304 | tf_op jit(solution)/shard_map/all_to_all | solution.py:329
  744.9 1.6 copy-start.6
  761.4 2.0 copy-start.3
  800.2 4.6 copy-start.2
  813.2 4.8 copy-start.1
  813.2 2.3 copy-start.4
Sparse Core Ops, SparseCore 0:
  213.6 92.0 all-gather.1

commit v3 on v2

--- a/solution.py
+++ b/solution.py
@@ -44,42 +44,35 @@
     return words.astype(jnp.float32) * (row_scale(code) * (1.0 / LARGEST))
 
 
-def pack_kernel(first, count, few_rows, *refs):
-    source_ref, out_ref, sem = refs[0], refs[-2], refs[-1]
+def pack_kernel(source_ref, *refs):
+    out_ref = refs[-1]
+    count, wide, _ = source_ref.shape
     dests = out_ref.shape[0]
-
-    def copy(d, v):
-        return pltpu.make_async_copy(
-            source_ref.at[first + v, pl.ds(d * few_rows, few_rows)],
-            out_ref.at[d, pl.ds(v * few_rows, few_rows)],
-            sem.at[d, v],
-        )
-
-    def head(d):
-        return pltpu.make_async_copy(refs[1], out_ref.at[d, pl.ds(count * few_rows, TILE)], sem.at[d, count])
-
-    def all_of(act):
-        for d in range(dests):
-            for v in range(count):
-                act(copy(d, v))
-            if len(refs) == 4:
-                act(head(d))
-
-    all_of(lambda c: c.start())
-    all_of(lambda c: c.wait())
+    few_rows = wide // dests
+    for d in range(dests):
+        for v in range(count):
+            out_ref[d, v * few_rows : (v + 1) * few_rows, :] = source_ref[v, d * few_rows : (d + 1) * few_rows, :]
+        if len(refs) == 2:
+            out_ref[d, count * few_rows :, :] = refs[0][...]
 
 
 def pack(ci_vectors, heads, first, count, ring):
     _, rows, strip = ci_vectors.shape
     few_rows = rows // ring
     depth = count * few_rows + (0 if heads is None else TILE)
-    args = (ci_vectors,) if heads is None else (ci_vectors, heads)
+    each = 4
+    in_specs = [pl.BlockSpec((count, each * few_rows, strip), lambda d: (first // count, d, 0))]
+    args = [ci_vectors]
+    if heads is not None:
+        in_specs.append(pl.BlockSpec((TILE, strip), lambda d: (0, 0)))
+        args.append(heads)
     return pl.pallas_call(
-        functools.partial(pack_kernel, first, count, few_rows),
-        in_specs=[ANYWHERE] * len(args),
-        out_specs=ANYWHERE,
+        pack_kernel,
+        grid=(ring // each,),
+        in_specs=in_specs,
+        out_specs=pl.BlockSpec((each, depth, strip), lambda d: (d, 0, 0)),
         out_shape=jax.ShapeDtypeStruct((ring, depth, strip), jnp.bfloat16),
-        scratch_shapes=[pltpu.SemaphoreType.DMA((ring, count + 1))],
+        compiler_params=pltpu.CompilerParams(vmem_limit_bytes=24 * MIB),
         cost_estimate=pl.CostEstimate(flops=0, bytes_accessed=4 * ring * depth * strip, transcendentals=0),
         name="pack_pieces",
     )(*args)
@@ -171,7 +164,8 @@
 
 
 def alpha_kernel(pieces, cols_ref, place_ref, *refs):
-    blocks_ref, diag_ref, out_ref, whole_ref = refs[pieces:]
+    blocks_ref, diag_ref = refs[pieces : pieces + 2]
+    out_ref, whole_ref = refs[-2:]
     own_ref = refs[0]
     owned, slots, block, _ = blocks_ref.shape
     rows = own_ref.shape[1]
@@ -192,26 +186,37 @@
         out_ref[0, here, :] = term + diag_ref[here, :] * own_ref[0, here, :].astype(jnp.float32)
 
 
-def alpha_term(columns, place, own, others, blocks, diagonal, first):
-    count, rows, strip = others[0].shape if others else own.shape
+def alpha_term(columns, place, own, others, blocks, diagonal, first, count, before):
+    vectors, rows, strip = own.shape
     owned, slots, block, _ = blocks.shape
     pieces = 1 + len(others)
     once = pl.Buffered(1)
+    mine = pl.BlockSpec((1, rows, strip), lambda v, *_: (first + v, 0, 0))
+    in_specs = (
+        [mine]
+        + [pl.BlockSpec((1, rows, strip), lambda v, *_: (v, 0, 0))] * len(others)
+        + [
+            pl.BlockSpec(blocks.shape, lambda v, *_: (0, 0, 0, 0), pipeline_mode=once),
+            pl.BlockSpec(diagonal.shape, lambda v, *_: (0, 0), pipeline_mode=once),
+        ]
+    )
+    args = [columns, place, own, *others, blocks, diagonal]
+    aliases = {}
+    if before is not None:
+        aliases = {len(args): 0}
+        args.append(before)
+        in_specs.append(ANYWHERE)
     return pl.pallas_call(
         functools.partial(alpha_kernel, pieces),
         grid_spec=pltpu.PrefetchScalarGridSpec(
             num_scalar_prefetch=2,
             grid=(count,),
-            in_specs=[pl.BlockSpec((1, rows, strip), lambda v, *_: (first + v, 0, 0))]
-            + [pl.BlockSpec((1, rows, strip), lambda v, *_: (v, 0, 0))] * len(others)
-            + [
-                pl.BlockSpec(blocks.shape, lambda v, *_: (0, 0, 0, 0), pipeline_mode=once),
-                pl.BlockSpec(diagonal.shape, lambda v, *_: (0, 0), pipeline_mode=once),
-            ],
-            out_specs=pl.BlockSpec((1, rows, strip), lambda v, *_: (v, 0, 0)),
+            in_specs=in_specs,
+            out_specs=mine,
             scratch_shapes=[pltpu.VMEM((pieces * rows, strip), jnp.bfloat16)],
         ),
-        out_shape=jax.ShapeDtypeStruct((count, rows, strip), jnp.float32),
+        out_shape=jax.ShapeDtypeStruct((vectors, rows, strip), jnp.float32),
+        input_output_aliases=aliases,
         compiler_params=pltpu.CompilerParams(vmem_limit_bytes=44 * MIB),
         cost_estimate=pl.CostEstimate(
             flops=6 * count * rows * strip * slots * block,
@@ -219,7 +224,7 @@
             transcendentals=0,
         ),
         name="alpha_term",
-    )(columns, place, own, *others, blocks, diagonal)
+    )(*args)
 
 
 def join_kernel(few_rows, acc_ref, words_ref, *rest):
@@ -231,12 +236,13 @@
 
 
 def join(acc, words, first, vectors, before):
-    count, rows, strip = acc.shape
+    _, rows, strip = acc.shape
     sources = words.shape[0]
     few_rows = rows // (sources * CORES)
-    words = words.reshape(sources, CORES, count, few_rows, strip)
+    words = words.reshape(sources, CORES, -1, few_rows, strip)
+    count = words.shape[2]
     in_specs = [
-        pl.BlockSpec((1, rows, strip), lambda v: (v, 0, 0)),
+        pl.BlockSpec((1, rows, strip), lambda v: (first + v, 0, 0)),
         pl.BlockSpec((sources, CORES, 1, few_rows, strip), lambda v: (0, 0, v, 0, 0)),
     ]
     args = [acc, words]
@@ -274,7 +280,8 @@
     at_a, at_b = lax.axis_index("alpha"), lax.axis_index("beta")
     parity = lax.rem(at_a, 2)
     place = jnp.stack([lax.rem(at_b, CORES), lax.rem(lax.div(at_b, CORES), xs), parity, at_a]).astype(jnp.int32)
-    cuts = [(0, 6), (6, 2)]
+    cuts = [(6, 2), (0, 6)]
+    halves = [(0, vectors // 2), (vectors // 2, vectors // 2)]
 
     def swap(value, bit):
         return lax.ppermute(value, "beta", [(i, i ^ bit) for i in range(ring)])
@@ -287,11 +294,14 @@
             lax.ppermute(value, "alpha", [((i + s) % ring_a, i) for i in range(ring_a)]) for s in range(1, ring_a)
         ]
 
+    others = [exchange(ci_vectors[: halves[0][1]])]
+
     stored = beta_blocks.reshape(2, owned * slots // 2, block, block)
     mine = lax.dynamic_index_in_dim(stored, parity, 0, keepdims=False)
     mine = mine.transpose(0, 2, 1).reshape(-1, block)
     far = [[o * inner + i for o in range(outer)] for i in range(inner)]
-    carried = [lax.all_gather(mine, "beta", axis=0, tiled=False, axis_index_groups=far)]
+    carried = lax.all_gather(mine, "beta", axis=0, tiled=False, axis_index_groups=far)
+    carried = [after(carried, others[0][-1])]
     bit = CORES
     while bit < inner:
         carried = carried + [swap(m, bit) for m in carried]
@@ -299,6 +309,7 @@
     messages = []
     for m in carried:
         messages += [m, across(m)]
+    others.append(exchange(after(ci_vectors[halves[1][0] :], messages[-1])))
 
     heads = jnp.pad(beta_cols.reshape(1, -1).astype(jnp.bfloat16), ((0, TILE - 1), (0, strip - owned * slots)))
     turned = []
@@ -308,17 +319,13 @@
             piece = after(piece, turned[i - 1])
         turned.append(lax.all_to_all(piece, "beta", split_axis=0, concat_axis=0, tiled=True))
     columns = turned[0][:, cuts[0][1] * few_rows, : owned * slots].reshape(-1).astype(jnp.int32)
-
     twins = [swap(t, 1) for t in turned]
 
-    own_late = ci_vectors[cuts[0][0] : cuts[0][0] + cuts[0][1]]
-    own_early = ci_vectors[cuts[1][0] : cuts[1][0] + cuts[1][1]]
-    acc_late = alpha_term(
-        alpha_cols.reshape(-1), place, ci_vectors, exchange(after(own_late, messages[-1])), alpha_blocks, diagonal, 0
-    )
-    acc_early = alpha_term(
-        alpha_cols.reshape(-1), place, ci_vectors, exchange(own_early), alpha_blocks, diagonal, cuts[1][0]
-    )
+    acc = None
+    for (first, count), others_now in zip(halves, others):
+        acc = alpha_term(
+            alpha_cols.reshape(-1), place, ci_vectors, others_now, alpha_blocks, diagonal, first, count, acc
+        )
 
     near = [[j * CORES + c for j in range(ring // CORES)] for c in range(CORES)]
     total = None
@@ -328,7 +335,7 @@
         term = after(term, last)
         words = lax.all_to_all(term, "beta", split_axis=0, concat_axis=0, tiled=True, axis_index_groups=near)
         last = words
-        total = join((acc_late, acc_early)[i], words, first, vectors, total)
+        total = join(acc, words, first, vectors, total)
     return total
 
 

time: 827 us -> 574 us (0.69)
  Pallas kernels: 380 us -> 126 us
    pallas_call x2, Pallas kernels: 262 us -> 2.93 us  [pack(): pl.pallas_call(pack_kernel, grid=(ring // each,), in_specs=in_specs, out_...]
    all_to_all x2, waiting for transfers between devices: 106 us -> 11.9 us  [shards(): lax.all_to_all(term, 'beta', split_axis=0, concat_axis=0, tiled=True, axi...]
    ppermute x2, waiting for transfers between devices: 0.01 us -> 44 us  [across(): return lax.ppermute(value, 'alpha', [(i, i ^ 1) for i in range(ring_a)])]
    all_to_all x2, waiting for transfers between devices: 176 us -> 206 us  [shards(): lax.all_to_all(piece, 'beta', split_axis=0, concat_axis=0, tiled=True)]
    ppermute x2, waiting for transfers between devices: 45.9 us -> 60.8 us  [exchange(): lax.ppermute(value, 'alpha', [((i + s) % ring_a, i) for i in range(ring_a)])]
    unnamed x20 -> x28, local copies, waits for them, and re-layouts: 14.9 us -> 24.4 us
  transfers between devices with their start and end apart: 12 -> 12, of which waited for: 5 -> 7; matrix products, arithmetic and copies ran while one was open for 1% -> 1% of each run, Pallas kernels for 22% -> 20%
where the time goes in v3:
time: 574 us; the launch traced here: 569 us
  waiting for transfers between devices  369 us (64%)
  Pallas kernels  126 us (22%)
  local copies, waits for them, and re-layouts  31.4 us (5%)
  starting transfers between devices  28.1 us (5%)
  between operations  13.5 us (2%)
    all_to_all x2, waiting for transfers between devices, shards(): lax.all_to_all(piece, 'beta', split_axis=0, concat_axis=0, tiled=True)  206 us
    ppermute x2, waiting for transfers between devices, exchange(): lax.ppermute(value, 'alpha', [((i + s) % ring_a, i) for i in range(ring_a)])  60.8 us
    pallas_call x2, Pallas kernels, beta_term(): pl.pallas_call(functools.partial(beta_kernel, slots, xs), grid_spec=pltpu...  55.6 us
    pallas_call x2, Pallas kernels, alpha_term(): pl.pallas_call(functools.partial(alpha_kernel, pieces), grid_spec=pltpu.P...  53.1 us
    ppermute x3, waiting for transfers between devices, swap(): return lax.ppermute(value, 'beta', [(i, i ^ bit) for i in range(ring)])  45.6 us
    ppermute x2, waiting for transfers between devices, across(): return lax.ppermute(value, 'alpha', [(i, i ^ 1) for i in range(ring_a)])  44 us
    unnamed x28, local copies, waits for them, and re-layouts  24.4 us
    pallas_call x2, Pallas kernels, join(): pl.pallas_call(functools.partial(join_kernel, few_rows), grid=(count,), i...  13.9 us
  transfers between devices with their start and end apart: 12, of which 7 were waited for; matrix products, arithmetic and copies ran while one was open for 1% of the time, Pallas kernels for 20%

profile of v3, /device:TPU:11, one launch (start us, length us, event | category | flops | bytes accessed | tf_op | source)
XLA Modules:
  0.0 568.9 jit_solution(12074826610157777634)
XLA Ops:
  7.4 3.4 copy-done.2
  10.8 2.0 pack_pieces.2
  12.8 6.6 %all-to-all-start = ((bf16[16,272,256]{2,1,0:T(8,128)(2,1)}), bf16[16,272,256]{2,1,0:T(8,128)(2,1)S(1)}, u32[]{:S(2)}, u32[]{:S(2)}) async-start(bf16[16,272,256]{2,1,0:T(8,128)(2,1)} %pack_pieces.2), calls=%async_computation | async-start | bytes 4456448 | tf_op jit(solution)/shard_map/all_to_all | solution.py:320
  19.4 3.4 copy-done.3
  23.7 2.7 copy-done.5
  26.4 43.2 %all-to-all-done.refs_0_ = bf16[16,272,256]{2,1,0:T(8,128)(2,1)S(1)} async-done(((bf16[16,272,256]{2,1,0:T(8,128)(2,1)}), bf16[16,272,256]{2,1,0:T(8,128)(2,1)S(1)}, u32[]{:S(2)}, u32[]{:S(2)}) %all-to-all-start) | async-done | bytes 2228256 | tf_op jit(solution)/shard_map/all_to_all | solution.py:320
  71.0 4.9 all-to-all-start.1
  76.0 5.8 %fusion.1 = (bf16[4,2048,256]{2,1,0:T(8,128)(2,1)}, bf16[4,2048,256]{2,1,0:T(8,128)(2,1)}) fusion(bf16[8,2048,256]{2,1,0:T(8,128)(2,1)} %source_ref.3), kind=kLoop, calls=%fused_computation.4 | loop fusion | bytes 16777216 | tf_op jit(solution)/shard_map/slice | solution.py:297
  84.0 162.9 %all-to-all-done.1.refs_0_ = bf16[16,768,256]{2,1,0:T(8,128)(2,1)} async-done(((bf16[16,768,256]{2,1,0:T(8,128)(2,1)}), bf16[16,768,256]{2,1,0:T(8,128)(2,1)}, u32[]{:S(2)}, u32[]{:S(2)}) %all-to-all-start.1) | async-done | bytes 6291488 | tf_op jit(solution)/shard_map/all_to_all | solution.py:320
  248.8 45.6 %collective-permute-done.1.refs_4_ = bf16[4,2048,128]{2,1,0:T(8,128)(2,1)S(1)} collective-permute-done((bf16[4,2048,128]{2,1,0:T(8,128)(2,1)}, bf16[4,2048,128]{2,1,0:T(8,128)(2,1)S(1)}, u32[]{:S(2)}, u32[]{:S(2)}) %collective-permute-start.1) | collective-permute-done | bytes 2097184 | tf_op jit(solution)/shard_map/ppermute | solution.py:287
  296.6 44.0 %collective-permute-done.2.refs_5_ = bf16[4,2048,128]{2,1,0:T(8,128)(2,1)} collective-permute-done((bf16[4,2048,128]{2,1,0:T(8,128)(2,1)S(1)}, bf16[4,2048,128]{2,1,0:T(8,128)(2,1)}, u32[]{:S(2)}, u32[]{:S(2)}) %collective-permute-start.2) | collective-permute-done | bytes 2097184 | tf_op jit(solution)/shard_map/ppermute | solution.py:290
  340.7 1.6 copy-done.8
  342.2 14.7 %beta_term.3 = s16[8,512,256]{2,1,0:T(8,128)(2,1)S(1)} custom-call(s32[512]{0:T(512)S(1)} %reshape.29.cols_ref, s32[4]{0:T(128)S(1)} %pad_add_fusion.place_ref, bf16[16,272,256]{2,1,0:T(8,128)(2,1)} %copy-done.12, bf16[16,272,256]{2,1,0:T(8,128)(2,1)} %collective-permute-done.6.refs_1_, bf16[4,2048,128]{2,1,0:T(8,128)(2,1)S(1)} %copy-done.8, ...), custom_call_target="tpu_custom_call" | custom-call | flops 8589934592 | bytes 25165824 | tf_op jit(solution)/shard_map/beta_term/pallas_call | solution.py:141
  358.3 4.7 all-to-all-start.2
  366.3 40.9 %beta_term.2 = s16[8,1536,256]{2,1,0:T(8,128)(2,1)} custom-call(s32[512]{0:T(512)S(1)} %reshape.29.cols_ref, s32[4]{0:T(128)S(1)} %pad_add_fusion.place_ref, bf16[16,768,256]{2,1,0:T(8,128)(2,1)} %all-to-all-done.1.refs_0_, bf16[16,768,256]{2,1,0:T(8,128)(2,1)} %collective-permute-done.4.refs_1_, bf16[4,2048,128]{2,1,0:T(8,128)(2,1)S(1)} %copy-done.9, ...), custom_call_target="tpu_custom_call" | custom-call | flops 25769803776 | bytes 41943040 | tf_op jit(solution)/shard_map/beta_term/pallas_call | solution.py:141
  408.8 6.3 %all-to-all-start.3 = ((s16[8,1536,256]{2,1,0:T(8,128)(2,1)}), s16[8,1536,256]{2,1,0:T(8,128)(2,1)}, u32[]{:S(2)}, u32[]{:S(2)}) async-start(s16[8,1536,256]{2,1,0:T(8,128)(2,1)} %beta_term.2), calls=%async_computation.3 | async-start | bytes 12582912 | tf_op jit(solution)/shard_map/all_to_all | solution.py:336
  416.5 1.6 copy-done.7
  418.0 26.6 %alpha_term.2.refs_4_ = f32[8,2048,256]{2,1,0:T(8,128)} custom-call(s32[256]{0:T(256)S(1)} %reshape.26.cols_ref, s32[4]{0:T(128)S(1)} %pad_add_fusion.place_ref, bf16[8,2048,256]{2,1,0:T(8,128)(2,1)} %source_ref.3, bf16[4,2048,256]{2,1,0:T(8,128)(2,1)} %collective-permute-done.refs_1_, bf16[16,16,128,128]{3,2,1,0:T(8,128)(2,1)} %refs_2_.3, ...), custom_call_target="tpu_custom_call" | custom-call | flops 25769803776 | bytes 27262976 | tf_op jit(solution)/shard_map/alpha_term/pallas_call | solution.py:209
  444.6 60.8 %collective-permute-done.3.refs_1_ = bf16[4,2048,256]{2,1,0:T(8,128)(2,1)} collective-permute-done((bf16[4,2048,256]{2,1,0:T(8,128)(2,1)}, bf16[4,2048,256]{2,1,0:T(8,128)(2,1)}, u32[]{:S(2)}, u32[]{:S(2)}) %collective-permute-start.3) | collective-permute-done | bytes 4194336 | tf_op jit(solution)/shard_map/ppermute | solution.py:294
  505.5 26.5 %alpha_term.3.acc_ref = f32[8,2048,256]{2,1,0:T(8,128)} custom-call(s32[256]{0:T(256)S(1)} %reshape.26.cols_ref, s32[4]{0:T(128)S(1)} %pad_add_fusion.place_ref, bf16[8,2048,256]{2,1,0:T(8,128)(2,1)} %source_ref.3, bf16[4,2048,256]{2,1,0:T(8,128)(2,1)} %collective-permute-done.3.refs_1_, ...), custom_call_target="tpu_custom_call", output_to_operand_aliasing={{}: (6, {})} | custom-call | flops 25769803776 | bytes 27262976 | tf_op jit(solution)/shard_map/alpha_term/pallas_call | solution.py:209
  532.0 5.8 %copy-done.4 = f32[8,2048,256]{2,1,0:T(8,128)S(1)} copy-done((f32[8,2048,256]{2,1,0:T(8,128)S(1)}, f32[8,2048,256]{2,1,0:T(8,128)}, u32[]{:S(2)}) %copy-start.4) | copy-done | bytes 16777240
  537.8 2.6 join_terms.2.rest_0_
  540.3 10.4 %all-to-all-done.3 = s16[8,1536,256]{2,1,0:T(8,128)(2,1)} async-done(((s16[8,1536,256]{2,1,0:T(8,128)(2,1)}), s16[8,1536,256]{2,1,0:T(8,128)(2,1)}, u32[]{:S(2)}, u32[]{:S(2)}) %all-to-all-start.3) | async-done | bytes 6291488 | tf_op jit(solution)/shard_map/all_to_all | solution.py:336
  550.7 11.4 %join_terms.3 = bf16[8,2048,256]{2,1,0:T(8,128)(2,1)} custom-call(f32[8,2048,256]{2,1,0:T(8,128)} %alpha_term.3.acc_ref, s16[8,2,6,128,256]{4,3,2,1,0:T(8,128)(2,1)} %bitcast.7.words_ref, bf16[8,2048,256]{2,1,0:T(8,128)(2,1)} %join_terms.2.rest_0_), custom_call_target="tpu_custom_call", output_to_operand_aliasing={{}: (2, {})} | custom-call | flops 25165824 | bytes 25165824 | tf_op jit(solution)/shard_map/join_terms/pallas_call | solution.py:254
  (47 shorter events, 17.0 us)
Async XLA Ops:
  6.5 76.4 %copy-start = (bf16[2,16,128,128]{3,2,1,0:T(8,128)(2,1)S(1)}, bf16[2,16,128,128]{3,2,1,0:T(8,128)(2,1)}, u32[]{:S(2)}) copy-start(bf16[2,16,128,128]{3,2,1,0:T(8,128)(2,1)} %param.9) | copy-start | bytes 3145732
  7.4 3.4 copy-start.2
  12.8 56.8 %all-to-all-start = ((bf16[16,272,256]{2,1,0:T(8,128)(2,1)}), bf16[16,272,256]{2,1,0:T(8,128)(2,1)S(1)}, u32[]{:S(2)}, u32[]{:S(2)}) async-start(bf16[16,272,256]{2,1,0:T(8,128)(2,1)} %pack_pieces.2), calls=%async_computation | async-start | bytes 4456448 | tf_op jit(solution)/shard_map/all_to_all | solution.py:320
  19.4 3.4 copy-start.3
  23.7 2.7 copy-start.5
  71.0 176.0 %all-to-all-start.1 = ((bf16[16,768,256]{2,1,0:T(8,128)(2,1)}), bf16[16,768,256]{2,1,0:T(8,128)(2,1)}, u32[]{:S(2)}, u32[]{:S(2)}) async-start(bf16[16,768,256]{2,1,0:T(8,128)(2,1)} %copy-done.5), calls=%async_computation.1 | async-start | bytes 12582912 | tf_op jit(solution)/shard_map/all_to_all | solution.py:320
  75.9 171.3 %all-gather.2.cloned.1.call-start = ((), (), s32[]{:S(2)}) async-start(), calls=%async_computation.4 | async-start | bytes 2621440 | tf_op jit(solution)/shard_map/all_gather | solution.py:303
  81.7 165.5 %collective-permute-start = (bf16[4,2048,256]{2,1,0:T(8,128)(2,1)}, bf16[4,2048,256]{2,1,0:T(8,128)(2,1)}, u32[]{:S(2)}, u32[]{:S(2)}) collective-permute-start(bf16[4,2048,256]{2,1,0:T(8,128)(2,1)} %get-tuple-element.15), channel_id=1, source_target_pairs={{16,0},{0,16},{17,1},{1,17},{18,2},{2,18},{19,3},{3,19},{20,4},{4,... | collective-permute-start | bytes 12582920 | tf_op jit(solution)/shard_map/ppermute | solution.py:294
  247.0 116.1 %collective-permute-start.4 = (bf16[16,768,256]{2,1,0:T(8,128)(2,1)}, bf16[16,768,256]{2,1,0:T(8,128)(2,1)}, u32[]{:S(2)}, u32[]{:S(2)}) collective-permute-start(bf16[16,768,256]{2,1,0:T(8,128)(2,1)} %all-to-all-done.1.refs_0_), channel_id=1, source_target_pairs={{0,1},{1,0},{2,3},{3,2},{4,5},{5,4},{6,7},{7,6},{8,9},{9,8},{10,11... | collective-permute-start | bytes 18874376 | tf_op jit(solution)/shard_map/ppermute | solution.py:287
  247.2 47.2 %collective-permute-start.1 = (bf16[4,2048,128]{2,1,0:T(8,128)(2,1)}, bf16[4,2048,128]{2,1,0:T(8,128)(2,1)S(1)}, u32[]{:S(2)}, u32[]{:S(2)}) collective-permute-start(bf16[4,2048,128]{2,1,0:T(8,128)(2,1)} %all-gather.2.cloned.1.call-done.refs_2_), channel_id=1, source_target_pairs={{0,2},{1,3},{2,0},{3,1},{4,6},{5,7},{6,4},{7,5},{8,10},{9,11},{10,... | collective-permute-start | bytes 6291464 | tf_op jit(solution)/shard_map/ppermute | solution.py:287
  247.2 49.4 %collective-permute-start.6 = (bf16[16,272,256]{2,1,0:T(8,128)(2,1)}, bf16[16,272,256]{2,1,0:T(8,128)(2,1)}, u32[]{:S(2)}, u32[]{:S(2)}) collective-permute-start(bf16[16,272,256]{2,1,0:T(8,128)(2,1)} %copy-done.12), channel_id=1, source_target_pairs={{0,1},{1,0},{2,3},{3,2},{4,5},{5,4},{6,7},{7,6},{8,9},{9,8},{10,11... | collective-permute-start | bytes 6684680 | tf_op jit(solution)/shard_map/ppermute | solution.py:287
  247.6 49.1 %collective-permute-start.5 = (bf16[4,2048,128]{2,1,0:T(8,128)(2,1)}, bf16[4,2048,128]{2,1,0:T(8,128)(2,1)}, u32[]{:S(2)}, u32[]{:S(2)}) collective-permute-start(bf16[4,2048,128]{2,1,0:T(8,128)(2,1)} %all-gather.2.cloned.1.call-done.refs_2_), channel_id=1, source_target_pairs={{0,16},{16,0},{1,17},{17,1},{2,18},{18,2},{3,19},{19,3},{4,20},{20... | collective-permute-start | bytes 6291464 | tf_op jit(solution)/shard_map/ppermute | solution.py:290
  294.4 62.5 %copy-start.10 = (bf16[4,2048,128]{2,1,0:T(8,128)(2,1)}, bf16[4,2048,128]{2,1,0:T(8,128)(2,1)S(1)}, u32[]{:S(2)}) copy-start(bf16[4,2048,128]{2,1,0:T(8,128)(2,1)S(1)} %collective-permute-done.1.refs_4_) | copy-start | bytes 6291460
  294.4 46.2 %collective-permute-start.2 = (bf16[4,2048,128]{2,1,0:T(8,128)(2,1)S(1)}, bf16[4,2048,128]{2,1,0:T(8,128)(2,1)}, u32[]{:S(2)}, u32[]{:S(2)}) collective-permute-start(bf16[4,2048,128]{2,1,0:T(8,128)(2,1)S(1)} %collective-permute-done.1.refs_4_), channel_id=1, source_target_pairs={{0,16},{16,0},{1,17},{17,1},{2,18},{18,2},{3,19},{19,3},{4,20},{20... | collective-permute-start | bytes 6291464 | tf_op jit(solution)/shard_map/ppermute | solution.py:290
  340.7 1.6 copy-start.8
  358.3 50.5 %all-to-all-start.2 = ((s16[8,512,256]{2,1,0:T(8,128)(2,1)}), s16[8,512,256]{2,1,0:T(8,128)(2,1)S(1)}, u32[]{:S(2)}, u32[]{:S(2)}) async-start(s16[8,512,256]{2,1,0:T(8,128)(2,1)} %copy-done.6), calls=%async_computation.2 | async-start | bytes 4194304 | tf_op jit(solution)/shard_map/all_to_all | solution.py:336
  363.1 1.6 copy-start.9
  364.7 1.6 copy-start.11
  407.2 9.2 %copy-start.13 = (s32[16,16]{1,0:T(8,128)S(1)}, s32[16,16]{1,0:T(8,128)}, u32[]{:S(2)}) copy-start(s32[16,16]{1,0:T(8,128)} %param.8) | copy-start | bytes 3076
  408.8 141.9 %all-to-all-start.3 = ((s16[8,1536,256]{2,1,0:T(8,128)(2,1)}), s16[8,1536,256]{2,1,0:T(8,128)(2,1)}, u32[]{:S(2)}, u32[]{:S(2)}) async-start(s16[8,1536,256]{2,1,0:T(8,128)(2,1)} %beta_term.2), calls=%async_computation.3 | async-start | bytes 12582912 | tf_op jit(solution)/shard_map/all_to_all | solution.py:336
  415.1 90.3 %collective-permute-start.3 = (bf16[4,2048,256]{2,1,0:T(8,128)(2,1)}, bf16[4,2048,256]{2,1,0:T(8,128)(2,1)}, u32[]{:S(2)}, u32[]{:S(2)}) collective-permute-start(bf16[4,2048,256]{2,1,0:T(8,128)(2,1)} %get-tuple-element.11), channel_id=1, source_target_pairs={{16,0},{0,16},{17,1},{1,17},{18,2},{2,18},{19,3},{3,19},{20,4},{4,... | collective-permute-start | bytes 12582920 | tf_op jit(solution)/shard_map/ppermute | solution.py:294
  416.5 1.6 copy-start.7
  532.0 5.8 %copy-start.4 = (f32[8,2048,256]{2,1,0:T(8,128)S(1)}, f32[8,2048,256]{2,1,0:T(8,128)}, u32[]{:S(2)}) copy-start(f32[8,2048,256]{2,1,0:T(8,128)} %alpha_term.3.acc_ref) | copy-start | bytes 50331652
  550.7 11.4 %copy-start.1 = (bf16[2,16,128,128]{3,2,1,0:T(8,128)(2,1)S(1)}, bf16[2,16,128,128]{3,2,1,0:T(8,128)(2,1)}, u32[]{:S(2)}) copy-start(bf16[2,16,128,128]{3,2,1,0:T(8,128)(2,1)} %param.9) | copy-start | bytes 3145732
  (2 other events, 2.8 us)
Sparse Core Ops, SparseCore 0:
  84.2 92.0 all-gather.1

commit v4 on v3

--- a/solution.py
+++ b/solution.py
@@ -280,8 +280,10 @@
     at_a, at_b = lax.axis_index("alpha"), lax.axis_index("beta")
     parity = lax.rem(at_a, 2)
     place = jnp.stack([lax.rem(at_b, CORES), lax.rem(lax.div(at_b, CORES), xs), parity, at_a]).astype(jnp.int32)
-    cuts = [(6, 2), (0, 6)]
-    halves = [(0, vectors // 2), (vectors // 2, vectors // 2)]
+    few = vectors // 4
+    cuts = [(vectors - few, few), (0, vectors - few)]
+    shares = [(0, few), (few, few), (2 * few, vectors - 2 * few)]
+    sent = [ci_vectors[first : first + count] for first, count in shares]
 
     def swap(value, bit):
         return lax.ppermute(value, "beta", [(i, i ^ bit) for i in range(ring)])
@@ -294,35 +296,40 @@
             lax.ppermute(value, "alpha", [((i + s) % ring_a, i) for i in range(ring_a)]) for s in range(1, ring_a)
         ]
 
-    others = [exchange(ci_vectors[: halves[0][1]])]
+    others = [exchange(sent[0])]
 
     stored = beta_blocks.reshape(2, owned * slots // 2, block, block)
     mine = lax.dynamic_index_in_dim(stored, parity, 0, keepdims=False)
     mine = mine.transpose(0, 2, 1).reshape(-1, block)
     far = [[o * inner + i for o in range(outer)] for i in range(inner)]
     carried = lax.all_gather(mine, "beta", axis=0, tiled=False, axis_index_groups=far)
-    carried = [after(carried, others[0][-1])]
+    gathered = carried
+    carried = [after(carried, tuple(sent[1:]))]
     bit = CORES
     while bit < inner:
         carried = carried + [swap(m, bit) for m in carried]
         bit *= 2
-    messages = []
-    for m in carried:
-        messages += [m, across(m)]
-    others.append(exchange(after(ci_vectors[halves[1][0] :], messages[-1])))
 
     heads = jnp.pad(beta_cols.reshape(1, -1).astype(jnp.bfloat16), ((0, TILE - 1), (0, strip - owned * slots)))
     turned = []
     for i, (first, count) in enumerate(cuts):
         piece = pack(ci_vectors, heads if i == 0 else None, first, count, ring)
         if i > 0:
-            piece = after(piece, turned[i - 1])
+            piece = after(piece, (turned[i - 1], gathered, others[0][-1]))
         turned.append(lax.all_to_all(piece, "beta", split_axis=0, concat_axis=0, tiled=True))
     columns = turned[0][:, cuts[0][1] * few_rows, : owned * slots].reshape(-1).astype(jnp.int32)
-    twins = [swap(t, 1) for t in turned]
+    twins = [swap(turned[0], 1)]
+
+    messages = []
+    for m in carried:
+        if messages:
+            m = after(m, (messages[-1], twins[0]))
+        messages += [m, across(m)]
+    for value in sent[1:]:
+        others.append(exchange(after(value, messages[-1])))
 
     acc = None
-    for (first, count), others_now in zip(halves, others):
+    for (first, count), others_now in zip(shares, others):
         acc = alpha_term(
             alpha_cols.reshape(-1), place, ci_vectors, others_now, alpha_blocks, diagonal, first, count, acc
         )
@@ -331,8 +338,10 @@
     total = None
     last = turned[-1]
     for i, (first, count) in enumerate(cuts):
+        if i > 0:
+            twins.append(swap(after(turned[i], term), 1))
         term = beta_term(slots, xs, columns, place, turned[i], twins[i], messages, count * few_rows)
-        term = after(term, last)
+        term = after(term, last if i == 0 else (last, others[1][-1]))
         words = lax.all_to_all(term, "beta", split_axis=0, concat_axis=0, tiled=True, axis_index_groups=near)
         last = words
         total = join(acc, words, first, vectors, total)

time: 574 us -> 508 us (0.89)
  waiting for transfers between devices: 369 us -> 275 us
  starting transfers between devices: 28.1 us -> 40.5 us
  local copies, waits for them, and re-layouts: 31.4 us -> 41.6 us
    all_to_all x2, waiting for transfers between devices: 206 us -> 5.46 us  [shards(): lax.all_to_all(piece, 'beta', split_axis=0, concat_axis=0, tiled=True)]
    ppermute x2, waiting for transfers between devices: 44 us -> 90.2 us  [across(): return lax.ppermute(value, 'alpha', [(i, i ^ 1) for i in range(ring_a)])]
    ppermute x2 -> x3, waiting for transfers between devices: 60.8 us -> 95.4 us  [exchange(): lax.ppermute(value, 'alpha', [((i + s) % ring_a, i) for i in range(ring_a)])]
    all_gather x1, waiting for transfers between devices: 0.01 us -> 23.5 us  [shards(): lax.all_gather(mine, 'beta', axis=0, tiled=False, axis_index_groups=far)]
    all_to_all x2, starting transfers between devices: 11.1 us -> 20.3 us  [shards(): lax.all_to_all(term, 'beta', split_axis=0, concat_axis=0, tiled=True, axi...]
    ppermute x3, waiting for transfers between devices: 45.6 us -> 51.6 us  [swap(): return lax.ppermute(value, 'beta', [(i, i ^ bit) for i in range(ring)])]
    unnamed x28 -> x40, local copies, waits for them, and re-layouts: 24.4 us -> 30 us
    pallas_call x2 -> x3, Pallas kernels: 53.1 us -> 58.6 us  [alpha_term(): pl.pallas_call(functools.partial(alpha_kernel, pieces), grid_spec=pltpu.P...]
  transfers between devices with their start and end apart: 12 -> 13, of which waited for: 7 -> 9; matrix products, arithmetic and copies ran while one was open for 1% -> 2% of each run, Pallas kernels for 20% -> 23%
where the time goes in v4:
time: 508 us; the launch traced here: 503 us
  waiting for transfers between devices  275 us (54%)
  Pallas kernels  131 us (26%)
  local copies, waits for them, and re-layouts  41.6 us (8%)
  starting transfers between devices  40.5 us (8%)
  between operations  13.5 us (3%)
    ppermute x3, waiting for transfers between devices, exchange(): lax.ppermute(value, 'alpha', [((i + s) % ring_a, i) for i in range(ring_a)])  95.4 us
    ppermute x2, waiting for transfers between devices, across(): return lax.ppermute(value, 'alpha', [(i, i ^ 1) for i in range(ring_a)])  90.2 us
    pallas_call x3, Pallas kernels, alpha_term(): pl.pallas_call(functools.partial(alpha_kernel, pieces), grid_spec=pltpu.P...  58.6 us
    pallas_call x2, Pallas kernels, beta_term(): pl.pallas_call(functools.partial(beta_kernel, slots, xs), grid_spec=pltpu...  55.6 us
    ppermute x3, waiting for transfers between devices, swap(): return lax.ppermute(value, 'beta', [(i, i ^ bit) for i in range(ring)])  51.6 us
    unnamed x40, local copies, waits for them, and re-layouts  30 us
    all_gather x1, waiting for transfers between devices, shards(): lax.all_gather(mine, 'beta', axis=0, tiled=False, axis_index_groups=far)  23.5 us
    all_to_all x2, starting transfers between devices, shards(): lax.all_to_all(term, 'beta', split_axis=0, concat_axis=0, tiled=True, axi...  20.3 us
  transfers between devices with their start and end apart: 13, of which 9 were waited for; matrix products, arithmetic and copies ran while one was open for 2% of the time, Pallas kernels for 23%

profile of v4, /device:TPU:11, one launch (start us, length us, event | category | flops | bytes accessed | tf_op | source)
XLA Modules:
  0.0 503.5 jit_solution(18183854062453406189)
XLA Ops:
  7.4 3.4 copy-done.3
  12.8 6.6 %all-to-all-start = ((bf16[16,272,256]{2,1,0:T(8,128)(2,1)}), bf16[16,272,256]{2,1,0:T(8,128)(2,1)S(1)}, u32[]{:S(2)}, u32[]{:S(2)}) async-start(bf16[16,272,256]{2,1,0:T(8,128)(2,1)} %pack_pieces.2), calls=%async_computation | async-start | bytes 4456448 | tf_op jit(solution)/shard_map/all_to_all | solution.py:319
  22.3 3.8 fusion.1
  27.4 3.5 copy-done.4
  31.8 2.7 copy-done.5
  34.5 38.5 %collective-permute-done.6.refs_1_ = bf16[2,2048,256]{2,1,0:T(8,128)(2,1)S(1)} collective-permute-done((bf16[2,2048,256]{2,1,0:T(8,128)(2,1)S(1)}, bf16[2,2048,256]{2,1,0:T(8,128)(2,1)S(1)}, u32[]{:S(2)}, u32[]{:S(2)}) %collective-permute-start.6) | collective-permute-done | bytes 2097184 | tf_op jit(solution)/shard_map/ppermute | solution.py:296
  74.3 23.5 %all-gather.2.cloned.1.call-done.refs_2_ = bf16[4,2048,128]{2,1,0:T(8,128)(2,1)} async-done(((bf16[1,2048,128]{2,1,0:T(8,128)(2,1)}), bf16[4,2048,128]{2,1,0:T(8,128)(2,1)}) %all-gather.2.cloned.1.call-update) | async-done | bytes 2097168 | tf_op jit(solution)/shard_map/all_gather | solution.py:305
  97.8 5.5 %all-to-all-done.refs_0_ = bf16[16,272,256]{2,1,0:T(8,128)(2,1)S(1)} async-done(((bf16[16,272,256]{2,1,0:T(8,128)(2,1)}), bf16[16,272,256]{2,1,0:T(8,128)(2,1)S(1)}, u32[]{:S(2)}, u32[]{:S(2)}) %all-to-all-start) | async-done | bytes 2228256 | tf_op jit(solution)/shard_map/all_to_all | solution.py:319
  104.7 4.9 all-to-all-start.1
  110.0 4.6 slice.12
  116.2 45.8 %collective-permute-done.1.refs_3_ = bf16[4,2048,128]{2,1,0:T(8,128)(2,1)S(1)} collective-permute-done((bf16[4,2048,128]{2,1,0:T(8,128)(2,1)S(1)}, bf16[4,2048,128]{2,1,0:T(8,128)(2,1)S(1)}, u32[]{:S(2)}, u32[]{:S(2)}) %collective-permute-start.1) | collective-permute-done | bytes 2097184 | tf_op jit(solution)/shard_map/ppermute | solution.py:292
  163.3 51.6 %collective-permute-done.refs_4_ = bf16[4,2048,128]{2,1,0:T(8,128)(2,1)} collective-permute-done((bf16[4,2048,128]{2,1,0:T(8,128)(2,1)S(1)}, bf16[4,2048,128]{2,1,0:T(8,128)(2,1)}, u32[]{:S(2)}, u32[]{:S(2)}) %collective-permute-start) | collective-permute-done | bytes 2097184 | tf_op jit(solution)/shard_map/ppermute | solution.py:289
  217.1 44.4 %collective-permute-done.3.refs_5_ = bf16[4,2048,128]{2,1,0:T(8,128)(2,1)} collective-permute-done((bf16[4,2048,128]{2,1,0:T(8,128)(2,1)}, bf16[4,2048,128]{2,1,0:T(8,128)(2,1)}, u32[]{:S(2)}, u32[]{:S(2)}) %collective-permute-start.3) | collective-permute-done | bytes 2097184 | tf_op jit(solution)/shard_map/ppermute | solution.py:292
  263.0 14.7 %beta_term.2 = s16[8,512,256]{2,1,0:T(8,128)(2,1)S(1)} custom-call(s32[512]{0:T(512)S(1)} %reshape.30.cols_ref, s32[4]{0:T(128)S(1)} %pad_add_fusion.place_ref, bf16[16,272,256]{2,1,0:T(8,128)(2,1)} %copy-done.18, bf16[16,272,256]{2,1,0:T(8,128)(2,1)} %collective-permute-done.2.refs_1_, bf16[4,2048,128]{2,1,0:T(8,128)(2,1)S(1)} %copy-done.13, ...), custom_call_target="tpu_custom_call" | custom-call | flops 8589934592 | bytes 25165824 | tf_op jit(solution)/shard_map/beta_term/pallas_call | solution.py:141
  280.8 12.4 %all-to-all-start.2 = ((s16[8,512,256]{2,1,0:T(8,128)(2,1)}), s16[8,512,256]{2,1,0:T(8,128)(2,1)S(1)}, u32[]{:S(2)}, u32[]{:S(2)}) async-start(s16[8,512,256]{2,1,0:T(8,128)(2,1)} %copy-done.10), calls=%async_computation.2 | async-start | bytes 4194304 | tf_op jit(solution)/shard_map/all_to_all | solution.py:345
  297.7 40.9 %beta_term.3 = s16[8,1536,256]{2,1,0:T(8,128)(2,1)} custom-call(s32[512]{0:T(512)S(1)} %reshape.30.cols_ref, s32[4]{0:T(128)S(1)} %pad_add_fusion.place_ref, bf16[16,768,256]{2,1,0:T(8,128)(2,1)} %all-to-all-done.1.refs_0_, bf16[16,768,256]{2,1,0:T(8,128)(2,1)} %collective-permute-done.7.refs_1_, bf16[4,2048,128]{2,1,0:T(8,128)(2,1)S(1)} %copy-done.14, ...), custom_call_target="tpu_custom_call" | custom-call | flops 25769803776 | bytes 41943040 | tf_op jit(solution)/shard_map/beta_term/pallas_call | solution.py:141
  341.8 7.9 %all-to-all-start.3 = ((s16[8,1536,256]{2,1,0:T(8,128)(2,1)}), s16[8,1536,256]{2,1,0:T(8,128)(2,1)}, u32[]{:S(2)}, u32[]{:S(2)}) async-start(s16[8,1536,256]{2,1,0:T(8,128)(2,1)} %beta_term.3), calls=%async_computation.3 | async-start | bytes 12582912 | tf_op jit(solution)/shard_map/all_to_all | solution.py:345
  354.2 16.1 %alpha_term.3.refs_4_ = f32[8,2048,256]{2,1,0:T(8,128)} custom-call(s32[256]{0:T(256)S(1)} %reshape.27.cols_ref, s32[4]{0:T(128)S(1)} %pad_add_fusion.place_ref, bf16[8,2048,256]{2,1,0:T(8,128)(2,1)} %source_ref.3, bf16[2,2048,256]{2,1,0:T(8,128)(2,1)S(1)} %copy-done.12, bf16[16,16,128,128]{3,2,1,0:T(8,128)(2,1)} %refs_2_.5, f32[2048,256]{1,0:T(8,128)S(1)} %copy-done.6), custom_call_target="tpu_custom_call" | custom-call | flops 12884901888 | bytes 18874368 | tf_op jit(solution)/shard_map/alpha_term/pallas_call | solution.py:209
  370.3 16.0 %alpha_term.4.refs_4_ = f32[8,2048,256]{2,1,0:T(8,128)} custom-call(s32[256]{0:T(256)S(1)} %reshape.27.cols_ref, s32[4]{0:T(128)S(1)} %pad_add_fusion.place_ref, bf16[8,2048,256]{2,1,0:T(8,128)(2,1)} %source_ref.3, bf16[2,2048,256]{2,1,0:T(8,128)(2,1)S(1)} %copy-done.9, bf16[16,16,128,128]{3,2,1,0:T(8,128)(2,1)} %refs_2_.5, ...), custom_call_target="tpu_custom_call", output_to_operand_aliasing={{}: (6, {})} | custom-call | flops 12884901888 | bytes 18874368 | tf_op jit(solution)/shard_map/alpha_term/pallas_call | solution.py:209
  386.3 55.1 %collective-permute-done.4.refs_1_ = bf16[4,2048,256]{2,1,0:T(8,128)(2,1)} collective-permute-done((bf16[4,2048,256]{2,1,0:T(8,128)(2,1)}, bf16[4,2048,256]{2,1,0:T(8,128)(2,1)}, u32[]{:S(2)}, u32[]{:S(2)}) %collective-permute-start.4) | collective-permute-done | bytes 4194336 | tf_op jit(solution)/shard_map/ppermute | solution.py:296
  441.4 26.5 %alpha_term.5.acc_ref = f32[8,2048,256]{2,1,0:T(8,128)} custom-call(s32[256]{0:T(256)S(1)} %reshape.27.cols_ref, s32[4]{0:T(128)S(1)} %pad_add_fusion.place_ref, bf16[8,2048,256]{2,1,0:T(8,128)(2,1)} %source_ref.3, bf16[4,2048,256]{2,1,0:T(8,128)(2,1)} %collective-permute-done.4.refs_1_, ...), custom_call_target="tpu_custom_call", output_to_operand_aliasing={{}: (6, {})} | custom-call | flops 25769803776 | bytes 27262976 | tf_op jit(solution)/shard_map/alpha_term/pallas_call | solution.py:209
  467.9 5.8 %copy-done.2 = f32[8,2048,256]{2,1,0:T(8,128)S(1)} copy-done((f32[8,2048,256]{2,1,0:T(8,128)S(1)}, f32[8,2048,256]{2,1,0:T(8,128)}, u32[]{:S(2)}) %copy-start.2) | copy-done | bytes 16777240
  476.3 9.0 %all-to-all-done.3 = s16[8,1536,256]{2,1,0:T(8,128)(2,1)} async-done(((s16[8,1536,256]{2,1,0:T(8,128)(2,1)}), s16[8,1536,256]{2,1,0:T(8,128)(2,1)}, u32[]{:S(2)}, u32[]{:S(2)}) %all-to-all-start.3) | async-done | bytes 6291488 | tf_op jit(solution)/shard_map/all_to_all | solution.py:345
  485.3 11.4 %join_terms.3 = bf16[8,2048,256]{2,1,0:T(8,128)(2,1)} custom-call(f32[8,2048,256]{2,1,0:T(8,128)} %alpha_term.5.acc_ref, s16[8,2,6,128,256]{4,3,2,1,0:T(8,128)(2,1)} %bitcast.7.words_ref, bf16[8,2048,256]{2,1,0:T(8,128)(2,1)} %join_terms.2.rest_0_), custom_call_target="tpu_custom_call", output_to_operand_aliasing={{}: (2, {})} | custom-call | flops 25165824 | bytes 25165824 | tf_op jit(solution)/shard_map/join_terms/pallas_call | solution.py:254
  (63 shorter events, 35.5 us)
Async XLA Ops:
  6.5 12.9 %copy-start = (bf16[2,16,128,128]{3,2,1,0:T(8,128)(2,1)S(1)}, bf16[2,16,128,128]{3,2,1,0:T(8,128)(2,1)}, u32[]{:S(2)}) copy-start(bf16[2,16,128,128]{3,2,1,0:T(8,128)(2,1)} %param.9) | copy-start | bytes 3145732
  7.4 3.4 copy-start.3
  12.8 90.5 %all-to-all-start = ((bf16[16,272,256]{2,1,0:T(8,128)(2,1)}), bf16[16,272,256]{2,1,0:T(8,128)(2,1)S(1)}, u32[]{:S(2)}, u32[]{:S(2)}) async-start(bf16[16,272,256]{2,1,0:T(8,128)(2,1)} %pack_pieces.2), calls=%async_computation | async-start | bytes 4456448 | tf_op jit(solution)/shard_map/all_to_all | solution.py:319
  19.3 78.5 %all-gather.2.cloned.1.call-start = ((), (), s32[]{:S(2)}) async-start(), calls=%async_computation.4 | async-start | bytes 2621440 | tf_op jit(solution)/shard_map/all_gather | solution.py:305
  26.1 46.9 %collective-permute-start.6 = (bf16[2,2048,256]{2,1,0:T(8,128)(2,1)S(1)}, bf16[2,2048,256]{2,1,0:T(8,128)(2,1)S(1)}, u32[]{:S(2)}, u32[]{:S(2)}) collective-permute-start(bf16[2,2048,256]{2,1,0:T(8,128)(2,1)S(1)} %get-tuple-element.21), channel_id=1, source_target_pairs={{16,0},{0,16},{17,1},{1,17},{18,2},{2,18},{19,3},{3,19},{20,4},{4,... | collective-permute-start | bytes 6291464 | tf_op jit(solution)/shard_map/ppermute | solution.py:296
  27.4 3.5 copy-start.4
  31.8 2.7 copy-start.5
  104.7 174.4 %all-to-all-start.1 = ((bf16[16,768,256]{2,1,0:T(8,128)(2,1)}), bf16[16,768,256]{2,1,0:T(8,128)(2,1)}, u32[]{:S(2)}, u32[]{:S(2)}) async-start(bf16[16,768,256]{2,1,0:T(8,128)(2,1)} %copy-done.5), calls=%async_computation.1 | async-start | bytes 12582912 | tf_op jit(solution)/shard_map/all_to_all | solution.py:319
  109.6 5.1 %copy-start.13 = (bf16[4,2048,128]{2,1,0:T(8,128)(2,1)S(1)}, bf16[4,2048,128]{2,1,0:T(8,128)(2,1)}, u32[]{:S(2)}) copy-start(bf16[4,2048,128]{2,1,0:T(8,128)(2,1)} %all-gather.2.cloned.1.call-done.refs_2_) | copy-start | bytes 6291460
  109.6 105.3 %collective-permute-start.2 = (bf16[16,272,256]{2,1,0:T(8,128)(2,1)}, bf16[16,272,256]{2,1,0:T(8,128)(2,1)}, u32[]{:S(2)}, u32[]{:S(2)}) collective-permute-start(bf16[16,272,256]{2,1,0:T(8,128)(2,1)} %copy-done.18), channel_id=1, source_target_pairs={{0,1},{1,0},{2,3},{3,2},{4,5},{5,4},{6,7},{7,6},{8,9},{9,8},{10,11... | collective-permute-start | bytes 6684680 | tf_op jit(solution)/shard_map/ppermute | solution.py:289
  114.6 47.3 %collective-permute-start.1 = (bf16[4,2048,128]{2,1,0:T(8,128)(2,1)S(1)}, bf16[4,2048,128]{2,1,0:T(8,128)(2,1)S(1)}, u32[]{:S(2)}, u32[]{:S(2)}) collective-permute-start(bf16[4,2048,128]{2,1,0:T(8,128)(2,1)S(1)} %copy-done.13), channel_id=1, source_target_pairs={{0,16},{16,0},{1,17},{17,1},{2,18},{18,2},{3,19},{19,3},{4,20},{20... | collective-permute-start | bytes 6291464 | tf_op jit(solution)/shard_map/ppermute | solution.py:292
  115.9 99.0 %collective-permute-start = (bf16[4,2048,128]{2,1,0:T(8,128)(2,1)S(1)}, bf16[4,2048,128]{2,1,0:T(8,128)(2,1)}, u32[]{:S(2)}, u32[]{:S(2)}) collective-permute-start(bf16[4,2048,128]{2,1,0:T(8,128)(2,1)S(1)} %copy-done.13), channel_id=1, source_target_pairs={{0,2},{1,3},{2,0},{3,1},{4,6},{5,7},{6,4},{7,5},{8,10},{9,11},{10,... | collective-permute-start | bytes 6291464 | tf_op jit(solution)/shard_map/ppermute | solution.py:289
  214.9 46.6 %collective-permute-start.3 = (bf16[4,2048,128]{2,1,0:T(8,128)(2,1)}, bf16[4,2048,128]{2,1,0:T(8,128)(2,1)}, u32[]{:S(2)}, u32[]{:S(2)}) collective-permute-start(bf16[4,2048,128]{2,1,0:T(8,128)(2,1)} %collective-permute-done.refs_4_), channel_id=1, source_target_pairs={{0,16},{16,0},{1,17},{17,1},{2,18},{18,2},{3,19},{19,3},{4,20},{20... | collective-permute-start | bytes 6291464 | tf_op jit(solution)/shard_map/ppermute | solution.py:292
  279.1 15.5 %collective-permute-start.7 = (bf16[16,768,256]{2,1,0:T(8,128)(2,1)}, bf16[16,768,256]{2,1,0:T(8,128)(2,1)}, u32[]{:S(2)}, u32[]{:S(2)}) collective-permute-start(bf16[16,768,256]{2,1,0:T(8,128)(2,1)} %all-to-all-done.1.refs_0_), channel_id=1, source_target_pairs={{0,1},{1,0},{2,3},{3,2},{4,5},{5,4},{6,7},{7,6},{8,9},{9,8},{10,11... | collective-permute-start | bytes 18874376 | tf_op jit(solution)/shard_map/ppermute | solution.py:289
  280.8 60.9 %all-to-all-start.2 = ((s16[8,512,256]{2,1,0:T(8,128)(2,1)}), s16[8,512,256]{2,1,0:T(8,128)(2,1)S(1)}, u32[]{:S(2)}, u32[]{:S(2)}) async-start(s16[8,512,256]{2,1,0:T(8,128)(2,1)} %copy-done.10), calls=%async_computation.2 | async-start | bytes 4194304 | tf_op jit(solution)/shard_map/all_to_all | solution.py:345
  293.3 47.2 %collective-permute-start.5 = (bf16[2,2048,256]{2,1,0:T(8,128)(2,1)}, bf16[2,2048,256]{2,1,0:T(8,128)(2,1)S(1)}, u32[]{:S(2)}, u32[]{:S(2)}) collective-permute-start(bf16[2,2048,256]{2,1,0:T(8,128)(2,1)} %get-tuple-element.16), channel_id=1, source_target_pairs={{16,0},{0,16},{17,1},{1,17},{18,2},{2,18},{19,3},{3,19},{20,4},{4,... | collective-permute-start | bytes 6291464 | tf_op jit(solution)/shard_map/ppermute | solution.py:296
  338.7 12.2 %copy-start.19 = (s32[16,16]{1,0:T(8,128)S(1)}, s32[16,16]{1,0:T(8,128)}, u32[]{:S(2)}) copy-start(s32[16,16]{1,0:T(8,128)} %param.8) | copy-start | bytes 3076
  341.8 143.5 %all-to-all-start.3 = ((s16[8,1536,256]{2,1,0:T(8,128)(2,1)}), s16[8,1536,256]{2,1,0:T(8,128)(2,1)}, u32[]{:S(2)}, u32[]{:S(2)}) async-start(s16[8,1536,256]{2,1,0:T(8,128)(2,1)} %beta_term.3), calls=%async_computation.3 | async-start | bytes 12582912 | tf_op jit(solution)/shard_map/all_to_all | solution.py:345
  349.7 91.8 %collective-permute-start.4 = (bf16[4,2048,256]{2,1,0:T(8,128)(2,1)}, bf16[4,2048,256]{2,1,0:T(8,128)(2,1)}, u32[]{:S(2)}, u32[]{:S(2)}) collective-permute-start(bf16[4,2048,256]{2,1,0:T(8,128)(2,1)} %slice.12), channel_id=1, source_target_pairs={{16,0},{0,16},{17,1},{1,17},{18,2},{2,18},{19,3},{3,19},{20,4},{4,... | collective-permute-start | bytes 12582920 | tf_op jit(solution)/shard_map/ppermute | solution.py:296
  351.0 1.6 copy-start.6
  354.2 16.2 %copy-start.7 = (f32[2048,256]{1,0:T(8,128)S(1)}, f32[2048,256]{1,0:T(8,128)}, u32[]{:S(2)}) copy-start(f32[2048,256]{1,0:T(8,128)} %refs_3_.5) | copy-start | bytes 6291460
  354.2 16.2 %copy-start.9 = (bf16[2,2048,256]{2,1,0:T(8,128)(2,1)S(1)}, bf16[2,2048,256]{2,1,0:T(8,128)(2,1)}, u32[]{:S(2)}) copy-start(bf16[2,2048,256]{2,1,0:T(8,128)(2,1)} %copy-done.8) | copy-start | bytes 6291460
  467.9 5.8 %copy-start.2 = (f32[8,2048,256]{2,1,0:T(8,128)S(1)}, f32[8,2048,256]{2,1,0:T(8,128)}, u32[]{:S(2)}) copy-start(f32[8,2048,256]{2,1,0:T(8,128)} %alpha_term.5.acc_ref) | copy-start | bytes 50331652
  485.3 11.4 %copy-start.1 = (bf16[2,16,128,128]{3,2,1,0:T(8,128)(2,1)S(1)}, bf16[2,16,128,128]{3,2,1,0:T(8,128)(2,1)}, u32[]{:S(2)}) copy-start(bf16[2,16,128,128]{3,2,1,0:T(8,128)(2,1)} %param.9) | copy-start | bytes 3145732
  (9 other events, 13.1 us)
Sparse Core Ops, SparseCore 0:
  22.4 75.3 all-gather.1

commit v5 on v4

--- a/solution.py
+++ b/solution.py
@@ -14,6 +14,7 @@
 CODE_BITS = 11
 LARGEST = 32767.0
 TILE = 16
+HINTS = (42, 4)
 CORES = 2
 ANYWHERE = pl.BlockSpec(memory_space=pl.ANY)
 
@@ -35,13 +36,20 @@
     return head.astype(jnp.int16)
 
 
-def from_words(words):
+def bit_weights():
+    lane = lax.broadcasted_iota(jnp.int32, (128, 128), 0)
+    weight = jnp.where(lane < CODE_BITS, lax.shift_left(jnp.ones_like(lane), jnp.minimum(lane, CODE_BITS)), 0)
+    return weight.astype(jnp.float32).astype(jnp.bfloat16)
+
+
+def from_words(words, weights):
     words = words.astype(jnp.int32)
-    head = words[:, :128]
-    lane = lax.broadcasted_iota(jnp.int32, head.shape, 1)
-    bits = jnp.where(lane < CODE_BITS, lax.shift_left(head & 1, jnp.minimum(lane, CODE_BITS)), 0)
-    code = jnp.sum(bits.astype(jnp.float32), axis=1, keepdims=True).astype(jnp.int32)
-    return words.astype(jnp.float32) * (row_scale(code) * (1.0 / LARGEST))
+    bits = (words[:, :128] & 1).astype(jnp.float32).astype(jnp.bfloat16)
+    code = jnp.dot(bits, weights, preferred_element_type=jnp.float32)
+    scale = jnp.exp2((code - SHIFT) * (1.0 / STEPS_PER_OCTAVE)) * (1.0 / LARGEST)
+    if words.shape[1] > 128:
+        scale = jnp.concatenate([scale] * (words.shape[1] // 128), axis=1)
+    return words.astype(jnp.float32) * scale
 
 
 def pack_kernel(source_ref, *refs):
@@ -131,7 +139,7 @@
     out_ref[0] = to_words(term)
 
 
-def beta_term(slots, xs, columns, place, own, twin, messages, rows):
+def beta_term(slots, xs, columns, place, own, twin, messages, rows, hint):
     sources, _, strip = own.shape
     outer, half, block = messages[0].shape
     dests = outer * xs
@@ -155,7 +163,7 @@
         out_shape=jax.ShapeDtypeStruct((dests, both, strip), jnp.int16),
         compiler_params=pltpu.CompilerParams(vmem_limit_bytes=44 * MIB),
         cost_estimate=pl.CostEstimate(
-            flops=4 * dests * both * strip * slots * block,
+            flops=hint * dests * both * strip * slots * block,
             bytes_accessed=8 * half * block * dests + 4 * count * both * block,
             transcendentals=0,
         ),
@@ -229,10 +237,11 @@
 
 def join_kernel(few_rows, acc_ref, words_ref, *rest):
     out_ref = rest[-1]
+    weights = bit_weights()
     for j in range(words_ref.shape[0]):
         for c in range(CORES):
             here = pl.ds((j * CORES + c) * few_rows, few_rows)
-            out_ref[0, here, :] = (acc_ref[0, here, :] + from_words(words_ref[j, c, 0])).astype(jnp.bfloat16)
+            out_ref[0, here, :] = (acc_ref[0, here, :] + from_words(words_ref[j, c, 0], weights)).astype(jnp.bfloat16)
 
 
 def join(acc, words, first, vectors, before):
@@ -314,8 +323,7 @@
     turned = []
     for i, (first, count) in enumerate(cuts):
         piece = pack(ci_vectors, heads if i == 0 else None, first, count, ring)
-        if i > 0:
-            piece = after(piece, (turned[i - 1], gathered, others[0][-1]))
+        piece = after(piece, (turned[i - 1], gathered, others[0][-1]) if i > 0 else mine)
         turned.append(lax.all_to_all(piece, "beta", split_axis=0, concat_axis=0, tiled=True))
     columns = turned[0][:, cuts[0][1] * few_rows, : owned * slots].reshape(-1).astype(jnp.int32)
     twins = [swap(turned[0], 1)]
@@ -340,7 +348,7 @@
     for i, (first, count) in enumerate(cuts):
         if i > 0:
             twins.append(swap(after(turned[i], term), 1))
-        term = beta_term(slots, xs, columns, place, turned[i], twins[i], messages, count * few_rows)
+        term = beta_term(slots, xs, columns, place, turned[i], twins[i], messages, count * few_rows, HINTS[i])
         term = after(term, last if i == 0 else (last, others[1][-1]))
         words = lax.all_to_all(term, "beta", split_axis=0, concat_axis=0, tiled=True, axis_index_groups=near)
         last = words

time: 508 us -> 480 us (0.945)
  starting transfers between devices: 40.5 us -> 25.3 us
  waiting for transfers between devices: 275 us -> 265 us
    all_to_all x2, waiting for transfers between devices: 5.46 us -> 101 us  [shards(): lax.all_to_all(piece, 'beta', split_axis=0, concat_axis=0, tiled=True)]
    ppermute x3, waiting for transfers between devices: 95.4 us -> 56.5 us  [exchange(): lax.ppermute(value, 'alpha', [((i + s) % ring_a, i) for i in range(ring_a)])]
    ppermute x3, waiting for transfers between devices: 51.6 us -> 23.4 us  [swap(): return lax.ppermute(value, 'beta', [(i, i ^ bit) for i in range(ring)])]
    all_gather x1, waiting for transfers between devices: 23.5 us -> 0.01 us  [shards(): lax.all_gather(mine, 'beta', axis=0, tiled=False, axis_index_groups=far)]
    ppermute x2, waiting for transfers between devices: 90.2 us -> 75.5 us  [across(): return lax.ppermute(value, 'alpha', [(i, i ^ 1) for i in range(ring_a)])]
    all_to_all x2, starting transfers between devices: 20.3 us -> 9.09 us  [shards(): lax.all_to_all(term, 'beta', split_axis=0, concat_axis=0, tiled=True, axi...]
    unnamed x40 -> x36, local copies, waits for them, and re-layouts: 30 us -> 28.5 us
  transfers between devices with their start and end apart: 13 -> 13, of which waited for: 9 -> 8; matrix products, arithmetic and copies ran while one was open for 2% -> 2% of each run, Pallas kernels for 23% -> 25%
where the time goes in v5:
time: 480 us; the launch traced here: 475 us
  waiting for transfers between devices  265 us (55%)
  Pallas kernels  131 us (27%)
  local copies, waits for them, and re-layouts  38.7 us (8%)
  starting transfers between devices  25.3 us (5%)
  between operations  13.5 us (3%)
    all_to_all x2, waiting for transfers between devices, shards(): lax.all_to_all(piece, 'beta', split_axis=0, concat_axis=0, tiled=True)  101 us
    ppermute x2, waiting for transfers between devices, across(): return lax.ppermute(value, 'alpha', [(i, i ^ 1) for i in range(ring_a)])  75.5 us
    pallas_call x3, Pallas kernels, alpha_term(): pl.pallas_call(functools.partial(alpha_kernel, pieces), grid_spec=pltpu.P...  58.6 us
    ppermute x3, waiting for transfers between devices, exchange(): lax.ppermute(value, 'alpha', [((i + s) % ring_a, i) for i in range(ring_a)])  56.5 us
    pallas_call x2, Pallas kernels, beta_term(): pl.pallas_call(functools.partial(beta_kernel, slots, xs), grid_spec=pltpu...  55.8 us
    unnamed x36, local copies, waits for them, and re-layouts  28.5 us
    ppermute x3, waiting for transfers between devices, swap(): return lax.ppermute(value, 'beta', [(i, i ^ bit) for i in range(ring)])  23.4 us
    pallas_call x2, Pallas kernels, join(): pl.pallas_call(functools.partial(join_kernel, few_rows), grid=(count,), i...  13.4 us
  transfers between devices with their start and end apart: 13, of which 8 were waited for; matrix products, arithmetic and copies ran while one was open for 2% of the time, Pallas kernels for 25%

profile of v5, /device:TPU:11, one launch (start us, length us, event | category | flops | bytes accessed | tf_op | source)
XLA Modules:
  0.0 475.0 jit_solution(7590836789565528852)
XLA Ops:
  7.4 3.4 copy-done.3
  12.8 6.6 %all-to-all-start = ((bf16[16,272,256]{2,1,0:T(8,128)(2,1)}), bf16[16,272,256]{2,1,0:T(8,128)(2,1)}, u32[]{:S(2)}, u32[]{:S(2)}) async-start(bf16[16,272,256]{2,1,0:T(8,128)(2,1)} %pack_pieces.2), calls=%async_computation | async-start | bytes 4456448 | tf_op jit(solution)/shard_map/all_to_all | solution.py:327
  20.5 4.5 fusion.1
  26.2 77.2 %all-to-all-done.refs_0_ = bf16[16,272,256]{2,1,0:T(8,128)(2,1)} async-done(((bf16[16,272,256]{2,1,0:T(8,128)(2,1)}), bf16[16,272,256]{2,1,0:T(8,128)(2,1)}, u32[]{:S(2)}, u32[]{:S(2)}) %all-to-all-start) | async-done | bytes 2228256 | tf_op jit(solution)/shard_map/all_to_all | solution.py:327
  103.6 4.4 slice.12
  109.2 3.4 copy-done.4
  113.6 2.7 copy-done.5
  117.6 6.0 %all-to-all-start.1 = ((bf16[16,768,256]{2,1,0:T(8,128)(2,1)}), bf16[16,768,256]{2,1,0:T(8,128)(2,1)}, u32[]{:S(2)}, u32[]{:S(2)}) async-start(bf16[16,768,256]{2,1,0:T(8,128)(2,1)} %copy-done.5), calls=%async_computation.1 | async-start | bytes 12582912 | tf_op jit(solution)/shard_map/all_to_all | solution.py:327
  123.5 31.7 %collective-permute-done.1.refs_3_ = bf16[4,2048,128]{2,1,0:T(8,128)(2,1)} collective-permute-done((bf16[4,2048,128]{2,1,0:T(8,128)(2,1)}, bf16[4,2048,128]{2,1,0:T(8,128)(2,1)}, u32[]{:S(2)}, u32[]{:S(2)}) %collective-permute-start.1) | collective-permute-done | bytes 2097184 | tf_op jit(solution)/shard_map/ppermute | solution.py:301
  155.2 17.8 %collective-permute-done.refs_4_ = bf16[4,2048,128]{2,1,0:T(8,128)(2,1)} collective-permute-done((bf16[4,2048,128]{2,1,0:T(8,128)(2,1)}, bf16[4,2048,128]{2,1,0:T(8,128)(2,1)}, u32[]{:S(2)}, u32[]{:S(2)}) %collective-permute-start) | collective-permute-done | bytes 2097184 | tf_op jit(solution)/shard_map/ppermute | solution.py:298
  174.2 43.8 %collective-permute-done.3.refs_5_ = bf16[4,2048,128]{2,1,0:T(8,128)(2,1)S(1)} collective-permute-done((bf16[4,2048,128]{2,1,0:T(8,128)(2,1)}, bf16[4,2048,128]{2,1,0:T(8,128)(2,1)S(1)}, u32[]{:S(2)}, u32[]{:S(2)}) %collective-permute-start.3) | collective-permute-done | bytes 2097184 | tf_op jit(solution)/shard_map/ppermute | solution.py:301
  220.9 14.9 %beta_term.2 = s16[8,512,256]{2,1,0:T(8,128)(2,1)S(1)} custom-call(s32[512]{0:T(512)S(1)} %reshape.31.cols_ref, s32[4]{0:T(128)S(1)} %pad_add_fusion.place_ref, bf16[16,272,256]{2,1,0:T(8,128)(2,1)} %all-to-all-done.refs_0_, bf16[16,272,256]{2,1,0:T(8,128)(2,1)} %collective-permute-done.2.refs_1_, bf16[4,2048,128]{2,1,0:T(8,128)(2,1)S(1)} %copy-done.13, ...), custom_call_target="tpu_custom_call" | custom-call | flops 90194313216 | bytes 25165824 | tf_op jit(solution)/shard_map/beta_term/pallas_call | solution.py:149
  237.1 23.9 %all-to-all-done.1.refs_0_ = bf16[16,768,256]{2,1,0:T(8,128)(2,1)} async-done(((bf16[16,768,256]{2,1,0:T(8,128)(2,1)}), bf16[16,768,256]{2,1,0:T(8,128)(2,1)}, u32[]{:S(2)}, u32[]{:S(2)}) %all-to-all-start.1) | async-done | bytes 6291488 | tf_op jit(solution)/shard_map/all_to_all | solution.py:327
  261.2 4.4 all-to-all-start.2
  265.8 5.7 %collective-permute-done.7.refs_1_ = bf16[16,768,256]{2,1,0:T(8,128)(2,1)} collective-permute-done((bf16[16,768,256]{2,1,0:T(8,128)(2,1)}, bf16[16,768,256]{2,1,0:T(8,128)(2,1)}, u32[]{:S(2)}, u32[]{:S(2)}) %collective-permute-start.7) | collective-permute-done | bytes 6291488 | tf_op jit(solution)/shard_map/ppermute | solution.py:298
  274.7 40.9 %beta_term.3 = s16[8,1536,256]{2,1,0:T(8,128)(2,1)} custom-call(s32[512]{0:T(512)S(1)} %reshape.31.cols_ref, s32[4]{0:T(128)S(1)} %pad_add_fusion.place_ref, bf16[16,768,256]{2,1,0:T(8,128)(2,1)} %all-to-all-done.1.refs_0_, bf16[16,768,256]{2,1,0:T(8,128)(2,1)} %collective-permute-done.7.refs_1_, bf16[4,2048,128]{2,1,0:T(8,128)(2,1)S(1)} %copy-done.14, ...), custom_call_target="tpu_custom_call" | custom-call | flops 25769803776 | bytes 41943040 | tf_op jit(solution)/shard_map/beta_term/pallas_call | solution.py:149
  317.0 4.7 all-to-all-start.3
  325.3 16.1 %alpha_term.3.refs_4_ = f32[8,2048,256]{2,1,0:T(8,128)} custom-call(s32[256]{0:T(256)S(1)} %reshape.28.cols_ref, s32[4]{0:T(128)S(1)} %pad_add_fusion.place_ref, bf16[8,2048,256]{2,1,0:T(8,128)(2,1)} %source_ref.3, bf16[2,2048,256]{2,1,0:T(8,128)(2,1)S(1)} %copy-done.12, bf16[16,16,128,128]{3,2,1,0:T(8,128)(2,1)} %refs_2_.5, f32[2048,256]{1,0:T(8,128)S(1)} %copy-done.6), custom_call_target="tpu_custom_call" | custom-call | flops 12884901888 | bytes 18874368 | tf_op jit(solution)/shard_map/alpha_term/pallas_call | solution.py:217
  341.4 15.9 %alpha_term.4.refs_4_ = f32[8,2048,256]{2,1,0:T(8,128)} custom-call(s32[256]{0:T(256)S(1)} %reshape.28.cols_ref, s32[4]{0:T(128)S(1)} %pad_add_fusion.place_ref, bf16[8,2048,256]{2,1,0:T(8,128)(2,1)} %source_ref.3, bf16[2,2048,256]{2,1,0:T(8,128)(2,1)S(1)} %copy-done.9, bf16[16,16,128,128]{3,2,1,0:T(8,128)(2,1)} %refs_2_.5, ...), custom_call_target="tpu_custom_call", output_to_operand_aliasing={{}: (6, {})} | custom-call | flops 12884901888 | bytes 18874368 | tf_op jit(solution)/shard_map/alpha_term/pallas_call | solution.py:217
  357.4 56.5 %collective-permute-done.4.refs_1_ = bf16[4,2048,256]{2,1,0:T(8,128)(2,1)} collective-permute-done((bf16[4,2048,256]{2,1,0:T(8,128)(2,1)}, bf16[4,2048,256]{2,1,0:T(8,128)(2,1)}, u32[]{:S(2)}, u32[]{:S(2)}) %collective-permute-start.4) | collective-permute-done | bytes 4194336 | tf_op jit(solution)/shard_map/ppermute | solution.py:305
  413.8 26.5 %alpha_term.5.acc_ref = f32[8,2048,256]{2,1,0:T(8,128)} custom-call(s32[256]{0:T(256)S(1)} %reshape.28.cols_ref, s32[4]{0:T(128)S(1)} %pad_add_fusion.place_ref, bf16[8,2048,256]{2,1,0:T(8,128)(2,1)} %source_ref.3, bf16[4,2048,256]{2,1,0:T(8,128)(2,1)} %collective-permute-done.4.refs_1_, ...), custom_call_target="tpu_custom_call", output_to_operand_aliasing={{}: (6, {})} | custom-call | flops 25769803776 | bytes 27262976 | tf_op jit(solution)/shard_map/alpha_term/pallas_call | solution.py:217
  440.3 5.8 %copy-done.2 = f32[8,2048,256]{2,1,0:T(8,128)S(1)} copy-done((f32[8,2048,256]{2,1,0:T(8,128)S(1)}, f32[8,2048,256]{2,1,0:T(8,128)}, u32[]{:S(2)}) %copy-start.2) | copy-done | bytes 16777240
  448.4 8.7 %all-to-all-done.3 = s16[8,1536,256]{2,1,0:T(8,128)(2,1)} async-done(((s16[8,1536,256]{2,1,0:T(8,128)(2,1)}), s16[8,1536,256]{2,1,0:T(8,128)(2,1)}, u32[]{:S(2)}, u32[]{:S(2)}) %all-to-all-start.3) | async-done | bytes 6291488 | tf_op jit(solution)/shard_map/all_to_all | solution.py:353
  457.1 11.0 %join_terms.3 = bf16[8,2048,256]{2,1,0:T(8,128)(2,1)} custom-call(f32[8,2048,256]{2,1,0:T(8,128)} %alpha_term.5.acc_ref, s16[8,2,6,128,256]{4,3,2,1,0:T(8,128)(2,1)} %bitcast.7.words_ref, bf16[8,2048,256]{2,1,0:T(8,128)(2,1)} %join_terms.2.rest_0_), custom_call_target="tpu_custom_call", output_to_operand_aliasing={{}: (2, {})} | custom-call | flops 25165824 | bytes 25165824 | tf_op jit(solution)/shard_map/join_terms/pallas_call | solution.py:263
  (59 shorter events, 25.2 us)
Async XLA Ops:
  6.5 12.8 %copy-start = (bf16[2,16,128,128]{3,2,1,0:T(8,128)(2,1)S(1)}, bf16[2,16,128,128]{3,2,1,0:T(8,128)(2,1)}, u32[]{:S(2)}) copy-start(bf16[2,16,128,128]{3,2,1,0:T(8,128)(2,1)} %param.9) | copy-start | bytes 3145732
  7.4 3.4 copy-start.3
  12.8 90.6 %all-to-all-start = ((bf16[16,272,256]{2,1,0:T(8,128)(2,1)}), bf16[16,272,256]{2,1,0:T(8,128)(2,1)}, u32[]{:S(2)}, u32[]{:S(2)}) async-start(bf16[16,272,256]{2,1,0:T(8,128)(2,1)} %pack_pieces.2), calls=%async_computation | async-start | bytes 4456448 | tf_op jit(solution)/shard_map/all_to_all | solution.py:327
  19.3 88.7 %all-gather.2.cloned.1.call-start = ((), (), s32[]{:S(2)}) async-start(), calls=%async_computation.4 | async-start | bytes 2621440 | tf_op jit(solution)/shard_map/all_gather | solution.py:314
  24.9 91.3 %collective-permute-start.6 = (bf16[2,2048,256]{2,1,0:T(8,128)(2,1)}, bf16[2,2048,256]{2,1,0:T(8,128)(2,1)S(1)}, u32[]{:S(2)}, u32[]{:S(2)}) collective-permute-start(bf16[2,2048,256]{2,1,0:T(8,128)(2,1)} %get-tuple-element.21), channel_id=1, source_target_pairs={{16,0},{0,16},{17,1},{1,17},{18,2},{2,18},{19,3},{3,19},{20,4},{4,... | collective-permute-start | bytes 6291464 | tf_op jit(solution)/shard_map/ppermute | solution.py:305
  103.4 69.6 %collective-permute-start.2 = (bf16[16,272,256]{2,1,0:T(8,128)(2,1)}, bf16[16,272,256]{2,1,0:T(8,128)(2,1)}, u32[]{:S(2)}, u32[]{:S(2)}) collective-permute-start(bf16[16,272,256]{2,1,0:T(8,128)(2,1)} %all-to-all-done.refs_0_), channel_id=1, source_target_pairs={{0,1},{1,0},{2,3},{3,2},{4,5},{5,4},{6,7},{7,6},{8,9},{9,8},{10,11... | collective-permute-start | bytes 6684680 | tf_op jit(solution)/shard_map/ppermute | solution.py:298
  108.0 47.2 %collective-permute-start.1 = (bf16[4,2048,128]{2,1,0:T(8,128)(2,1)}, bf16[4,2048,128]{2,1,0:T(8,128)(2,1)}, u32[]{:S(2)}, u32[]{:S(2)}) collective-permute-start(bf16[4,2048,128]{2,1,0:T(8,128)(2,1)} %all-gather.2.cloned.1.call-done.refs_2_), channel_id=1, source_target_pairs={{0,16},{16,0},{1,17},{17,1},{2,18},{18,2},{3,19},{19,3},{4,20},{20... | collective-permute-start | bytes 6291464 | tf_op jit(solution)/shard_map/ppermute | solution.py:301
  109.2 63.8 %collective-permute-start = (bf16[4,2048,128]{2,1,0:T(8,128)(2,1)}, bf16[4,2048,128]{2,1,0:T(8,128)(2,1)}, u32[]{:S(2)}, u32[]{:S(2)}) collective-permute-start(bf16[4,2048,128]{2,1,0:T(8,128)(2,1)} %all-gather.2.cloned.1.call-done.refs_2_), channel_id=1, source_target_pairs={{0,2},{1,3},{2,0},{3,1},{4,6},{5,7},{6,4},{7,5},{8,10},{9,11},{10,... | collective-permute-start | bytes 6291464 | tf_op jit(solution)/shard_map/ppermute | solution.py:298
  109.2 3.4 copy-start.4
  113.5 2.7 copy-start.5
  117.6 143.5 %all-to-all-start.1 = ((bf16[16,768,256]{2,1,0:T(8,128)(2,1)}), bf16[16,768,256]{2,1,0:T(8,128)(2,1)}, u32[]{:S(2)}, u32[]{:S(2)}) async-start(bf16[16,768,256]{2,1,0:T(8,128)(2,1)} %copy-done.5), calls=%async_computation.1 | async-start | bytes 12582912 | tf_op jit(solution)/shard_map/all_to_all | solution.py:327
  173.0 45.0 %collective-permute-start.3 = (bf16[4,2048,128]{2,1,0:T(8,128)(2,1)}, bf16[4,2048,128]{2,1,0:T(8,128)(2,1)S(1)}, u32[]{:S(2)}, u32[]{:S(2)}) collective-permute-start(bf16[4,2048,128]{2,1,0:T(8,128)(2,1)} %collective-permute-done.refs_4_), channel_id=1, source_target_pairs={{0,16},{16,0},{1,17},{17,1},{2,18},{18,2},{3,19},{19,3},{4,20},{20... | collective-permute-start | bytes 6291464 | tf_op jit(solution)/shard_map/ppermute | solution.py:301
  261.0 10.5 %collective-permute-start.7 = (bf16[16,768,256]{2,1,0:T(8,128)(2,1)}, bf16[16,768,256]{2,1,0:T(8,128)(2,1)}, u32[]{:S(2)}, u32[]{:S(2)}) collective-permute-start(bf16[16,768,256]{2,1,0:T(8,128)(2,1)} %all-to-all-done.1.refs_0_), channel_id=1, source_target_pairs={{0,1},{1,0},{2,3},{3,2},{4,5},{5,4},{6,7},{7,6},{8,9},{9,8},{10,11... | collective-permute-start | bytes 18874376 | tf_op jit(solution)/shard_map/ppermute | solution.py:298
  261.2 55.8 %all-to-all-start.2 = ((s16[8,512,256]{2,1,0:T(8,128)(2,1)}), s16[8,512,256]{2,1,0:T(8,128)(2,1)S(1)}, u32[]{:S(2)}, u32[]{:S(2)}) async-start(s16[8,512,256]{2,1,0:T(8,128)(2,1)} %copy-done.10), calls=%async_computation.2 | async-start | bytes 4194304 | tf_op jit(solution)/shard_map/all_to_all | solution.py:353
  265.6 50.0 %collective-permute-start.5 = (bf16[2,2048,256]{2,1,0:T(8,128)(2,1)}, bf16[2,2048,256]{2,1,0:T(8,128)(2,1)S(1)}, u32[]{:S(2)}, u32[]{:S(2)}) collective-permute-start(bf16[2,2048,256]{2,1,0:T(8,128)(2,1)} %get-tuple-element.16), channel_id=1, source_target_pairs={{16,0},{0,16},{17,1},{1,17},{18,2},{2,18},{19,3},{3,19},{20,4},{4,... | collective-permute-start | bytes 6291464 | tf_op jit(solution)/shard_map/ppermute | solution.py:305
  271.5 1.6 copy-start.14
  315.7 6.4 %copy-start.17 = (s32[16,16]{1,0:T(8,128)S(1)}, s32[16,16]{1,0:T(8,128)}, u32[]{:S(2)}) copy-start(s32[16,16]{1,0:T(8,128)} %param.8) | copy-start | bytes 3076
  317.0 140.1 %all-to-all-start.3 = ((s16[8,1536,256]{2,1,0:T(8,128)(2,1)}), s16[8,1536,256]{2,1,0:T(8,128)(2,1)}, u32[]{:S(2)}, u32[]{:S(2)}) async-start(s16[8,1536,256]{2,1,0:T(8,128)(2,1)} %beta_term.3), calls=%async_computation.3 | async-start | bytes 12582912 | tf_op jit(solution)/shard_map/all_to_all | solution.py:353
  321.7 92.1 %collective-permute-start.4 = (bf16[4,2048,256]{2,1,0:T(8,128)(2,1)}, bf16[4,2048,256]{2,1,0:T(8,128)(2,1)}, u32[]{:S(2)}, u32[]{:S(2)}) collective-permute-start(bf16[4,2048,256]{2,1,0:T(8,128)(2,1)} %slice.12), channel_id=1, source_target_pairs={{16,0},{0,16},{17,1},{1,17},{18,2},{2,18},{19,3},{3,19},{20,4},{4,... | collective-permute-start | bytes 12582920 | tf_op jit(solution)/shard_map/ppermute | solution.py:305
  322.1 1.6 copy-start.6
  325.3 16.1 %copy-start.7 = (f32[2048,256]{1,0:T(8,128)S(1)}, f32[2048,256]{1,0:T(8,128)}, u32[]{:S(2)}) copy-start(f32[2048,256]{1,0:T(8,128)} %refs_3_.5) | copy-start | bytes 6291460
  325.3 16.1 %copy-start.9 = (bf16[2,2048,256]{2,1,0:T(8,128)(2,1)S(1)}, bf16[2,2048,256]{2,1,0:T(8,128)(2,1)}, u32[]{:S(2)}) copy-start(bf16[2,2048,256]{2,1,0:T(8,128)(2,1)} %copy-done.8) | copy-start | bytes 6291460
  440.3 5.8 %copy-start.2 = (f32[8,2048,256]{2,1,0:T(8,128)S(1)}, f32[8,2048,256]{2,1,0:T(8,128)}, u32[]{:S(2)}) copy-start(f32[8,2048,256]{2,1,0:T(8,128)} %alpha_term.5.acc_ref) | copy-start | bytes 50331652
  457.1 11.0 %copy-start.1 = (bf16[2,16,128,128]{3,2,1,0:T(8,128)(2,1)S(1)}, bf16[2,16,128,128]{3,2,1,0:T(8,128)(2,1)}, u32[]{:S(2)}) copy-start(bf16[2,16,128,128]{3,2,1,0:T(8,128)(2,1)} %param.9) | copy-start | bytes 3145732
  (7 other events, 10.1 us)
Sparse Core Ops, SparseCore 0:
  21.7 76.0 all-gather.1

commit v6 on v5

--- a/solution.py
+++ b/solution.py
@@ -15,6 +15,7 @@
 LARGEST = 32767.0
 TILE = 16
 HINTS = (42, 4)
+VMEM = 60 * MIB
 CORES = 2
 ANYWHERE = pl.BlockSpec(memory_space=pl.ANY)
 
@@ -80,37 +81,66 @@
         in_specs=in_specs,
         out_specs=pl.BlockSpec((each, depth, strip), lambda d: (d, 0, 0)),
         out_shape=jax.ShapeDtypeStruct((ring, depth, strip), jnp.bfloat16),
-        compiler_params=pltpu.CompilerParams(vmem_limit_bytes=24 * MIB),
+        compiler_params=pltpu.CompilerParams(vmem_limit_bytes=VMEM),
         cost_estimate=pl.CostEstimate(flops=0, bytes_accessed=4 * ring * depth * strip, transcendentals=0),
         name="pack_pieces",
     )(*args)
 
 
+def turn_kernel(place_ref, blocks_ref, out_ref):
+    _, count, block, _ = blocks_ref.shape
+    for k in range(count):
+        out_ref[k * block : (k + 1) * block, :] = blocks_ref[0, k].T
+
+
+def turn_half(place, stored):
+    _, count, block, _ = stored.shape
+    return pl.pallas_call(
+        turn_kernel,
+        grid_spec=pltpu.PrefetchScalarGridSpec(
+            num_scalar_prefetch=1,
+            grid=(1,),
+            in_specs=[pl.BlockSpec((1, count, block, block), lambda g, place_ref: (place_ref[2], 0, 0, 0))],
+            out_specs=pl.BlockSpec((count * block, block), lambda g, place_ref: (0, 0)),
+        ),
+        out_shape=jax.ShapeDtypeStruct((count * block, block), jnp.bfloat16),
+        compiler_params=pltpu.CompilerParams(vmem_limit_bytes=VMEM),
+        cost_estimate=pl.CostEstimate(flops=0, bytes_accessed=4 * count * block * block, transcendentals=0),
+        name="turn_blocks",
+    )(place, stored)
+
+
+def row_tile(rows):
+    return max(t for t in range(TILE, 513, TILE) if rows % t == 0)
+
+
 def beta_kernel(slots, xs, cols_ref, place_ref, *refs):
-    own_ref, twin_ref = refs[:2]
+    sources_of_rows = refs[:2]
     message_refs = refs[2:-5]
     out_ref, picked_ref, blocks_ref, picked_sem, blocks_sem = refs[-5:]
     block = blocks_ref.shape[-1]
-    sources = own_ref.shape[0]
-    per_strip = own_ref.shape[2] // block
-    _, both_rows, _ = picked_ref.shape
-    rows = both_rows // CORES
+    sources = sources_of_rows[0].shape[0]
+    per_strip = sources_of_rows[0].shape[2] // block
+    size = out_ref.shape[1]
+    tiles = picked_ref.shape[0]
     half = blocks_ref.shape[1] // 2
     outer = message_refs[0].shape[0]
-    dest, tile = pl.program_id(0), pl.program_id(1)
+    tile, dest = pl.program_id(0), pl.program_id(1)
     core, x_here, parity = place_ref[0], place_ref[1], place_ref[2]
 
-    @pl.when((dest == 0) & (tile == 0))
+    def fetch_rows(t):
+        ref, at = sources_of_rows[t // (tiles // CORES)], t % (tiles // CORES) * size
+        for src in range(sources):
+            for s in range(per_strip):
+                pltpu.make_async_copy(
+                    ref.at[src, pl.ds(at, size), pl.ds(s * block, block)],
+                    picked_ref.at[t, src * per_strip + s],
+                    picked_sem.at[t],
+                ).start()
+
+    @pl.when((tile == 0) & (dest == 0))
     def _():
-        for which, ref in enumerate((own_ref, twin_ref)):
-            at = pl.multiple_of((core ^ which) * rows, rows)
-            for src in range(sources):
-                for s in range(per_strip):
-                    pltpu.make_async_copy(
-                        ref.at[src, pl.ds(0, rows), pl.ds(s * block, block)],
-                        picked_ref.at[src * per_strip + s, pl.ds(at, rows)],
-                        picked_sem,
-                    ).start()
+        fetch_rows(0)
         for z in range(outer):
             for q in range(xs):
                 for r in range(2):
@@ -119,19 +149,22 @@
                     pltpu.make_async_copy(
                         message_refs[q * 2 + r].at[z], blocks_ref.at[d, pl.ds(at, half)], blocks_sem.at[d]
                     ).start()
-        pltpu.make_async_copy(picked_ref, picked_ref, picked_sem).wait()
+        for t in range(1, tiles):
+            fetch_rows(t)
+
+    @pl.when(dest == 0)
+    def _():
+        pltpu.make_async_copy(picked_ref.at[tile], picked_ref.at[tile], picked_sem.at[tile]).wait()
 
     @pl.when(tile == 0)
     def _():
         pltpu.make_async_copy(blocks_ref.at[dest], blocks_ref.at[dest], blocks_sem.at[dest]).wait()
 
-    size = out_ref.shape[1]
-    here = pl.ds(pl.multiple_of(tile * size, size), size)
     strip = dest * CORES + core
     parts = []
     for n in range(per_strip):
         wide = jnp.concatenate(
-            [picked_ref[cols_ref[(strip * per_strip + n) * slots + k], here, :] for k in range(slots)], axis=1
+            [picked_ref[tile, cols_ref[(strip * per_strip + n) * slots + k]] for k in range(slots)], axis=1
         )
         tall = blocks_ref[dest, n * slots * block : (n + 1) * slots * block, :]
         parts.append(jnp.dot(wide, tall, preferred_element_type=jnp.float32))
@@ -144,24 +177,30 @@
     outer, half, block = messages[0].shape
     dests = outer * xs
     both = rows * CORES
-    size = math.gcd(both, 512)
+    size = row_tile(rows)
+    per_core = rows // size
+    tiles = CORES * per_core
     count = sources * strip // block
+
+    def out_at(t, d, cols_ref, place_ref):
+        return d, (place_ref[0] ^ (t // per_core)) * per_core + t % per_core, 0
+
     return pl.pallas_call(
         functools.partial(beta_kernel, slots, xs),
         grid_spec=pltpu.PrefetchScalarGridSpec(
             num_scalar_prefetch=2,
-            grid=(dests, both // size),
+            grid=(tiles, dests),
             in_specs=[ANYWHERE] * (2 + len(messages)),
-            out_specs=pl.BlockSpec((1, size, strip), lambda d, m, *_: (d, m, 0)),
+            out_specs=pl.BlockSpec((1, size, strip), out_at),
             scratch_shapes=[
-                pltpu.VMEM((count, both, block), jnp.bfloat16),
+                pltpu.VMEM((tiles, count, size, block), jnp.bfloat16),
                 pltpu.VMEM((dests, 2 * half, block), jnp.bfloat16),
-                pltpu.SemaphoreType.DMA,
+                pltpu.SemaphoreType.DMA((tiles,)),
                 pltpu.SemaphoreType.DMA((dests,)),
             ],
         ),
         out_shape=jax.ShapeDtypeStruct((dests, both, strip), jnp.int16),
-        compiler_params=pltpu.CompilerParams(vmem_limit_bytes=44 * MIB),
+        compiler_params=pltpu.CompilerParams(vmem_limit_bytes=VMEM),
         cost_estimate=pl.CostEstimate(
             flops=hint * dests * both * strip * slots * block,
             bytes_accessed=8 * half * block * dests + 4 * count * both * block,
@@ -225,7 +264,7 @@
         ),
         out_shape=jax.ShapeDtypeStruct((vectors, rows, strip), jnp.float32),
         input_output_aliases=aliases,
-        compiler_params=pltpu.CompilerParams(vmem_limit_bytes=44 * MIB),
+        compiler_params=pltpu.CompilerParams(vmem_limit_bytes=VMEM),
         cost_estimate=pl.CostEstimate(
             flops=6 * count * rows * strip * slots * block,
             bytes_accessed=count * rows * strip * (2 * pieces + 4) + blocks.size * 2 + diagonal.size * 4,
@@ -250,10 +289,9 @@
     few_rows = rows // (sources * CORES)
     words = words.reshape(sources, CORES, -1, few_rows, strip)
     count = words.shape[2]
-    in_specs = [
-        pl.BlockSpec((1, rows, strip), lambda v: (first + v, 0, 0)),
-        pl.BlockSpec((sources, CORES, 1, few_rows, strip), lambda v: (0, 0, v, 0, 0)),
-    ]
+    cut = 2
+    here = pl.BlockSpec((1, rows // cut, strip), lambda v, h: (first + v, h, 0))
+    in_specs = [here, pl.BlockSpec((sources // cut, CORES, 1, few_rows, strip), lambda v, h: (h, 0, v, 0, 0))]
     args = [acc, words]
     aliases = {}
     if before is not None:
@@ -262,12 +300,12 @@
         aliases = {2: 0}
     return pl.pallas_call(
         functools.partial(join_kernel, few_rows),
-        grid=(count,),
+        grid=(count, cut),
         in_specs=in_specs,
-        out_specs=pl.BlockSpec((1, rows, strip), lambda v: (first + v, 0, 0)),
+        out_specs=here,
         out_shape=jax.ShapeDtypeStruct((vectors, rows, strip), jnp.bfloat16),
         input_output_aliases=aliases,
-        compiler_params=pltpu.CompilerParams(vmem_limit_bytes=32 * MIB),
+        compiler_params=pltpu.CompilerParams(vmem_limit_bytes=VMEM),
         cost_estimate=pl.CostEstimate(
             flops=8 * count * rows * strip, bytes_accessed=8 * count * rows * strip, transcendentals=0
         ),
@@ -291,7 +329,8 @@
     place = jnp.stack([lax.rem(at_b, CORES), lax.rem(lax.div(at_b, CORES), xs), parity, at_a]).astype(jnp.int32)
     few = vectors // 4
     cuts = [(vectors - few, few), (0, vectors - few)]
-    shares = [(0, few), (few, few), (2 * few, vectors - 2 * few)]
+    early = (3 * vectors) // 8
+    shares = [(0, early), (early, vectors // 2 - early), (vectors // 2, vectors - vectors // 2)]
     sent = [ci_vectors[first : first + count] for first, count in shares]
 
     def swap(value, bit):
@@ -305,25 +344,26 @@
             lax.ppermute(value, "alpha", [((i + s) % ring_a, i) for i in range(ring_a)]) for s in range(1, ring_a)
         ]
 
-    others = [exchange(sent[0])]
-
-    stored = beta_blocks.reshape(2, owned * slots // 2, block, block)
-    mine = lax.dynamic_index_in_dim(stored, parity, 0, keepdims=False)
-    mine = mine.transpose(0, 2, 1).reshape(-1, block)
+    mine = turn_half(place, beta_blocks.reshape(2, owned * slots // 2, block, block))
     far = [[o * inner + i for o in range(outer)] for i in range(inner)]
-    carried = lax.all_gather(mine, "beta", axis=0, tiled=False, axis_index_groups=far)
-    gathered = carried
-    carried = [after(carried, tuple(sent[1:]))]
+    gathered = lax.all_gather(mine, "beta", axis=0, tiled=False, axis_index_groups=far)
+
+    heads = jnp.pad(beta_cols.reshape(1, -1).astype(jnp.bfloat16), ((0, TILE - 1), (0, strip - owned * slots)))
+    pieces = [pack(ci_vectors, heads if i == 0 else None, *cut, ring) for i, cut in enumerate(cuts)]
+    pieces[0] = after(pieces[0], mine)
+
+    others = [exchange(after(sent[0], (pieces[1], *sent[1:])))]
+
+    carried = [gathered]
     bit = CORES
     while bit < inner:
         carried = carried + [swap(m, bit) for m in carried]
         bit *= 2
 
-    heads = jnp.pad(beta_cols.reshape(1, -1).astype(jnp.bfloat16), ((0, TILE - 1), (0, strip - owned * slots)))
     turned = []
-    for i, (first, count) in enumerate(cuts):
-        piece = pack(ci_vectors, heads if i == 0 else None, first, count, ring)
-        piece = after(piece, (turned[i - 1], gathered, others[0][-1]) if i > 0 else mine)
+    for i, piece in enumerate(pieces):
+        if i > 0:
+            piece = after(piece, (turned[i - 1], gathered, others[0][-1]))
         turned.append(lax.all_to_all(piece, "beta", split_axis=0, concat_axis=0, tiled=True))
     columns = turned[0][:, cuts[0][1] * few_rows, : owned * slots].reshape(-1).astype(jnp.int32)
     twins = [swap(turned[0], 1)]

time: 480 us -> 476 us (level)
  local copies, waits for them, and re-layouts: 38.7 us -> 13.8 us
  Pallas kernels: 131 us -> 154 us
  waiting for transfers between devices: 265 us -> 255 us
  starting transfers between devices: 25.3 us -> 32.6 us
    unnamed x36 -> x8, local copies, waits for them, and re-layouts: 28.5 us -> 3.01 us
    all_to_all x2, waiting for transfers between devices: 101 us -> 84.1 us  [shards(): lax.all_to_all(piece, 'beta', split_axis=0, concat_axis=0, tiled=True)]
    pallas_call x2 -> x3, Pallas kernels: 13.4 us -> 21.6 us  [the longest x2 18.8 us: join(): pl.pallas_call(functools.partial(join_kernel, few_rows), grid=(count, cut...]
    all_to_all x2, starting transfers between devices: 9.09 us -> 16.3 us  [shards(): lax.all_to_all(term, 'beta', split_axis=0, concat_axis=0, tiled=True, axi...]
    pallas_call x2, Pallas kernels: 2.89 us -> 9.87 us  [pack(): pl.pallas_call(pack_kernel, grid=(ring // each,), in_specs=in_specs, out_...]
    ppermute x2, waiting for transfers between devices: 75.5 us -> 82.3 us  [across(): return lax.ppermute(value, 'alpha', [(i, i ^ 1) for i in range(ring_a)])]
    pallas_call x2, Pallas kernels: 55.8 us -> 61.5 us  [beta_term(): pl.pallas_call(functools.partial(beta_kernel, slots, xs), grid_spec=pltpu...]
  transfers between devices with their start and end apart: 13 -> 13, of which waited for: 8 -> 8; matrix products, arithmetic and copies ran while one was open for 2% -> 2% of each run, Pallas kernels for 25% -> 28%
where the time goes in v6:
time: 476 us; the launch traced here: 471 us
  waiting for transfers between devices  255 us (54%)
  Pallas kernels  154 us (32%)
  starting transfers between devices  32.6 us (7%)
  local copies, waits for them, and re-layouts  13.8 us (3%)
  between operations  13.5 us (3%)
    all_to_all x2, waiting for transfers between devices, shards(): lax.all_to_all(piece, 'beta', split_axis=0, concat_axis=0, tiled=True)  84.1 us
    ppermute x2, waiting for transfers between devices, across(): return lax.ppermute(value, 'alpha', [(i, i ^ 1) for i in range(ring_a)])  82.3 us
    pallas_call x2, Pallas kernels, beta_term(): pl.pallas_call(functools.partial(beta_kernel, slots, xs), grid_spec=pltpu...  61.5 us
    pallas_call x3, Pallas kernels, alpha_term(): pl.pallas_call(functools.partial(alpha_kernel, pieces), grid_spec=pltpu.P...  61.2 us
    ppermute x3, waiting for transfers between devices, exchange(): lax.ppermute(value, 'alpha', [((i + s) % ring_a, i) for i in range(ring_a)])  56.6 us
    ppermute x3, waiting for transfers between devices, swap(): return lax.ppermute(value, 'beta', [(i, i ^ bit) for i in range(ring)])  19.6 us
    pallas_call x2, Pallas kernels, join(): pl.pallas_call(functools.partial(join_kernel, few_rows), grid=(count, cut...  18.8 us
    all_to_all x2, starting transfers between devices, shards(): lax.all_to_all(term, 'beta', split_axis=0, concat_axis=0, tiled=True, axi...  16.3 us
  transfers between devices with their start and end apart: 13, of which 8 were waited for; matrix products, arithmetic and copies ran while one was open for 2% of the time, Pallas kernels for 28%

profile of v6, /device:TPU:11, one launch (start us, length us, event | category | flops | bytes accessed | tf_op | source)
XLA Modules:
  0.0 471.1 jit_solution(17022044914072168815)
XLA Ops:
  8.5 2.7 turn_blocks.1
  11.2 3.8 pack_pieces.2
  15.0 6.6 %all-to-all-start = ((bf16[16,272,256]{2,1,0:T(8,128)(2,1)}), bf16[16,272,256]{2,1,0:T(8,128)(2,1)}, u32[]{:S(2)}, u32[]{:S(2)}) async-start(bf16[16,272,256]{2,1,0:T(8,128)(2,1)} %pack_pieces.2), calls=%async_computation | async-start | bytes 4456448 | tf_op jit(solution)/shard_map/all_to_all | solution.py:367
  22.3 2.3 slice.13
  24.6 2.1 slice.14
  26.7 4.4 slice.12
  31.1 6.1 %pack_pieces.3 = bf16[16,768,256]{2,1,0:T(8,128)(2,1)} custom-call(bf16[8,2048,256]{2,1,0:T(8,128)(2,1)} %refs_0_.5), custom_call_target="tpu_custom_call" | custom-call | bytes 12582912 | tf_op jit(solution)/shard_map/pack_pieces/pallas_call | solution.py:78
  38.4 67.5 %all-to-all-done.refs_0_ = bf16[16,272,256]{2,1,0:T(8,128)(2,1)} async-done(((bf16[16,272,256]{2,1,0:T(8,128)(2,1)}), bf16[16,272,256]{2,1,0:T(8,128)(2,1)}, u32[]{:S(2)}, u32[]{:S(2)}) %all-to-all-start) | async-done | bytes 2228256 | tf_op jit(solution)/shard_map/all_to_all | solution.py:367
  107.2 6.3 %all-to-all-start.1 = ((bf16[16,768,256]{2,1,0:T(8,128)(2,1)}), bf16[16,768,256]{2,1,0:T(8,128)(2,1)}, u32[]{:S(2)}, u32[]{:S(2)}) async-start(bf16[16,768,256]{2,1,0:T(8,128)(2,1)} %pack_pieces.3), calls=%async_computation.1 | async-start | bytes 12582912 | tf_op jit(solution)/shard_map/all_to_all | solution.py:367
  113.4 39.5 %collective-permute-done.1.refs_3_ = bf16[4,2048,128]{2,1,0:T(8,128)(2,1)} collective-permute-done((bf16[4,2048,128]{2,1,0:T(8,128)(2,1)}, bf16[4,2048,128]{2,1,0:T(8,128)(2,1)}, u32[]{:S(2)}, u32[]{:S(2)}) %collective-permute-start.1) | collective-permute-done | bytes 2097184 | tf_op jit(solution)/shard_map/ppermute | solution.py:340
  152.9 17.8 %collective-permute-done.refs_4_ = bf16[4,2048,128]{2,1,0:T(8,128)(2,1)} collective-permute-done((bf16[4,2048,128]{2,1,0:T(8,128)(2,1)}, bf16[4,2048,128]{2,1,0:T(8,128)(2,1)}, u32[]{:S(2)}, u32[]{:S(2)}) %collective-permute-start) | collective-permute-done | bytes 2097184 | tf_op jit(solution)/shard_map/ppermute | solution.py:337
  172.4 42.8 %collective-permute-done.3.refs_5_ = bf16[4,2048,128]{2,1,0:T(8,128)(2,1)S(1)} collective-permute-done((bf16[4,2048,128]{2,1,0:T(8,128)(2,1)}, bf16[4,2048,128]{2,1,0:T(8,128)(2,1)S(1)}, u32[]{:S(2)}, u32[]{:S(2)}) %collective-permute-start.3) | collective-permute-done | bytes 2097184 | tf_op jit(solution)/shard_map/ppermute | solution.py:340
  216.5 17.8 %beta_term.2 = s16[8,512,256]{2,1,0:T(8,128)(2,1)} custom-call(s32[512]{0:T(512)} %reshape.30.cols_ref, s32[4]{0:T(128)} %pad_add_fusion.place_ref, bf16[16,272,256]{2,1,0:T(8,128)(2,1)} %all-to-all-done.refs_0_, bf16[16,272,256]{2,1,0:T(8,128)(2,1)} %collective-permute-done.2.refs_1_, bf16[4,2048,128]{2,1,0:T(8,128)(2,1)} %bitcast.10, ...), custom_call_target="tpu_custom_call" | custom-call | flops 90194313216 | bytes 25165824 | tf_op jit(solution)/shard_map/beta_term/pallas_call | solution.py:188
  234.4 16.6 %all-to-all-done.1.refs_0_ = bf16[16,768,256]{2,1,0:T(8,128)(2,1)} async-done(((bf16[16,768,256]{2,1,0:T(8,128)(2,1)}), bf16[16,768,256]{2,1,0:T(8,128)(2,1)}, u32[]{:S(2)}, u32[]{:S(2)}) %all-to-all-start.1) | async-done | bytes 6291488 | tf_op jit(solution)/shard_map/all_to_all | solution.py:367
  251.2 8.2 %all-to-all-start.2 = ((s16[8,512,256]{2,1,0:T(8,128)(2,1)}), s16[8,512,256]{2,1,0:T(8,128)(2,1)S(1)}, u32[]{:S(2)}, u32[]{:S(2)}) async-start(s16[8,512,256]{2,1,0:T(8,128)(2,1)} %beta_term.2), calls=%async_computation.2 | async-start | bytes 4194304 | tf_op jit(solution)/shard_map/all_to_all | solution.py:393
  261.5 43.7 %beta_term.3 = s16[8,1536,256]{2,1,0:T(8,128)(2,1)} custom-call(s32[512]{0:T(512)} %reshape.30.cols_ref, s32[4]{0:T(128)} %pad_add_fusion.place_ref, bf16[16,768,256]{2,1,0:T(8,128)(2,1)} %all-to-all-done.1.refs_0_, bf16[16,768,256]{2,1,0:T(8,128)(2,1)} %collective-permute-done.7.refs_1_, bf16[4,2048,128]{2,1,0:T(8,128)(2,1)} %bitcast.11, ...), custom_call_target="tpu_custom_call" | custom-call | flops 25769803776 | bytes 41943040 | tf_op jit(solution)/shard_map/beta_term/pallas_call | solution.py:188
  306.9 8.1 %all-to-all-start.3 = ((s16[8,1536,256]{2,1,0:T(8,128)(2,1)}), s16[8,1536,256]{2,1,0:T(8,128)(2,1)}, u32[]{:S(2)}, u32[]{:S(2)}) async-start(s16[8,1536,256]{2,1,0:T(8,128)(2,1)} %beta_term.3), calls=%async_computation.3 | async-start | bytes 12582912 | tf_op jit(solution)/shard_map/all_to_all | solution.py:393
  315.9 22.1 %alpha_term.3.refs_4_ = f32[8,2048,256]{2,1,0:T(8,128)} custom-call(s32[256]{0:T(256)} %reshape.27.cols_ref, s32[4]{0:T(128)} %pad_add_fusion.place_ref, bf16[8,2048,256]{2,1,0:T(8,128)(2,1)} %refs_0_.5, bf16[3,2048,256]{2,1,0:T(8,128)(2,1)} %collective-permute-done.6.refs_1_, bf16[16,16,128,128]{3,2,1,0:T(8,128)(2,1)} %refs_2_.5, f32[2048,256]{1,0:T(8,128)} %refs_3_.5), custom_call_target="tpu_custom_call" | custom-call | flops 19327352832 | bytes 23068672 | tf_op jit(solution)/shard_map/alpha_term/pallas_call | solution.py:256
  338.0 11.8 %alpha_term.4.refs_4_ = f32[8,2048,256]{2,1,0:T(8,128)} custom-call(s32[256]{0:T(256)} %reshape.27.cols_ref, s32[4]{0:T(128)} %pad_add_fusion.place_ref, bf16[8,2048,256]{2,1,0:T(8,128)(2,1)} %refs_0_.5, bf16[1,2048,256]{2,1,0:T(8,128)(2,1)} %copy-done.1, bf16[16,16,128,128]{3,2,1,0:T(8,128)(2,1)} %refs_2_.5, ...), custom_call_target="tpu_custom_call", output_to_operand_aliasing={{}: (6, {})} | custom-call | flops 6442450944 | bytes 14680064 | tf_op jit(solution)/shard_map/alpha_term/pallas_call | solution.py:256
  349.8 56.6 %collective-permute-done.4.refs_1_ = bf16[4,2048,256]{2,1,0:T(8,128)(2,1)} collective-permute-done((bf16[4,2048,256]{2,1,0:T(8,128)(2,1)}, bf16[4,2048,256]{2,1,0:T(8,128)(2,1)}, u32[]{:S(2)}, u32[]{:S(2)}) %collective-permute-start.4) | collective-permute-done | bytes 4194336 | tf_op jit(solution)/shard_map/ppermute | solution.py:344
  406.4 27.2 %alpha_term.5.acc_ref = f32[8,2048,256]{2,1,0:T(8,128)} custom-call(s32[256]{0:T(256)} %reshape.27.cols_ref, s32[4]{0:T(128)} %pad_add_fusion.place_ref, bf16[8,2048,256]{2,1,0:T(8,128)(2,1)} %refs_0_.5, bf16[4,2048,256]{2,1,0:T(8,128)(2,1)} %collective-permute-done.4.refs_1_, bf16[16,16,128,128]{3,2,1,0:T(8,128)(2,1)} %refs_2_.5, ...), custom_call_target="tpu_custom_call", output_to_operand_aliasing={{}: (6, {})} | custom-call | flops 25769803776 | bytes 27262976 | tf_op jit(solution)/shard_map/alpha_term/pallas_call | solution.py:256
  433.7 5.2 %join_terms.2.rest_0_ = bf16[8,2048,256]{2,1,0:T(8,128)(2,1)} custom-call(f32[8,2048,256]{2,1,0:T(8,128)} %alpha_term.5.acc_ref, s16[8,2,2,128,256]{4,3,2,1,0:T(8,128)(2,1)} %bitcast.7), custom_call_target="tpu_custom_call" | custom-call | flops 8388608 | bytes 8388608 | tf_op jit(solution)/shard_map/join_terms/pallas_call | solution.py:301
  438.8 11.7 %all-to-all-done.3 = s16[8,1536,256]{2,1,0:T(8,128)(2,1)} async-done(((s16[8,1536,256]{2,1,0:T(8,128)(2,1)}), s16[8,1536,256]{2,1,0:T(8,128)(2,1)}, u32[]{:S(2)}, u32[]{:S(2)}) %all-to-all-start.3) | async-done | bytes 6291488 | tf_op jit(solution)/shard_map/all_to_all | solution.py:393
  450.5 13.7 %join_terms.3 = bf16[8,2048,256]{2,1,0:T(8,128)(2,1)} custom-call(f32[8,2048,256]{2,1,0:T(8,128)} %alpha_term.5.acc_ref, s16[8,2,6,128,256]{4,3,2,1,0:T(8,128)(2,1)} %bitcast.5.words_ref, bf16[8,2048,256]{2,1,0:T(8,128)(2,1)} %join_terms.2.rest_0_), custom_call_target="tpu_custom_call", output_to_operand_aliasing={{}: (2, {})} | custom-call | flops 25165824 | bytes 25165824 | tf_op jit(solution)/shard_map/join_terms/pallas_call | solution.py:301
  (31 shorter events, 13.0 us)
Async XLA Ops:
  15.0 90.9 %all-to-all-start = ((bf16[16,272,256]{2,1,0:T(8,128)(2,1)}), bf16[16,272,256]{2,1,0:T(8,128)(2,1)}, u32[]{:S(2)}, u32[]{:S(2)}) async-start(bf16[16,272,256]{2,1,0:T(8,128)(2,1)} %pack_pieces.2), calls=%async_computation | async-start | bytes 4456448 | tf_op jit(solution)/shard_map/all_to_all | solution.py:367
  21.6 84.3 %all-gather.3.cloned.1.call-start = ((), (), s32[]{:S(2)}) async-start(), calls=%async_computation.4 | async-start | bytes 2621440 | tf_op jit(solution)/shard_map/all_gather | solution.py:349
  37.2 70.0 %collective-permute-start.6 = (bf16[3,2048,256]{2,1,0:T(8,128)(2,1)S(1)}, bf16[3,2048,256]{2,1,0:T(8,128)(2,1)}, u32[]{:S(2)}, u32[]{:S(2)}) collective-permute-start(bf16[3,2048,256]{2,1,0:T(8,128)(2,1)S(1)} %slice.14), channel_id=1, source_target_pairs={{16,0},{0,16},{17,1},{1,17},{18,2},{2,18},{19,3},{3,19},{20,4},{4,... | collective-permute-start | bytes 9437192 | tf_op jit(solution)/shard_map/ppermute | solution.py:344
  105.9 64.8 %collective-permute-start.2 = (bf16[16,272,256]{2,1,0:T(8,128)(2,1)}, bf16[16,272,256]{2,1,0:T(8,128)(2,1)}, u32[]{:S(2)}, u32[]{:S(2)}) collective-permute-start(bf16[16,272,256]{2,1,0:T(8,128)(2,1)} %all-to-all-done.refs_0_), channel_id=1, source_target_pairs={{0,1},{1,0},{2,3},{3,2},{4,5},{5,4},{6,7},{7,6},{8,9},{9,8},{10,11... | collective-permute-start | bytes 6684680 | tf_op jit(solution)/shard_map/ppermute | solution.py:337
  105.9 47.0 %collective-permute-start.1 = (bf16[4,2048,128]{2,1,0:T(8,128)(2,1)}, bf16[4,2048,128]{2,1,0:T(8,128)(2,1)}, u32[]{:S(2)}, u32[]{:S(2)}) collective-permute-start(bf16[4,2048,128]{2,1,0:T(8,128)(2,1)} %bitcast.8), channel_id=1, source_target_pairs={{0,16},{16,0},{1,17},{17,1},{2,18},{18,2},{3,19},{19,3},{4,20},{20... | collective-permute-start | bytes 6291464 | tf_op jit(solution)/shard_map/ppermute | solution.py:340
  107.2 63.5 %collective-permute-start = (bf16[4,2048,128]{2,1,0:T(8,128)(2,1)}, bf16[4,2048,128]{2,1,0:T(8,128)(2,1)}, u32[]{:S(2)}, u32[]{:S(2)}) collective-permute-start(bf16[4,2048,128]{2,1,0:T(8,128)(2,1)} %bitcast.9), channel_id=1, source_target_pairs={{0,2},{1,3},{2,0},{3,1},{4,6},{5,7},{6,4},{7,5},{8,10},{9,11},{10,... | collective-permute-start | bytes 6291464 | tf_op jit(solution)/shard_map/ppermute | solution.py:337
  107.2 143.8 %all-to-all-start.1 = ((bf16[16,768,256]{2,1,0:T(8,128)(2,1)}), bf16[16,768,256]{2,1,0:T(8,128)(2,1)}, u32[]{:S(2)}, u32[]{:S(2)}) async-start(bf16[16,768,256]{2,1,0:T(8,128)(2,1)} %pack_pieces.3), calls=%async_computation.1 | async-start | bytes 12582912 | tf_op jit(solution)/shard_map/all_to_all | solution.py:367
  170.7 44.5 %collective-permute-start.3 = (bf16[4,2048,128]{2,1,0:T(8,128)(2,1)}, bf16[4,2048,128]{2,1,0:T(8,128)(2,1)S(1)}, u32[]{:S(2)}, u32[]{:S(2)}) collective-permute-start(bf16[4,2048,128]{2,1,0:T(8,128)(2,1)} %collective-permute-done.refs_4_), channel_id=1, source_target_pairs={{0,16},{16,0},{1,17},{17,1},{2,18},{18,2},{3,19},{19,3},{4,20},{20... | collective-permute-start | bytes 6291464 | tf_op jit(solution)/shard_map/ppermute | solution.py:340
  215.2 1.3 copy-start.3
  251.0 10.5 %collective-permute-start.7 = (bf16[16,768,256]{2,1,0:T(8,128)(2,1)}, bf16[16,768,256]{2,1,0:T(8,128)(2,1)}, u32[]{:S(2)}, u32[]{:S(2)}) collective-permute-start(bf16[16,768,256]{2,1,0:T(8,128)(2,1)} %all-to-all-done.1.refs_0_), channel_id=1, source_target_pairs={{0,1},{1,0},{2,3},{3,2},{4,5},{5,4},{6,7},{7,6},{8,9},{9,8},{10,11... | collective-permute-start | bytes 18874376 | tf_op jit(solution)/shard_map/ppermute | solution.py:337
  251.2 54.0 %all-to-all-start.2 = ((s16[8,512,256]{2,1,0:T(8,128)(2,1)}), s16[8,512,256]{2,1,0:T(8,128)(2,1)S(1)}, u32[]{:S(2)}, u32[]{:S(2)}) async-start(s16[8,512,256]{2,1,0:T(8,128)(2,1)} %beta_term.2), calls=%async_computation.2 | async-start | bytes 4194304 | tf_op jit(solution)/shard_map/all_to_all | solution.py:393
  259.4 45.8 %collective-permute-start.5 = (bf16[1,2048,256]{2,1,0:T(8,128)(2,1)}, bf16[1,2048,256]{2,1,0:T(8,128)(2,1)S(1)}, u32[]{:S(2)}, u32[]{:S(2)}) collective-permute-start(bf16[1,2048,256]{2,1,0:T(8,128)(2,1)} %slice.13), channel_id=1, source_target_pairs={{16,0},{0,16},{17,1},{1,17},{18,2},{2,18},{19,3},{3,19},{20,4},{4,... | collective-permute-start | bytes 3145736 | tf_op jit(solution)/shard_map/ppermute | solution.py:344
  305.2 10.0 %copy-start.2 = (s32[16,16]{1,0:T(8,128)S(1)}, s32[16,16]{1,0:T(8,128)}, u32[]{:S(2)}) copy-start(s32[16,16]{1,0:T(8,128)} %param.8) | copy-start | bytes 3076
  305.2 1.0 copy-start.1
  305.2 1.7 copy-start
  306.9 143.7 %all-to-all-start.3 = ((s16[8,1536,256]{2,1,0:T(8,128)(2,1)}), s16[8,1536,256]{2,1,0:T(8,128)(2,1)}, u32[]{:S(2)}, u32[]{:S(2)}) async-start(s16[8,1536,256]{2,1,0:T(8,128)(2,1)} %beta_term.3), calls=%async_computation.3 | async-start | bytes 12582912 | tf_op jit(solution)/shard_map/all_to_all | solution.py:393
  314.9 91.5 %collective-permute-start.4 = (bf16[4,2048,256]{2,1,0:T(8,128)(2,1)}, bf16[4,2048,256]{2,1,0:T(8,128)(2,1)}, u32[]{:S(2)}, u32[]{:S(2)}) collective-permute-start(bf16[4,2048,256]{2,1,0:T(8,128)(2,1)} %slice.12), channel_id=1, source_target_pairs={{16,0},{0,16},{17,1},{1,17},{18,2},{2,18},{19,3},{3,19},{20,4},{4,... | collective-permute-start | bytes 12582920 | tf_op jit(solution)/shard_map/ppermute | solution.py:344
Sparse Core Ops, SparseCore 0:
  24.0 76.0 all-gather.2

commit v7 on v6

--- a/solution.py
+++ b/solution.py
@@ -14,7 +14,7 @@
 CODE_BITS = 11
 LARGEST = 32767.0
 TILE = 16
-HINTS = (42, 4)
+HINTS = (4, 4)
 VMEM = 60 * MIB
 CORES = 2
 ANYWHERE = pl.BlockSpec(memory_space=pl.ANY)
@@ -110,45 +110,48 @@
     )(place, stored)
 
 
-def row_tile(rows):
-    return max(t for t in range(TILE, 513, TILE) if rows % t == 0)
-
-
-def beta_kernel(slots, xs, cols_ref, place_ref, *refs):
-    sources_of_rows = refs[:2]
-    message_refs = refs[2:-5]
+def beta_kernel(slots, xs, segments, pieces, cols_ref, place_ref, *refs):
+    x_refs = refs[: 2 * len(segments)]
+    message_refs = refs[2 * len(segments) : -5]
     out_ref, picked_ref, blocks_ref, picked_sem, blocks_sem = refs[-5:]
     block = blocks_ref.shape[-1]
-    sources = sources_of_rows[0].shape[0]
-    per_strip = sources_of_rows[0].shape[2] // block
-    size = out_ref.shape[1]
-    tiles = picked_ref.shape[0]
-    half = blocks_ref.shape[1] // 2
+    sources = x_refs[0].shape[0]
+    per_strip = x_refs[0].shape[2] // block
+    tiles, _, size, _ = picked_ref.shape
+    rows = size * tiles // CORES
+    quarter = blocks_ref.shape[1] // (2 * pieces)
     outer = message_refs[0].shape[0]
     tile, dest = pl.program_id(0), pl.program_id(1)
     core, x_here, parity = place_ref[0], place_ref[1], place_ref[2]
 
     def fetch_rows(t):
-        ref, at = sources_of_rows[t // (tiles // CORES)], t % (tiles // CORES) * size
-        for src in range(sources):
-            for s in range(per_strip):
-                pltpu.make_async_copy(
-                    ref.at[src, pl.ds(at, size), pl.ds(s * block, block)],
-                    picked_ref.at[t, src * per_strip + s],
-                    picked_sem.at[t],
-                ).start()
+        for w in range(CORES // tiles):
+            which = t * (CORES // tiles) + w
+            base = 0 if tiles == CORES else (core ^ which) * rows
+            for i, (start, count) in enumerate(segments):
+                at = pl.multiple_of(base + sum(n for _, n in segments[:i]), TILE)
+                for src in range(sources):
+                    for s in range(per_strip):
+                        pltpu.make_async_copy(
+                            x_refs[2 * i + which].at[src, pl.ds(start, count), pl.ds(s * block, block)],
+                            picked_ref.at[t, src * per_strip + s, pl.ds(at, count)],
+                            picked_sem.at[t],
+                        ).start()
 
     @pl.when((tile == 0) & (dest == 0))
     def _():
         fetch_rows(0)
         for z in range(outer):
             for q in range(xs):
-                for r in range(2):
-                    d = z * xs + (x_here ^ q)
-                    at = pl.multiple_of((parity ^ r) * half, half)
-                    pltpu.make_async_copy(
-                        message_refs[q * 2 + r].at[z], blocks_ref.at[d, pl.ds(at, half)], blocks_sem.at[d]
-                    ).start()
+                for p in range(pieces):
+                    for r in range(2):
+                        d = z * xs + (x_here ^ q)
+                        at = pl.multiple_of(((parity ^ r) * pieces + p) * quarter, quarter)
+                        pltpu.make_async_copy(
+                            message_refs[(p * xs + q) * 2 + r].at[z],
+                            blocks_ref.at[d, pl.ds(at, quarter)],
+                            blocks_sem.at[d],
+                        ).start()
         for t in range(1, tiles):
             fetch_rows(t)
 
@@ -172,42 +175,44 @@
     out_ref[0] = to_words(term)
 
 
-def beta_term(slots, xs, columns, place, own, twin, messages, rows, hint):
-    sources, _, strip = own.shape
-    outer, half, block = messages[0].shape
+def beta_term(slots, xs, columns, place, parts, messages, pieces, hint):
+    sources, _, strip = parts[0][0].shape
+    outer, quarter, block = messages[0].shape
     dests = outer * xs
-    both = rows * CORES
-    size = row_tile(rows)
-    per_core = rows // size
-    tiles = CORES * per_core
+    segments = [(start, count) for _, _, start, count in parts]
+    rows = sum(count for _, count in segments)
+    tiles = CORES if rows >= 512 else 1
+    size = rows * CORES // tiles
     count = sources * strip // block
+    depth = 2 * pieces * quarter
+    arrays = [a for own, twin, _, _ in parts for a in (own, twin)] + list(messages)
 
     def out_at(t, d, cols_ref, place_ref):
-        return d, (place_ref[0] ^ (t // per_core)) * per_core + t % per_core, 0
+        return d, place_ref[0] ^ t if tiles == CORES else 0, 0
 
     return pl.pallas_call(
-        functools.partial(beta_kernel, slots, xs),
+        functools.partial(beta_kernel, slots, xs, segments, pieces),
         grid_spec=pltpu.PrefetchScalarGridSpec(
             num_scalar_prefetch=2,
             grid=(tiles, dests),
-            in_specs=[ANYWHERE] * (2 + len(messages)),
+            in_specs=[ANYWHERE] * len(arrays),
             out_specs=pl.BlockSpec((1, size, strip), out_at),
             scratch_shapes=[
                 pltpu.VMEM((tiles, count, size, block), jnp.bfloat16),
-                pltpu.VMEM((dests, 2 * half, block), jnp.bfloat16),
+                pltpu.VMEM((dests, depth, block), jnp.bfloat16),
                 pltpu.SemaphoreType.DMA((tiles,)),
                 pltpu.SemaphoreType.DMA((dests,)),
             ],
         ),
-        out_shape=jax.ShapeDtypeStruct((dests, both, strip), jnp.int16),
+        out_shape=jax.ShapeDtypeStruct((dests, rows * CORES, strip), jnp.int16),
         compiler_params=pltpu.CompilerParams(vmem_limit_bytes=VMEM),
         cost_estimate=pl.CostEstimate(
-            flops=hint * dests * both * strip * slots * block,
-            bytes_accessed=8 * half * block * dests + 4 * count * both * block,
+            flops=hint * dests * rows * CORES * strip * slots * block,
+            bytes_accessed=2 * depth * block * dests + 4 * count * rows * CORES * block,
             transcendentals=0,
         ),
         name="beta_term",
-    )(columns, place, own, twin, *messages)
+    )(columns, place, *arrays)
 
 
 def alpha_kernel(pieces, cols_ref, place_ref, *refs):
@@ -233,8 +238,8 @@
         out_ref[0, here, :] = term + diag_ref[here, :] * own_ref[0, here, :].astype(jnp.float32)
 
 
-def alpha_term(columns, place, own, others, blocks, diagonal, first, count, before):
-    vectors, rows, strip = own.shape
+def alpha_term(columns, place, own, others, blocks, diagonal, first, count, base, total, before):
+    _, rows, strip = own.shape
     owned, slots, block, _ = blocks.shape
     pieces = 1 + len(others)
     once = pl.Buffered(1)
@@ -259,10 +264,10 @@
             num_scalar_prefetch=2,
             grid=(count,),
             in_specs=in_specs,
-            out_specs=mine,
+            out_specs=pl.BlockSpec((1, rows, strip), lambda v, *_: (first - base + v, 0, 0)),
             scratch_shapes=[pltpu.VMEM((pieces * rows, strip), jnp.bfloat16)],
         ),
-        out_shape=jax.ShapeDtypeStruct((vectors, rows, strip), jnp.float32),
+        out_shape=jax.ShapeDtypeStruct((total, rows, strip), jnp.float32),
         input_output_aliases=aliases,
         compiler_params=pltpu.CompilerParams(vmem_limit_bytes=VMEM),
         cost_estimate=pl.CostEstimate(
@@ -284,14 +289,14 @@
 
 
 def join(acc, words, first, vectors, before):
-    _, rows, strip = acc.shape
+    count, rows, strip = acc.shape
     sources = words.shape[0]
     few_rows = rows // (sources * CORES)
-    words = words.reshape(sources, CORES, -1, few_rows, strip)
-    count = words.shape[2]
-    cut = 2
-    here = pl.BlockSpec((1, rows // cut, strip), lambda v, h: (first + v, h, 0))
-    in_specs = [here, pl.BlockSpec((sources // cut, CORES, 1, few_rows, strip), lambda v, h: (h, 0, v, 0, 0))]
+    words = words.reshape(sources, CORES, count, few_rows, strip)
+    in_specs = [
+        pl.BlockSpec((1, rows, strip), lambda v: (v, 0, 0)),
+        pl.BlockSpec((sources, CORES, 1, few_rows, strip), lambda v: (0, 0, v, 0, 0)),
+    ]
     args = [acc, words]
     aliases = {}
     if before is not None:
@@ -300,12 +305,12 @@
         aliases = {2: 0}
     return pl.pallas_call(
         functools.partial(join_kernel, few_rows),
-        grid=(count, cut),
+        grid=(count,),
         in_specs=in_specs,
-        out_specs=here,
+        out_specs=pl.BlockSpec((1, rows, strip), lambda v: (first + v, 0, 0)),
         out_shape=jax.ShapeDtypeStruct((vectors, rows, strip), jnp.bfloat16),
         input_output_aliases=aliases,
-        compiler_params=pltpu.CompilerParams(vmem_limit_bytes=VMEM),
+        compiler_params=pltpu.CompilerParams(vmem_limit_bytes=24 * MIB),
         cost_estimate=pl.CostEstimate(
             flops=8 * count * rows * strip, bytes_accessed=8 * count * rows * strip, transcendentals=0
         ),
@@ -328,10 +333,11 @@
     parity = lax.rem(at_a, 2)
     place = jnp.stack([lax.rem(at_b, CORES), lax.rem(lax.div(at_b, CORES), xs), parity, at_a]).astype(jnp.int32)
     few = vectors // 4
-    cuts = [(vectors - few, few), (0, vectors - few)]
-    early = (3 * vectors) // 8
-    shares = [(0, early), (early, vectors // 2 - early), (vectors // 2, vectors - vectors // 2)]
+    cuts = [(0, vectors - few), (vectors - few, few)]
+    back = [(0, few), (few, vectors - few)]
+    shares = [(0, few), (few, few), (2 * few, vectors - 2 * few)]
     sent = [ci_vectors[first : first + count] for first, count in shares]
+    pieces = 2
 
     def swap(value, bit):
         return lax.ppermute(value, "beta", [(i, i ^ bit) for i in range(ring)])
@@ -346,53 +352,62 @@
 
     mine = turn_half(place, beta_blocks.reshape(2, owned * slots // 2, block, block))
     far = [[o * inner + i for o in range(outer)] for i in range(inner)]
-    gathered = lax.all_gather(mine, "beta", axis=0, tiled=False, axis_index_groups=far)
+    gathered = [
+        lax.all_gather(m, "beta", axis=0, tiled=False, axis_index_groups=far) for m in jnp.split(mine, pieces)
+    ]
 
     heads = jnp.pad(beta_cols.reshape(1, -1).astype(jnp.bfloat16), ((0, TILE - 1), (0, strip - owned * slots)))
-    pieces = [pack(ci_vectors, heads if i == 0 else None, *cut, ring) for i, cut in enumerate(cuts)]
-    pieces[0] = after(pieces[0], mine)
-
-    others = [exchange(after(sent[0], (pieces[1], *sent[1:])))]
-
-    carried = [gathered]
-    bit = CORES
-    while bit < inner:
-        carried = carried + [swap(m, bit) for m in carried]
-        bit *= 2
-
-    turned = []
-    for i, piece in enumerate(pieces):
-        if i > 0:
-            piece = after(piece, (turned[i - 1], gathered, others[0][-1]))
-        turned.append(lax.all_to_all(piece, "beta", split_axis=0, concat_axis=0, tiled=True))
+    packed = [pack(ci_vectors, heads if i == 0 else None, *cut, ring) for i, cut in enumerate(cuts)]
+    packed[0] = after(packed[0], mine)
+
+    others = [exchange(after(sent[0], (packed[1], *sent[1:])))]
+
+    messages = []
+    for g in gathered:
+        carried = [after(g, messages[-2] if messages else others[0][-1])]
+        bit = CORES
+        while bit < inner:
+            carried = carried + [swap(m, bit) for m in carried]
+            bit *= 2
+        for m in carried:
+            messages += [m, across(m)]
+
+    turned = [lax.all_to_all(packed[0], "beta", split_axis=0, concat_axis=0, tiled=True)]
+    ahead = tuple(messages[1:-1])
+    second = after(packed[1], (turned[0], *ahead))
+    turned.append(lax.all_to_all(second, "beta", split_axis=0, concat_axis=0, tiled=True))
     columns = turned[0][:, cuts[0][1] * few_rows, : owned * slots].reshape(-1).astype(jnp.int32)
-    twins = [swap(turned[0], 1)]
-
-    messages = []
-    for m in carried:
-        if messages:
-            m = after(m, (messages[-1], twins[0]))
-        messages += [m, across(m)]
+    twins = [swap(after(turned[0], ahead), 1)]
     for value in sent[1:]:
         others.append(exchange(after(value, messages[-1])))
 
-    acc = None
-    for (first, count), others_now in zip(shares, others):
-        acc = alpha_term(
-            alpha_cols.reshape(-1), place, ci_vectors, others_now, alpha_blocks, diagonal, first, count, acc
+    def alpha(i, base, total, before):
+        return alpha_term(
+            alpha_cols.reshape(-1), place, ci_vectors, others[i], alpha_blocks, diagonal, *shares[i], base, total, before
         )
 
+    acc = [alpha(0, 0, few, None), alpha(2, few, vectors - few, alpha(1, few, vectors - few, None))]
+
     near = [[j * CORES + c for j in range(ring // CORES)] for c in range(CORES)]
+
+    def send_back(term):
+        return lax.all_to_all(term, "beta", split_axis=0, concat_axis=0, tiled=True, axis_index_groups=near)
+
+    rest = cuts[0][1] - few
+    parts = [(turned[0], twins[0], 0, few * few_rows)]
+    term = beta_term(slots, xs, columns, place, parts, messages, pieces, HINTS[0])
+    twins.append(swap(after(turned[1], term), 1))
+    words = [send_back(after(term, turned[1]))]
+    parts = [
+        (turned[0], twins[0], few * few_rows, rest * few_rows),
+        (turned[1], twins[1], 0, few * few_rows),
+    ]
+    term = beta_term(slots, xs, columns, place, parts, messages, pieces, HINTS[1])
+    words.append(send_back(after(term, (words[0], others[1][-1]))))
+
     total = None
-    last = turned[-1]
-    for i, (first, count) in enumerate(cuts):
-        if i > 0:
-            twins.append(swap(after(turned[i], term), 1))
-        term = beta_term(slots, xs, columns, place, turned[i], twins[i], messages, count * few_rows, HINTS[i])
-        term = after(term, last if i == 0 else (last, others[1][-1]))
-        words = lax.all_to_all(term, "beta", split_axis=0, concat_axis=0, tiled=True, axis_index_groups=near)
-        last = words
-        total = join(acc, words, first, vectors, total)
+    for i, (first, _) in enumerate(back):
+        total = join(acc[i], words[i], first, vectors, total)
     return total
 
 

time: 476 us -> 490 us (1.029)
  Pallas kernels: 154 us -> 140 us
  starting transfers between devices: 32.6 us -> 45.2 us
  waiting for transfers between devices: 255 us -> 265 us
    all_gather x1 -> x2, waiting for transfers between devices: 0.01 us -> 124 us  [shards(): lax.all_gather(m, 'beta', axis=0, tiled=False, axis_index_groups=far)]
    all_to_all x4, waiting for transfers between devices: 95.8 us -> 18.6 us  [the longest x2 13.3 us: send_back(): lax.all_to_all(term, 'beta', split_axis=0, concat_axis=0, tiled=True, axi...]
    ppermute x2 -> x4, waiting for transfers between devices: 82.3 us -> 45.8 us  [across(): return lax.ppermute(value, 'alpha', [(i, i ^ 1) for i in range(ring_a)])]
    pallas_call x4, Pallas kernels: 80.3 us -> 66.8 us  [the longest x2 56.2 us: beta_term(): pl.pallas_call(functools.partial(beta_kernel, slots, xs, segments, pieces...]
    ppermute x3 -> x4, starting transfers between devices: 0.22 us -> 8.19 us  [swap(): return lax.ppermute(value, 'beta', [(i, i ^ bit) for i in range(ring)])]
    ppermute x3 -> x4, waiting for transfers between devices: 19.6 us -> 15.1 us  [swap(): return lax.ppermute(value, 'beta', [(i, i ^ bit) for i in range(ring)])]
  transfers between devices with their start and end apart: 13 -> 17, of which waited for: 8 -> 10; matrix products, arithmetic and copies ran while one was open for 2% -> 2% of each run, Pallas kernels for 28% -> 26%
where the time goes in v7:
time: 490 us; the launch traced here: 484 us
  waiting for transfers between devices  265 us (54%)
  Pallas kernels  140 us (29%)
  starting transfers between devices  45.2 us (9%)
  local copies, waits for them, and re-layouts  17.9 us (4%)
  between operations  13.5 us (3%)
    all_gather x2, waiting for transfers between devices, shards(): lax.all_gather(m, 'beta', axis=0, tiled=False, axis_index_groups=far)  124 us
    ppermute x3, waiting for transfers between devices, exchange(): lax.ppermute(value, 'alpha', [((i + s) % ring_a, i) for i in range(ring_a)])  61.3 us
    pallas_call x3, Pallas kernels, alpha_term(): pl.pallas_call(functools.partial(alpha_kernel, pieces), grid_spec=pltpu.P...  61.2 us
    pallas_call x2, Pallas kernels, beta_term(): pl.pallas_call(functools.partial(beta_kernel, slots, xs, segments, pieces...  56.2 us
    ppermute x4, waiting for transfers between devices, across(): return lax.ppermute(value, 'alpha', [(i, i ^ 1) for i in range(ring_a)])  45.8 us
    ppermute x4, waiting for transfers between devices, swap(): return lax.ppermute(value, 'beta', [(i, i ^ bit) for i in range(ring)])  15.1 us
    all_to_all x2, waiting for transfers between devices, send_back(): lax.all_to_all(term, 'beta', split_axis=0, concat_axis=0, tiled=True, axi...  13.3 us
    all_to_all x1, starting transfers between devices, shards(): lax.all_to_all(second, 'beta', split_axis=0, concat_axis=0, tiled=True)  12.5 us
  transfers between devices with their start and end apart: 17, of which 10 were waited for; matrix products, arithmetic and copies ran while one was open for 2% of the time, Pallas kernels for 26%

profile of v7, /device:TPU:11, one launch (start us, length us, event | category | flops | bytes accessed | tf_op | source)
XLA Modules:
  0.0 484.4 jit_solution(16424189181351235431)
XLA Ops:
  11.2 6.0 %pack_pieces.3 = bf16[16,784,256]{2,1,0:T(8,128)(2,1)} custom-call(bf16[8,2048,256]{2,1,0:T(8,128)(2,1)} %refs_0_.5, bf16[16,256]{1,0:T(8,128)(2,1)} %pad.4.refs_0_), custom_call_target="tpu_custom_call" | custom-call | bytes 12845056 | tf_op jit(solution)/shard_map/pack_pieces/pallas_call | solution.py:78
  17.2 6.6 %all-to-all-start = ((bf16[16,784,256]{2,1,0:T(8,128)(2,1)}), bf16[16,784,256]{2,1,0:T(8,128)(2,1)}, u32[]{:S(2)}, u32[]{:S(2)}) async-start(bf16[16,784,256]{2,1,0:T(8,128)(2,1)} %pack_pieces.3), calls=%async_computation | async-start | bytes 12845056 | tf_op jit(solution)/shard_map/all_to_all | solution.py:375
  27.6 4.5 slice.12
  38.8 66.7 %all-gather.7.cloned.1.call-done = bf16[4096,128]{1,0:T(8,128)(2,1)} async-done(((bf16[1024,128]{1,0:T(8,128)(2,1)}), bf16[4096,128]{1,0:T(8,128)(2,1)}) %all-gather.7.cloned.1.call-update) | async-done | bytes 1048592 | tf_op jit(solution)/shard_map/all_gather | solution.py:356
  106.7 56.9 %all-gather.5.cloned.1.call-done = bf16[4096,128]{1,0:T(8,128)(2,1)} async-done(((bf16[1024,128]{1,0:T(8,128)(2,1)}), bf16[4096,128]{1,0:T(8,128)(2,1)}) %all-gather.5.cloned.1.call-update) | async-done | bytes 1048592 | tf_op jit(solution)/shard_map/all_gather | solution.py:356
  164.9 6.7 %collective-permute-start.2 = (bf16[4,1024,128]{2,1,0:T(8,128)(2,1)}, bf16[4,1024,128]{2,1,0:T(8,128)(2,1)}, u32[]{:S(2)}, u32[]{:S(2)}) collective-permute-start(bf16[4,1024,128]{2,1,0:T(8,128)(2,1)} %bitcast.14), channel_id=1, source_target_pairs={{0,2},{1,3},{2,0},{3,1},{4,6},{5,7},{6,4},{7,5},{8,10},{9,11},{10,... | collective-permute-start | bytes 3145736 | tf_op jit(solution)/shard_map/ppermute | solution.py:343
  171.8 16.4 %collective-permute-done.8.refs_7_.refs_9_ = bf16[4,1024,128]{2,1,0:T(8,128)(2,1)} collective-permute-done((bf16[4,1024,128]{2,1,0:T(8,128)(2,1)}, bf16[4,1024,128]{2,1,0:T(8,128)(2,1)}, u32[]{:S(2)}, u32[]{:S(2)}) %collective-permute-start.8) | collective-permute-done | bytes 1048608 | tf_op jit(solution)/shard_map/ppermute | solution.py:346
  188.2 15.1 %collective-permute-done.2.refs_8_.refs_10_ = bf16[4,1024,128]{2,1,0:T(8,128)(2,1)} collective-permute-done((bf16[4,1024,128]{2,1,0:T(8,128)(2,1)}, bf16[4,1024,128]{2,1,0:T(8,128)(2,1)}, u32[]{:S(2)}, u32[]{:S(2)}) %collective-permute-start.2) | collective-permute-done | bytes 1048608 | tf_op jit(solution)/shard_map/ppermute | solution.py:343
  203.4 7.3 %collective-permute-done.7.refs_5_.refs_7_ = bf16[4,1024,128]{2,1,0:T(8,128)(2,1)} collective-permute-done((bf16[4,1024,128]{2,1,0:T(8,128)(2,1)S(1)}, bf16[4,1024,128]{2,1,0:T(8,128)(2,1)}, u32[]{:S(2)}, u32[]{:S(2)}) %collective-permute-start.7) | collective-permute-done | bytes 1048608 | tf_op jit(solution)/shard_map/ppermute | solution.py:346
  212.0 12.5 %all-to-all-start.1 = ((bf16[16,256,256]{2,1,0:T(8,128)(2,1)}), bf16[16,256,256]{2,1,0:T(8,128)(2,1)}, u32[]{:S(2)}, u32[]{:S(2)}) async-start(bf16[16,256,256]{2,1,0:T(8,128)(2,1)} %pack_pieces.2), calls=%async_computation.1 | async-start | bytes 4194304 | tf_op jit(solution)/shard_map/all_to_all | solution.py:378
  227.2 22.0 %collective-permute-done.3.refs_9_.refs_11_ = bf16[4,1024,128]{2,1,0:T(8,128)(2,1)} collective-permute-done((bf16[4,1024,128]{2,1,0:T(8,128)(2,1)}, bf16[4,1024,128]{2,1,0:T(8,128)(2,1)}, u32[]{:S(2)}, u32[]{:S(2)}) %collective-permute-start.3) | collective-permute-done | bytes 1048608 | tf_op jit(solution)/shard_map/ppermute | solution.py:346
  249.3 17.5 %beta_term.2 = s16[8,512,256]{2,1,0:T(8,128)(2,1)} custom-call(s32[512]{0:T(512)} %reshape.30.cols_ref, s32[4]{0:T(128)} %pad_add_fusion.place_ref, bf16[16,784,256]{2,1,0:T(8,128)(2,1)} %all-to-all-done.refs_0_, bf16[16,784,256]{2,1,0:T(8,128)(2,1)} %collective-permute-done.9.refs_1_, bf16[4,1024,128]{2,1,0:T(8,128)(2,1)} %bitcast.11, ...), custom_call_target="tpu_custom_call" | custom-call | flops 8589934592 | bytes 16777216 | tf_op jit(solution)/shard_map/beta_term/pallas_call | solution.py:193
  266.8 5.3 %all-to-all-done.1.refs_2_ = bf16[16,256,256]{2,1,0:T(8,128)(2,1)} async-done(((bf16[16,256,256]{2,1,0:T(8,128)(2,1)}), bf16[16,256,256]{2,1,0:T(8,128)(2,1)}, u32[]{:S(2)}, u32[]{:S(2)}) %all-to-all-start.1) | async-done | bytes 2097184 | tf_op jit(solution)/shard_map/all_to_all | solution.py:378
  272.3 4.5 all-to-all-start.2
  278.0 38.7 %beta_term.3 = s16[8,1536,256]{2,1,0:T(8,128)(2,1)} custom-call(s32[512]{0:T(512)} %reshape.30.cols_ref, s32[4]{0:T(128)} %pad_add_fusion.place_ref, bf16[16,784,256]{2,1,0:T(8,128)(2,1)} %all-to-all-done.refs_0_, bf16[16,784,256]{2,1,0:T(8,128)(2,1)} %collective-permute-done.9.refs_1_, bf16[16,256,256]{2,1,0:T(8,128)(2,1)} %all-to-all-done.1.refs_2_, ...), custom_call_target="tpu_custom_call" | custom-call | flops 25769803776 | bytes 33554432 | tf_op jit(solution)/shard_map/beta_term/pallas_call | solution.py:193
  316.7 6.6 %collective-permute-done.5.refs_1_ = bf16[2,2048,256]{2,1,0:T(8,128)(2,1)} collective-permute-done((bf16[2,2048,256]{2,1,0:T(8,128)(2,1)}, bf16[2,2048,256]{2,1,0:T(8,128)(2,1)}, u32[]{:S(2)}, u32[]{:S(2)}) %collective-permute-start.5) | collective-permute-done | bytes 2097184 | tf_op jit(solution)/shard_map/ppermute | solution.py:350
  323.4 5.8 %all-to-all-start.3 = ((s16[8,1536,256]{2,1,0:T(8,128)(2,1)}), s16[8,1536,256]{2,1,0:T(8,128)(2,1)}, u32[]{:S(2)}, u32[]{:S(2)}) async-start(s16[8,1536,256]{2,1,0:T(8,128)(2,1)} %beta_term.3), calls=%async_computation.3 | async-start | bytes 12582912 | tf_op jit(solution)/shard_map/all_to_all | solution.py:394
  331.1 16.9 %alpha_term.5.acc_ref = f32[2,2048,256]{2,1,0:T(8,128)} custom-call(s32[256]{0:T(256)} %reshape.27.cols_ref, s32[4]{0:T(128)} %pad_add_fusion.place_ref, bf16[8,2048,256]{2,1,0:T(8,128)(2,1)} %refs_0_.5, bf16[2,2048,256]{2,1,0:T(8,128)(2,1)} %collective-permute-done.refs_1_, bf16[16,16,128,128]{3,2,1,0:T(8,128)(2,1)} %refs_2_.5, f32[2048,256]{1,0:T(8,128)} %refs_3_.5), custom_call_target="tpu_custom_call" | custom-call | flops 12884901888 | bytes 18874368 | tf_op jit(solution)/shard_map/alpha_term/pallas_call | solution.py:261
  348.0 16.9 %alpha_term.3.refs_4_ = f32[6,2048,256]{2,1,0:T(8,128)} custom-call(s32[256]{0:T(256)} %reshape.27.cols_ref, s32[4]{0:T(128)} %pad_add_fusion.place_ref, bf16[8,2048,256]{2,1,0:T(8,128)(2,1)} %refs_0_.5, bf16[2,2048,256]{2,1,0:T(8,128)(2,1)} %collective-permute-done.5.refs_1_, bf16[16,16,128,128]{3,2,1,0:T(8,128)(2,1)} %refs_2_.5, f32[2048,256]{1,0:T(8,128)} %refs_3_.5), custom_call_target="tpu_custom_call" | custom-call | flops 12884901888 | bytes 18874368 | tf_op jit(solution)/shard_map/alpha_term/pallas_call | solution.py:261
  364.9 54.7 %collective-permute-done.4.refs_1_ = bf16[4,2048,256]{2,1,0:T(8,128)(2,1)} collective-permute-done((bf16[4,2048,256]{2,1,0:T(8,128)(2,1)}, bf16[4,2048,256]{2,1,0:T(8,128)(2,1)}, u32[]{:S(2)}, u32[]{:S(2)}) %collective-permute-start.4) | collective-permute-done | bytes 4194336 | tf_op jit(solution)/shard_map/ppermute | solution.py:350
  419.6 27.3 %alpha_term.4.acc_ref = f32[6,2048,256]{2,1,0:T(8,128)} custom-call(s32[256]{0:T(256)} %reshape.27.cols_ref, s32[4]{0:T(128)} %pad_add_fusion.place_ref, bf16[8,2048,256]{2,1,0:T(8,128)(2,1)} %refs_0_.5, bf16[4,2048,256]{2,1,0:T(8,128)(2,1)} %collective-permute-done.4.refs_1_, bf16[16,16,128,128]{3,2,1,0:T(8,128)(2,1)} %refs_2_.5, ...), custom_call_target="tpu_custom_call", output_to_operand_aliasing={{}: (6, {})} | custom-call | flops 25769803776 | bytes 27262976 | tf_op jit(solution)/shard_map/alpha_term/pallas_call | solution.py:261
  451.5 13.3 %all-to-all-done.3 = s16[8,1536,256]{2,1,0:T(8,128)(2,1)} async-done(((s16[8,1536,256]{2,1,0:T(8,128)(2,1)}), s16[8,1536,256]{2,1,0:T(8,128)(2,1)}, u32[]{:S(2)}, u32[]{:S(2)}) %all-to-all-start.3) | async-done | bytes 6291488 | tf_op jit(solution)/shard_map/all_to_all | solution.py:394
  464.8 4.6 copy-done
  469.3 8.2 %join_terms.3 = bf16[8,2048,256]{2,1,0:T(8,128)(2,1)} custom-call(f32[6,2048,256]{2,1,0:T(8,128)S(1)} %copy-done, s16[8,2,6,128,256]{4,3,2,1,0:T(8,128)(2,1)} %bitcast.6.words_ref, bf16[8,2048,256]{2,1,0:T(8,128)(2,1)} %join_terms.2.rest_0_), custom_call_target="tpu_custom_call", output_to_operand_aliasing={{}: (2, {})} | custom-call | flops 25165824 | bytes 25165824 | tf_op jit(solution)/shard_map/join_terms/pallas_call | solution.py:306
  (44 shorter events, 29.7 us)
Async XLA Ops:
  17.2 193.5 %all-to-all-start = ((bf16[16,784,256]{2,1,0:T(8,128)(2,1)}), bf16[16,784,256]{2,1,0:T(8,128)(2,1)}, u32[]{:S(2)}, u32[]{:S(2)}) async-start(bf16[16,784,256]{2,1,0:T(8,128)(2,1)} %pack_pieces.3), calls=%async_computation | async-start | bytes 12845056 | tf_op jit(solution)/shard_map/all_to_all | solution.py:375
  23.7 81.8 %all-gather.7.cloned.1.call-start = ((), (), s32[]{:S(2)}) async-start(), calls=%async_computation.5 | async-start | bytes 1310720 | tf_op jit(solution)/shard_map/all_gather | solution.py:356
  32.1 5.1 %copy-start.2 = (bf16[2048,128]{1,0:T(8,128)(2,1)S(1)}, bf16[2048,128]{1,0:T(8,128)(2,1)}, u32[]{:S(2)}) copy-start(bf16[2048,128]{1,0:T(8,128)(2,1)} %turn_blocks.1) | copy-start | bytes 1572868
  35.9 69.6 %collective-permute-start = (bf16[2,2048,256]{2,1,0:T(8,128)(2,1)S(1)}, bf16[2,2048,256]{2,1,0:T(8,128)(2,1)}, u32[]{:S(2)}, u32[]{:S(2)}) collective-permute-start(bf16[2,2048,256]{2,1,0:T(8,128)(2,1)S(1)} %get-tuple-element.16), channel_id=1, source_target_pairs={{16,0},{0,16},{17,1},{1,17},{18,2},{2,18},{19,3},{3,19},{20,4},{4,... | collective-permute-start | bytes 6291464 | tf_op jit(solution)/shard_map/ppermute | solution.py:350
  38.0 125.6 %all-gather.5.cloned.1.call-start = ((), (), s32[]{:S(2)}) async-start(), calls=%async_computation.4 | async-start | bytes 1310720 | tf_op jit(solution)/shard_map/all_gather | solution.py:356
  105.5 58.1 %collective-permute-start.1 = (bf16[4,1024,128]{2,1,0:T(8,128)(2,1)}, bf16[4,1024,128]{2,1,0:T(8,128)(2,1)S(1)}, u32[]{:S(2)}, u32[]{:S(2)}) collective-permute-start(bf16[4,1024,128]{2,1,0:T(8,128)(2,1)} %bitcast.9), channel_id=1, source_target_pairs={{0,2},{1,3},{2,0},{3,1},{4,6},{5,7},{6,4},{7,5},{8,10},{9,11},{10,... | collective-permute-start | bytes 3145736 | tf_op jit(solution)/shard_map/ppermute | solution.py:343
  105.5 66.3 %collective-permute-start.6 = (bf16[4,1024,128]{2,1,0:T(8,128)(2,1)}, bf16[4,1024,128]{2,1,0:T(8,128)(2,1)S(1)}, u32[]{:S(2)}, u32[]{:S(2)}) collective-permute-start(bf16[4,1024,128]{2,1,0:T(8,128)(2,1)} %bitcast.10), channel_id=1, source_target_pairs={{0,16},{16,0},{1,17},{17,1},{2,18},{18,2},{3,19},{19,3},{4,20},{20... | collective-permute-start | bytes 3145736 | tf_op jit(solution)/shard_map/ppermute | solution.py:346
  163.6 85.6 %copy-start.4 = (bf16[4,1024,128]{2,1,0:T(8,128)(2,1)}, bf16[4,1024,128]{2,1,0:T(8,128)(2,1)S(1)}, u32[]{:S(2)}) copy-start(bf16[4,1024,128]{2,1,0:T(8,128)(2,1)S(1)} %collective-permute-done.1.refs_4_.refs_6_) | copy-start | bytes 3145732
  163.7 24.6 %collective-permute-start.8 = (bf16[4,1024,128]{2,1,0:T(8,128)(2,1)}, bf16[4,1024,128]{2,1,0:T(8,128)(2,1)}, u32[]{:S(2)}, u32[]{:S(2)}) collective-permute-start(bf16[4,1024,128]{2,1,0:T(8,128)(2,1)} %bitcast.13), channel_id=1, source_target_pairs={{0,16},{16,0},{1,17},{17,1},{2,18},{18,2},{3,19},{19,3},{4,20},{20... | collective-permute-start | bytes 3145736 | tf_op jit(solution)/shard_map/ppermute | solution.py:346
  164.9 38.5 %collective-permute-start.2 = (bf16[4,1024,128]{2,1,0:T(8,128)(2,1)}, bf16[4,1024,128]{2,1,0:T(8,128)(2,1)}, u32[]{:S(2)}, u32[]{:S(2)}) collective-permute-start(bf16[4,1024,128]{2,1,0:T(8,128)(2,1)} %bitcast.14), channel_id=1, source_target_pairs={{0,2},{1,3},{2,0},{3,1},{4,6},{5,7},{6,4},{7,5},{8,10},{9,11},{10,... | collective-permute-start | bytes 3145736 | tf_op jit(solution)/shard_map/ppermute | solution.py:343
  171.6 39.1 %collective-permute-start.7 = (bf16[4,1024,128]{2,1,0:T(8,128)(2,1)S(1)}, bf16[4,1024,128]{2,1,0:T(8,128)(2,1)}, u32[]{:S(2)}, u32[]{:S(2)}) collective-permute-start(bf16[4,1024,128]{2,1,0:T(8,128)(2,1)S(1)} %collective-permute-done.1.refs_4_.refs_6_), channel_id=1, source_target_pairs={{0,16},{16,0},{1,17},{17,1},{2,18},{18,2},{3,19},{19,3},{4,20},{20... | collective-permute-start | bytes 3145736 | tf_op jit(solution)/shard_map/ppermute | solution.py:346
  171.8 77.4 %copy-start.5 = (bf16[4,1024,128]{2,1,0:T(8,128)(2,1)}, bf16[4,1024,128]{2,1,0:T(8,128)(2,1)S(1)}, u32[]{:S(2)}) copy-start(bf16[4,1024,128]{2,1,0:T(8,128)(2,1)S(1)} %collective-permute-done.6.refs_3_.refs_5_) | copy-start | bytes 3145732
  210.7 38.5 %collective-permute-start.9 = (bf16[16,784,256]{2,1,0:T(8,128)(2,1)}, bf16[16,784,256]{2,1,0:T(8,128)(2,1)}, u32[]{:S(2)}, u32[]{:S(2)}) collective-permute-start(bf16[16,784,256]{2,1,0:T(8,128)(2,1)} %all-to-all-done.refs_0_), channel_id=1, source_target_pairs={{0,1},{1,0},{2,3},{3,2},{4,5},{5,4},{6,7},{7,6},{8,9},{9,8},{10,11... | collective-permute-start | bytes 19267592 | tf_op jit(solution)/shard_map/ppermute | solution.py:343
  212.0 60.0 %all-to-all-start.1 = ((bf16[16,256,256]{2,1,0:T(8,128)(2,1)}), bf16[16,256,256]{2,1,0:T(8,128)(2,1)}, u32[]{:S(2)}, u32[]{:S(2)}) async-start(bf16[16,256,256]{2,1,0:T(8,128)(2,1)} %pack_pieces.2), calls=%async_computation.1 | async-start | bytes 4194304 | tf_op jit(solution)/shard_map/all_to_all | solution.py:378
  224.5 24.7 %collective-permute-start.3 = (bf16[4,1024,128]{2,1,0:T(8,128)(2,1)}, bf16[4,1024,128]{2,1,0:T(8,128)(2,1)}, u32[]{:S(2)}, u32[]{:S(2)}) collective-permute-start(bf16[4,1024,128]{2,1,0:T(8,128)(2,1)} %collective-permute-done.2.refs_8_.refs_10_), channel_id=1, source_target_pairs={{0,16},{16,0},{1,17},{17,1},{2,18},{18,2},{3,19},{19,3},{4,20},{20... | collective-permute-start | bytes 3145736 | tf_op jit(solution)/shard_map/ppermute | solution.py:346
  272.1 5.9 %collective-permute-start.10 = (bf16[16,256,256]{2,1,0:T(8,128)(2,1)}, bf16[16,256,256]{2,1,0:T(8,128)(2,1)}, u32[]{:S(2)}, u32[]{:S(2)}) collective-permute-start(bf16[16,256,256]{2,1,0:T(8,128)(2,1)} %all-to-all-done.1.refs_2_), channel_id=1, source_target_pairs={{0,1},{1,0},{2,3},{3,2},{4,5},{5,4},{6,7},{7,6},{8,9},{9,8},{10,11... | collective-permute-start | bytes 6291464 | tf_op jit(solution)/shard_map/ppermute | solution.py:343
  272.3 51.1 %all-to-all-start.2 = ((s16[8,512,256]{2,1,0:T(8,128)(2,1)}), s16[8,512,256]{2,1,0:T(8,128)(2,1)S(1)}, u32[]{:S(2)}, u32[]{:S(2)}) async-start(s16[8,512,256]{2,1,0:T(8,128)(2,1)} %beta_term.2), calls=%async_computation.2 | async-start | bytes 4194304 | tf_op jit(solution)/shard_map/all_to_all | solution.py:394
  276.8 46.6 %collective-permute-start.5 = (bf16[2,2048,256]{2,1,0:T(8,128)(2,1)}, bf16[2,2048,256]{2,1,0:T(8,128)(2,1)}, u32[]{:S(2)}, u32[]{:S(2)}) collective-permute-start(bf16[2,2048,256]{2,1,0:T(8,128)(2,1)} %get-tuple-element.20), channel_id=1, source_target_pairs={{16,0},{0,16},{17,1},{1,17},{18,2},{2,18},{19,3},{3,19},{20,4},{4,... | collective-permute-start | bytes 6291464 | tf_op jit(solution)/shard_map/ppermute | solution.py:350
  316.7 13.7 %copy-start.3 = (s32[16,16]{1,0:T(8,128)S(1)}, s32[16,16]{1,0:T(8,128)}, u32[]{:S(2)}) copy-start(s32[16,16]{1,0:T(8,128)} %param.8) | copy-start | bytes 3076
  323.4 141.4 %all-to-all-start.3 = ((s16[8,1536,256]{2,1,0:T(8,128)(2,1)}), s16[8,1536,256]{2,1,0:T(8,128)(2,1)}, u32[]{:S(2)}, u32[]{:S(2)}) async-start(s16[8,1536,256]{2,1,0:T(8,128)(2,1)} %beta_term.3), calls=%async_computation.3 | async-start | bytes 12582912 | tf_op jit(solution)/shard_map/all_to_all | solution.py:394
  329.2 90.4 %collective-permute-start.4 = (bf16[4,2048,256]{2,1,0:T(8,128)(2,1)}, bf16[4,2048,256]{2,1,0:T(8,128)(2,1)}, u32[]{:S(2)}, u32[]{:S(2)}) collective-permute-start(bf16[4,2048,256]{2,1,0:T(8,128)(2,1)} %slice.12), channel_id=1, source_target_pairs={{16,0},{0,16},{17,1},{1,17},{18,2},{2,18},{19,3},{3,19},{20,4},{4,... | collective-permute-start | bytes 12582920 | tf_op jit(solution)/shard_map/ppermute | solution.py:350
  447.0 2.2 copy-start.1
  464.8 4.6 copy-start
Sparse Core Ops, SparseCore 0:
  38.2 67.3 all-gather.6
  107.1 56.5 all-gather.4

commit v8 on v7

--- a/solution.py
+++ b/solution.py
@@ -119,7 +119,7 @@
     per_strip = x_refs[0].shape[2] // block
     tiles, _, size, _ = picked_ref.shape
     rows = size * tiles // CORES
-    quarter = blocks_ref.shape[1] // (2 * pieces)
+    half = blocks_ref.shape[1] // 2
     outer = message_refs[0].shape[0]
     tile, dest = pl.program_id(0), pl.program_id(1)
     core, x_here, parity = place_ref[0], place_ref[1], place_ref[2]
@@ -141,15 +141,15 @@
     @pl.when((tile == 0) & (dest == 0))
     def _():
         fetch_rows(0)
-        for z in range(outer):
-            for q in range(xs):
-                for p in range(pieces):
+        for p in range(pieces):
+            for z in range(outer):
+                for q in range(xs):
                     for r in range(2):
-                        d = z * xs + (x_here ^ q)
-                        at = pl.multiple_of(((parity ^ r) * pieces + p) * quarter, quarter)
+                        d = (p * outer + z) * xs + (x_here ^ q)
+                        at = pl.multiple_of((parity ^ r) * half, half)
                         pltpu.make_async_copy(
                             message_refs[(p * xs + q) * 2 + r].at[z],
-                            blocks_ref.at[d, pl.ds(at, quarter)],
+                            blocks_ref.at[d, pl.ds(at, half)],
                             blocks_sem.at[d],
                         ).start()
         for t in range(1, tiles):
@@ -177,14 +177,14 @@
 
 def beta_term(slots, xs, columns, place, parts, messages, pieces, hint):
     sources, _, strip = parts[0][0].shape
-    outer, quarter, block = messages[0].shape
-    dests = outer * xs
+    outer, half, block = messages[0].shape
+    dests = pieces * outer * xs
     segments = [(start, count) for _, _, start, count in parts]
     rows = sum(count for _, count in segments)
     tiles = CORES if rows >= 512 else 1
     size = rows * CORES // tiles
     count = sources * strip // block
-    depth = 2 * pieces * quarter
+    depth = 2 * half
     arrays = [a for own, twin, _, _ in parts for a in (own, twin)] + list(messages)
 
     def out_at(t, d, cols_ref, place_ref):
@@ -310,7 +310,7 @@
         out_specs=pl.BlockSpec((1, rows, strip), lambda v: (first + v, 0, 0)),
         out_shape=jax.ShapeDtypeStruct((vectors, rows, strip), jnp.bfloat16),
         input_output_aliases=aliases,
-        compiler_params=pltpu.CompilerParams(vmem_limit_bytes=24 * MIB),
+        compiler_params=pltpu.CompilerParams(vmem_limit_bytes=VMEM),
         cost_estimate=pl.CostEstimate(
             flops=8 * count * rows * strip, bytes_accessed=8 * count * rows * strip, transcendentals=0
         ),
@@ -352,9 +352,7 @@
 
     mine = turn_half(place, beta_blocks.reshape(2, owned * slots // 2, block, block))
     far = [[o * inner + i for o in range(outer)] for i in range(inner)]
-    gathered = [
-        lax.all_gather(m, "beta", axis=0, tiled=False, axis_index_groups=far) for m in jnp.split(mine, pieces)
-    ]
+    gathered = lax.all_gather(mine, "beta", axis=0, tiled=False, axis_index_groups=far)
 
     heads = jnp.pad(beta_cols.reshape(1, -1).astype(jnp.bfloat16), ((0, TILE - 1), (0, strip - owned * slots)))
     packed = [pack(ci_vectors, heads if i == 0 else None, *cut, ring) for i, cut in enumerate(cuts)]
@@ -363,14 +361,14 @@
     others = [exchange(after(sent[0], (packed[1], *sent[1:])))]
 
     messages = []
-    for g in gathered:
-        carried = [after(g, messages[-2] if messages else others[0][-1])]
+    for g in jnp.split(gathered, pieces):
+        carried = [after(g, messages[-2]) if messages else g]
         bit = CORES
         while bit < inner:
             carried = carried + [swap(m, bit) for m in carried]
             bit *= 2
         for m in carried:
-            messages += [m, across(m)]
+            messages += [m, across(m if messages else after(m, others[0][-1]))]
 
     turned = [lax.all_to_all(packed[0], "beta", split_axis=0, concat_axis=0, tiled=True)]
     ahead = tuple(messages[1:-1])

time: 490 us -> 487 us (level)
  starting transfers between devices: 45.2 us -> 37.6 us
  Pallas kernels: 140 us -> 145 us
    all_gather x2 -> x1, waiting for transfers between devices: 124 us -> 80.1 us  [shards(): lax.all_gather(mine, 'beta', axis=0, tiled=False, axis_index_groups=far)]
    ppermute x4, waiting for transfers between devices: 15.1 us -> 54 us  [swap(): return lax.ppermute(value, 'beta', [(i, i ^ bit) for i in range(ring)])]
    ppermute x4, waiting for transfers between devices: 45.8 us -> 53.6 us  [across(): return lax.ppermute(value, 'alpha', [(i, i ^ 1) for i in range(ring_a)])]
    all_to_all x1, starting transfers between devices: 12.5 us -> 4.99 us  [shards(): lax.all_to_all(second, 'beta', split_axis=0, concat_axis=0, tiled=True)]
  transfers between devices with their start and end apart: 17 -> 16, of which waited for: 10 -> 10; matrix products, arithmetic and copies ran while one was open for 2% -> 3% of each run, Pallas kernels for 26% -> 26%
where the time goes in v8:
time: 487 us; the launch traced here: 482 us
  waiting for transfers between devices  268 us (55%)
  Pallas kernels  145 us (30%)
  starting transfers between devices  37.6 us (8%)
  local copies, waits for them, and re-layouts  14.6 us (3%)
  between operations  13.5 us (3%)
    all_gather x1, waiting for transfers between devices, shards(): lax.all_gather(mine, 'beta', axis=0, tiled=False, axis_index_groups=far)  80.1 us
    ppermute x3, waiting for transfers between devices, exchange(): lax.ppermute(value, 'alpha', [((i + s) % ring_a, i) for i in range(ring_a)])  61.4 us
    pallas_call x3, Pallas kernels, alpha_term(): pl.pallas_call(functools.partial(alpha_kernel, pieces), grid_spec=pltpu.P...  61.2 us
    pallas_call x2, Pallas kernels, beta_term(): pl.pallas_call(functools.partial(beta_kernel, slots, xs, segments, pieces...  56.4 us
    ppermute x4, waiting for transfers between devices, swap(): return lax.ppermute(value, 'beta', [(i, i ^ bit) for i in range(ring)])  54 us
    ppermute x4, waiting for transfers between devices, across(): return lax.ppermute(value, 'alpha', [(i, i ^ 1) for i in range(ring_a)])  53.6 us
    pallas_call x2, Pallas kernels, join(): pl.pallas_call(functools.partial(join_kernel, few_rows), grid=(count,), i...  15.3 us
    all_to_all x2, waiting for transfers between devices, send_back(): lax.all_to_all(term, 'beta', split_axis=0, concat_axis=0, tiled=True, axi...  13.4 us
  transfers between devices with their start and end apart: 16, of which 10 were waited for; matrix products, arithmetic and copies ran while one was open for 3% of the time, Pallas kernels for 26%

profile of v8, /device:TPU:11, one launch (start us, length us, event | category | flops | bytes accessed | tf_op | source)
XLA Modules:
  0.0 481.7 jit_solution(17983130497411412409)
XLA Ops:
  11.2 6.0 %pack_pieces.2 = bf16[16,784,256]{2,1,0:T(8,128)(2,1)} custom-call(bf16[8,2048,256]{2,1,0:T(8,128)(2,1)} %refs_0_.5, bf16[16,256]{1,0:T(8,128)(2,1)} %pad.4.refs_0_), custom_call_target="tpu_custom_call" | custom-call | bytes 12845056 | tf_op jit(solution)/shard_map/pack_pieces/pallas_call | solution.py:78
  17.2 6.6 %all-to-all-start = ((bf16[16,784,256]{2,1,0:T(8,128)(2,1)}), bf16[16,784,256]{2,1,0:T(8,128)(2,1)}, u32[]{:S(2)}, u32[]{:S(2)}) async-start(bf16[16,784,256]{2,1,0:T(8,128)(2,1)} %pack_pieces.2), calls=%async_computation | async-start | bytes 12845056 | tf_op jit(solution)/shard_map/all_to_all | solution.py:373
  28.4 4.4 slice.12
  32.8 4.1 fusion.1
  38.2 80.1 %all-gather.3.cloned.1.call-done = bf16[8192,128]{1,0:T(8,128)(2,1)} async-done(((bf16[2048,128]{1,0:T(8,128)(2,1)}), bf16[8192,128]{1,0:T(8,128)(2,1)}) %all-gather.3.cloned.1.call-update) | async-done | bytes 2097168 | tf_op jit(solution)/shard_map/all_gather | solution.py:355
  124.2 43.4 %collective-permute-done.refs_4_.refs_6_ = bf16[2,2048,128]{2,1,0:T(8,128)(2,1)S(1)} collective-permute-done((bf16[2,2048,128]{2,1,0:T(8,128)(2,1)S(1)}, bf16[2,2048,128]{2,1,0:T(8,128)(2,1)S(1)}, u32[]{:S(2)}, u32[]{:S(2)}) %collective-permute-start) | collective-permute-done | bytes 1048608 | tf_op jit(solution)/shard_map/ppermute | solution.py:343
  171.3 20.7 %collective-permute-done.8.refs_7_.refs_9_ = bf16[2,2048,128]{2,1,0:T(8,128)(2,1)S(1)} collective-permute-done((bf16[2,2048,128]{2,1,0:T(8,128)(2,1)S(1)}, bf16[2,2048,128]{2,1,0:T(8,128)(2,1)S(1)}, u32[]{:S(2)}, u32[]{:S(2)}) %collective-permute-start.8) | collective-permute-done | bytes 1048608 | tf_op jit(solution)/shard_map/ppermute | solution.py:346
  191.9 10.6 %collective-permute-done.1.refs_8_.refs_10_ = bf16[2,2048,128]{2,1,0:T(8,128)(2,1)S(1)} collective-permute-done((bf16[2,2048,128]{2,1,0:T(8,128)(2,1)S(1)}, bf16[2,2048,128]{2,1,0:T(8,128)(2,1)S(1)}, u32[]{:S(2)}, u32[]{:S(2)}) %collective-permute-start.1) | collective-permute-done | bytes 1048608 | tf_op jit(solution)/shard_map/ppermute | solution.py:343
  203.5 10.9 %collective-permute-done.7.refs_5_.refs_7_ = bf16[2,2048,128]{2,1,0:T(8,128)(2,1)} collective-permute-done((bf16[2,2048,128]{2,1,0:T(8,128)(2,1)S(1)}, bf16[2,2048,128]{2,1,0:T(8,128)(2,1)}, u32[]{:S(2)}, u32[]{:S(2)}) %collective-permute-start.7) | collective-permute-done | bytes 1048608 | tf_op jit(solution)/shard_map/ppermute | solution.py:346
  215.7 5.0 %all-to-all-start.1 = ((bf16[16,256,256]{2,1,0:T(8,128)(2,1)}), bf16[16,256,256]{2,1,0:T(8,128)(2,1)}, u32[]{:S(2)}, u32[]{:S(2)}) async-start(bf16[16,256,256]{2,1,0:T(8,128)(2,1)} %pack_pieces.3), calls=%async_computation.1 | async-start | bytes 4194304 | tf_op jit(solution)/shard_map/all_to_all | solution.py:376
  223.4 22.0 %collective-permute-done.2.refs_9_.refs_11_ = bf16[2,2048,128]{2,1,0:T(8,128)(2,1)} collective-permute-done((bf16[2,2048,128]{2,1,0:T(8,128)(2,1)}, bf16[2,2048,128]{2,1,0:T(8,128)(2,1)}, u32[]{:S(2)}, u32[]{:S(2)}) %collective-permute-start.2) | collective-permute-done | bytes 1048608 | tf_op jit(solution)/shard_map/ppermute | solution.py:346
  245.4 17.5 %beta_term.2 = s16[8,512,256]{2,1,0:T(8,128)(2,1)} custom-call(s32[512]{0:T(512)} %reshape.30.cols_ref, s32[4]{0:T(128)} %pad_add_fusion.place_ref, bf16[16,784,256]{2,1,0:T(8,128)(2,1)} %all-to-all-done.refs_0_, bf16[16,784,256]{2,1,0:T(8,128)(2,1)} %collective-permute-done.9.refs_1_, bf16[2,2048,128]{2,1,0:T(8,128)(2,1)} %bitcast.11, ...), custom_call_target="tpu_custom_call" | custom-call | flops 8589934592 | bytes 16777216 | tf_op jit(solution)/shard_map/beta_term/pallas_call | solution.py:193
  262.9 5.4 %all-to-all-done.1.refs_2_ = bf16[16,256,256]{2,1,0:T(8,128)(2,1)} async-done(((bf16[16,256,256]{2,1,0:T(8,128)(2,1)}), bf16[16,256,256]{2,1,0:T(8,128)(2,1)}, u32[]{:S(2)}, u32[]{:S(2)}) %all-to-all-start.1) | async-done | bytes 2097184 | tf_op jit(solution)/shard_map/all_to_all | solution.py:376
  268.6 5.7 %all-to-all-start.2 = ((s16[8,512,256]{2,1,0:T(8,128)(2,1)}), s16[8,512,256]{2,1,0:T(8,128)(2,1)S(1)}, u32[]{:S(2)}, u32[]{:S(2)}) async-start(s16[8,512,256]{2,1,0:T(8,128)(2,1)} %beta_term.2), calls=%async_computation.2 | async-start | bytes 4194304 | tf_op jit(solution)/shard_map/all_to_all | solution.py:392
  275.6 38.9 %beta_term.3 = s16[8,1536,256]{2,1,0:T(8,128)(2,1)} custom-call(s32[512]{0:T(512)} %reshape.30.cols_ref, s32[4]{0:T(128)} %pad_add_fusion.place_ref, bf16[16,784,256]{2,1,0:T(8,128)(2,1)} %all-to-all-done.refs_0_, bf16[16,784,256]{2,1,0:T(8,128)(2,1)} %collective-permute-done.9.refs_1_, bf16[16,256,256]{2,1,0:T(8,128)(2,1)} %all-to-all-done.1.refs_2_, ...), custom_call_target="tpu_custom_call" | custom-call | flops 25769803776 | bytes 33554432 | tf_op jit(solution)/shard_map/beta_term/pallas_call | solution.py:193
  314.5 6.6 %collective-permute-done.4.refs_1_ = bf16[2,2048,256]{2,1,0:T(8,128)(2,1)} collective-permute-done((bf16[2,2048,256]{2,1,0:T(8,128)(2,1)}, bf16[2,2048,256]{2,1,0:T(8,128)(2,1)}, u32[]{:S(2)}, u32[]{:S(2)}) %collective-permute-start.4) | collective-permute-done | bytes 2097184 | tf_op jit(solution)/shard_map/ppermute | solution.py:350
  322.5 5.8 %all-to-all-start.3 = ((s16[8,1536,256]{2,1,0:T(8,128)(2,1)}), s16[8,1536,256]{2,1,0:T(8,128)(2,1)}, u32[]{:S(2)}, u32[]{:S(2)}) async-start(s16[8,1536,256]{2,1,0:T(8,128)(2,1)} %beta_term.3), calls=%async_computation.3 | async-start | bytes 12582912 | tf_op jit(solution)/shard_map/all_to_all | solution.py:392
  330.2 16.9 %alpha_term.5.acc_ref = f32[2,2048,256]{2,1,0:T(8,128)} custom-call(s32[256]{0:T(256)} %reshape.27.cols_ref, s32[4]{0:T(128)} %pad_add_fusion.place_ref, bf16[8,2048,256]{2,1,0:T(8,128)(2,1)} %refs_0_.5, bf16[2,2048,256]{2,1,0:T(8,128)(2,1)} %collective-permute-done.5.refs_1_, bf16[16,16,128,128]{3,2,1,0:T(8,128)(2,1)} %refs_2_.5, f32[2048,256]{1,0:T(8,128)} %refs_3_.5), custom_call_target="tpu_custom_call" | custom-call | flops 12884901888 | bytes 18874368 | tf_op jit(solution)/shard_map/alpha_term/pallas_call | solution.py:261
  347.1 17.0 %alpha_term.3.refs_4_ = f32[6,2048,256]{2,1,0:T(8,128)} custom-call(s32[256]{0:T(256)} %reshape.27.cols_ref, s32[4]{0:T(128)} %pad_add_fusion.place_ref, bf16[8,2048,256]{2,1,0:T(8,128)(2,1)} %refs_0_.5, bf16[2,2048,256]{2,1,0:T(8,128)(2,1)} %collective-permute-done.4.refs_1_, bf16[16,16,128,128]{3,2,1,0:T(8,128)(2,1)} %refs_2_.5, f32[2048,256]{1,0:T(8,128)} %refs_3_.5), custom_call_target="tpu_custom_call" | custom-call | flops 12884901888 | bytes 18874368 | tf_op jit(solution)/shard_map/alpha_term/pallas_call | solution.py:261
  364.1 54.8 %collective-permute-done.3.refs_1_ = bf16[4,2048,256]{2,1,0:T(8,128)(2,1)} collective-permute-done((bf16[4,2048,256]{2,1,0:T(8,128)(2,1)}, bf16[4,2048,256]{2,1,0:T(8,128)(2,1)}, u32[]{:S(2)}, u32[]{:S(2)}) %collective-permute-start.3) | collective-permute-done | bytes 4194336 | tf_op jit(solution)/shard_map/ppermute | solution.py:350
  418.9 27.3 %alpha_term.4.acc_ref = f32[6,2048,256]{2,1,0:T(8,128)} custom-call(s32[256]{0:T(256)} %reshape.27.cols_ref, s32[4]{0:T(128)} %pad_add_fusion.place_ref, bf16[8,2048,256]{2,1,0:T(8,128)(2,1)} %refs_0_.5, bf16[4,2048,256]{2,1,0:T(8,128)(2,1)} %collective-permute-done.3.refs_1_, bf16[16,16,128,128]{3,2,1,0:T(8,128)(2,1)} %refs_2_.5, ...), custom_call_target="tpu_custom_call", output_to_operand_aliasing={{}: (6, {})} | custom-call | flops 25769803776 | bytes 27262976 | tf_op jit(solution)/shard_map/alpha_term/pallas_call | solution.py:261
  446.1 4.4 join_terms.2.rest_0_
  450.5 13.4 %all-to-all-done.3 = s16[8,1536,256]{2,1,0:T(8,128)(2,1)} async-done(((s16[8,1536,256]{2,1,0:T(8,128)(2,1)}), s16[8,1536,256]{2,1,0:T(8,128)(2,1)}, u32[]{:S(2)}, u32[]{:S(2)}) %all-to-all-start.3) | async-done | bytes 6291488 | tf_op jit(solution)/shard_map/all_to_all | solution.py:392
  463.9 10.9 %join_terms.3 = bf16[8,2048,256]{2,1,0:T(8,128)(2,1)} custom-call(f32[6,2048,256]{2,1,0:T(8,128)} %alpha_term.4.acc_ref, s16[8,2,6,128,256]{4,3,2,1,0:T(8,128)(2,1)} %bitcast.6.words_ref, bf16[8,2048,256]{2,1,0:T(8,128)(2,1)} %join_terms.2.rest_0_), custom_call_target="tpu_custom_call", output_to_operand_aliasing={{}: (2, {})} | custom-call | flops 25165824 | bytes 25165824 | tf_op jit(solution)/shard_map/join_terms/pallas_call | solution.py:306
  (45 shorter events, 30.0 us)
Async XLA Ops:
  17.2 197.2 %all-to-all-start = ((bf16[16,784,256]{2,1,0:T(8,128)(2,1)}), bf16[16,784,256]{2,1,0:T(8,128)(2,1)}, u32[]{:S(2)}, u32[]{:S(2)}) async-start(bf16[16,784,256]{2,1,0:T(8,128)(2,1)} %pack_pieces.2), calls=%async_computation | async-start | bytes 12845056 | tf_op jit(solution)/shard_map/all_to_all | solution.py:373
  23.8 94.5 %all-gather.3.cloned.1.call-start = ((), (), s32[]{:S(2)}) async-start(), calls=%async_computation.4 | async-start | bytes 2621440 | tf_op jit(solution)/shard_map/all_gather | solution.py:355
  36.9 85.9 %collective-permute-start.5 = (bf16[2,2048,256]{2,1,0:T(8,128)(2,1)S(1)}, bf16[2,2048,256]{2,1,0:T(8,128)(2,1)}, u32[]{:S(2)}, u32[]{:S(2)}) collective-permute-start(bf16[2,2048,256]{2,1,0:T(8,128)(2,1)S(1)} %get-tuple-element.20), channel_id=1, source_target_pairs={{16,0},{0,16},{17,1},{1,17},{18,2},{2,18},{19,3},{3,19},{20,4},{4,... | collective-permute-start | bytes 6291464 | tf_op jit(solution)/shard_map/ppermute | solution.py:350
  120.0 51.3 %copy-start.2 = (bf16[4096,128]{1,0:T(8,128)(2,1)}, bf16[4096,128]{1,0:T(8,128)(2,1)S(1)}, u32[]{:S(2)}) copy-start(bf16[4096,128]{1,0:T(8,128)(2,1)S(1)} %get-tuple-element.30) | copy-start | bytes 3145732
  120.0 125.5 %copy-start.1 = (bf16[4096,128]{1,0:T(8,128)(2,1)}, bf16[4096,128]{1,0:T(8,128)(2,1)S(1)}, u32[]{:S(2)}) copy-start(bf16[4096,128]{1,0:T(8,128)(2,1)S(1)} %get-tuple-element.29) | copy-start | bytes 3145732
  120.0 47.6 %collective-permute-start = (bf16[2,2048,128]{2,1,0:T(8,128)(2,1)S(1)}, bf16[2,2048,128]{2,1,0:T(8,128)(2,1)S(1)}, u32[]{:S(2)}, u32[]{:S(2)}) collective-permute-start(bf16[2,2048,128]{2,1,0:T(8,128)(2,1)S(1)} %bitcast.9), channel_id=1, source_target_pairs={{0,2},{1,3},{2,0},{3,1},{4,6},{5,7},{6,4},{7,5},{8,10},{9,11},{10,... | collective-permute-start | bytes 3145736 | tf_op jit(solution)/shard_map/ppermute | solution.py:343
  122.8 48.4 %collective-permute-start.6 = (bf16[2,2048,128]{2,1,0:T(8,128)(2,1)S(1)}, bf16[2,2048,128]{2,1,0:T(8,128)(2,1)S(1)}, u32[]{:S(2)}, u32[]{:S(2)}) collective-permute-start(bf16[2,2048,128]{2,1,0:T(8,128)(2,1)S(1)} %bitcast.10), channel_id=1, source_target_pairs={{0,16},{16,0},{1,17},{17,1},{2,18},{18,2},{3,19},{19,3},{4,20},{20... | collective-permute-start | bytes 3145736 | tf_op jit(solution)/shard_map/ppermute | solution.py:346
  167.6 34.9 %copy-start.4 = (bf16[2,2048,128]{2,1,0:T(8,128)(2,1)}, bf16[2,2048,128]{2,1,0:T(8,128)(2,1)S(1)}, u32[]{:S(2)}) copy-start(bf16[2,2048,128]{2,1,0:T(8,128)(2,1)S(1)} %collective-permute-done.refs_4_.refs_6_) | copy-start | bytes 3145732
  167.6 24.4 %collective-permute-start.8 = (bf16[2,2048,128]{2,1,0:T(8,128)(2,1)S(1)}, bf16[2,2048,128]{2,1,0:T(8,128)(2,1)S(1)}, u32[]{:S(2)}, u32[]{:S(2)}) collective-permute-start(bf16[2,2048,128]{2,1,0:T(8,128)(2,1)S(1)} %bitcast.13), channel_id=1, source_target_pairs={{0,16},{16,0},{1,17},{17,1},{2,18},{18,2},{3,19},{19,3},{4,20},{20... | collective-permute-start | bytes 3145736 | tf_op jit(solution)/shard_map/ppermute | solution.py:346
  168.8 33.7 %collective-permute-start.1 = (bf16[2,2048,128]{2,1,0:T(8,128)(2,1)S(1)}, bf16[2,2048,128]{2,1,0:T(8,128)(2,1)S(1)}, u32[]{:S(2)}, u32[]{:S(2)}) collective-permute-start(bf16[2,2048,128]{2,1,0:T(8,128)(2,1)S(1)} %bitcast.14), channel_id=1, source_target_pairs={{0,2},{1,3},{2,0},{3,1},{4,6},{5,7},{6,4},{7,5},{8,10},{9,11},{10,... | collective-permute-start | bytes 3145736 | tf_op jit(solution)/shard_map/ppermute | solution.py:343
  171.0 43.4 %collective-permute-start.7 = (bf16[2,2048,128]{2,1,0:T(8,128)(2,1)S(1)}, bf16[2,2048,128]{2,1,0:T(8,128)(2,1)}, u32[]{:S(2)}, u32[]{:S(2)}) collective-permute-start(bf16[2,2048,128]{2,1,0:T(8,128)(2,1)S(1)} %collective-permute-done.refs_4_.refs_6_), channel_id=1, source_target_pairs={{0,16},{16,0},{1,17},{17,1},{2,18},{18,2},{3,19},{19,3},{4,20},{20... | collective-permute-start | bytes 3145736 | tf_op jit(solution)/shard_map/ppermute | solution.py:346
  171.3 74.2 %copy-start.5 = (bf16[2,2048,128]{2,1,0:T(8,128)(2,1)}, bf16[2,2048,128]{2,1,0:T(8,128)(2,1)S(1)}, u32[]{:S(2)}) copy-start(bf16[2,2048,128]{2,1,0:T(8,128)(2,1)S(1)} %collective-permute-done.6.refs_3_.refs_5_) | copy-start | bytes 3145732
  191.9 10.6 %copy-start.6 = (bf16[2,2048,128]{2,1,0:T(8,128)(2,1)}, bf16[2,2048,128]{2,1,0:T(8,128)(2,1)S(1)}, u32[]{:S(2)}) copy-start(bf16[2,2048,128]{2,1,0:T(8,128)(2,1)S(1)} %collective-permute-done.8.refs_7_.refs_9_) | copy-start | bytes 3145732
  202.5 1.0 copy-start.7
  214.4 31.0 %collective-permute-start.9 = (bf16[16,784,256]{2,1,0:T(8,128)(2,1)}, bf16[16,784,256]{2,1,0:T(8,128)(2,1)}, u32[]{:S(2)}, u32[]{:S(2)}) collective-permute-start(bf16[16,784,256]{2,1,0:T(8,128)(2,1)} %all-to-all-done.refs_0_), channel_id=1, source_target_pairs={{0,1},{1,0},{2,3},{3,2},{4,5},{5,4},{6,7},{7,6},{8,9},{9,8},{10,11... | collective-permute-start | bytes 19267592 | tf_op jit(solution)/shard_map/ppermute | solution.py:343
  215.7 52.5 %all-to-all-start.1 = ((bf16[16,256,256]{2,1,0:T(8,128)(2,1)}), bf16[16,256,256]{2,1,0:T(8,128)(2,1)}, u32[]{:S(2)}, u32[]{:S(2)}) async-start(bf16[16,256,256]{2,1,0:T(8,128)(2,1)} %pack_pieces.3), calls=%async_computation.1 | async-start | bytes 4194304 | tf_op jit(solution)/shard_map/all_to_all | solution.py:376
  220.7 24.7 %collective-permute-start.2 = (bf16[2,2048,128]{2,1,0:T(8,128)(2,1)}, bf16[2,2048,128]{2,1,0:T(8,128)(2,1)}, u32[]{:S(2)}, u32[]{:S(2)}) collective-permute-start(bf16[2,2048,128]{2,1,0:T(8,128)(2,1)} %copy-done.7), channel_id=1, source_target_pairs={{0,16},{16,0},{1,17},{17,1},{2,18},{18,2},{3,19},{19,3},{4,20},{20... | collective-permute-start | bytes 3145736 | tf_op jit(solution)/shard_map/ppermute | solution.py:346
  268.3 7.3 %collective-permute-start.10 = (bf16[16,256,256]{2,1,0:T(8,128)(2,1)}, bf16[16,256,256]{2,1,0:T(8,128)(2,1)}, u32[]{:S(2)}, u32[]{:S(2)}) collective-permute-start(bf16[16,256,256]{2,1,0:T(8,128)(2,1)} %all-to-all-done.1.refs_2_), channel_id=1, source_target_pairs={{0,1},{1,0},{2,3},{3,2},{4,5},{5,4},{6,7},{7,6},{8,9},{9,8},{10,11... | collective-permute-start | bytes 6291464 | tf_op jit(solution)/shard_map/ppermute | solution.py:343
  268.6 52.5 %all-to-all-start.2 = ((s16[8,512,256]{2,1,0:T(8,128)(2,1)}), s16[8,512,256]{2,1,0:T(8,128)(2,1)S(1)}, u32[]{:S(2)}, u32[]{:S(2)}) async-start(s16[8,512,256]{2,1,0:T(8,128)(2,1)} %beta_term.2), calls=%async_computation.2 | async-start | bytes 4194304 | tf_op jit(solution)/shard_map/all_to_all | solution.py:392
  274.3 46.8 %collective-permute-start.4 = (bf16[2,2048,256]{2,1,0:T(8,128)(2,1)}, bf16[2,2048,256]{2,1,0:T(8,128)(2,1)}, u32[]{:S(2)}, u32[]{:S(2)}) collective-permute-start(bf16[2,2048,256]{2,1,0:T(8,128)(2,1)} %get-tuple-element.18), channel_id=1, source_target_pairs={{16,0},{0,16},{17,1},{1,17},{18,2},{2,18},{19,3},{3,19},{20,4},{4,... | collective-permute-start | bytes 6291464 | tf_op jit(solution)/shard_map/ppermute | solution.py:350
  314.5 15.0 %copy-start.3 = (s32[16,16]{1,0:T(8,128)S(1)}, s32[16,16]{1,0:T(8,128)}, u32[]{:S(2)}) copy-start(s32[16,16]{1,0:T(8,128)} %param.8) | copy-start | bytes 3076
  321.1 1.4 copy-start
  322.5 141.4 %all-to-all-start.3 = ((s16[8,1536,256]{2,1,0:T(8,128)(2,1)}), s16[8,1536,256]{2,1,0:T(8,128)(2,1)}, u32[]{:S(2)}, u32[]{:S(2)}) async-start(s16[8,1536,256]{2,1,0:T(8,128)(2,1)} %beta_term.3), calls=%async_computation.3 | async-start | bytes 12582912 | tf_op jit(solution)/shard_map/all_to_all | solution.py:392
  328.3 90.6 %collective-permute-start.3 = (bf16[4,2048,256]{2,1,0:T(8,128)(2,1)}, bf16[4,2048,256]{2,1,0:T(8,128)(2,1)}, u32[]{:S(2)}, u32[]{:S(2)}) collective-permute-start(bf16[4,2048,256]{2,1,0:T(8,128)(2,1)} %slice.12), channel_id=1, source_target_pairs={{16,0},{0,16},{17,1},{1,17},{18,2},{2,18},{19,3},{3,19},{20,4},{4,... | collective-permute-start | bytes 12582920 | tf_op jit(solution)/shard_map/ppermute | solution.py:350
Sparse Core Ops, SparseCore 0:
  26.2 92.0 all-gather.2

commit v9 on v8

--- a/solution.py
+++ b/solution.py
@@ -14,7 +14,7 @@
 CODE_BITS = 11
 LARGEST = 32767.0
 TILE = 16
-HINTS = (4, 4)
+HINTS = (26, 4)
 VMEM = 60 * MIB
 CORES = 2
 ANYWHERE = pl.BlockSpec(memory_space=pl.ANY)
@@ -53,30 +53,31 @@
     return words.astype(jnp.float32) * scale
 
 
-def pack_kernel(source_ref, *refs):
+def pack_kernel(skip, count, source_ref, *refs):
     out_ref = refs[-1]
-    count, wide, _ = source_ref.shape
     dests = out_ref.shape[0]
-    few_rows = wide // dests
+    few_rows = source_ref.shape[1] // dests
     for d in range(dests):
+        rows = slice(d * few_rows, (d + 1) * few_rows)
         for v in range(count):
-            out_ref[d, v * few_rows : (v + 1) * few_rows, :] = source_ref[v, d * few_rows : (d + 1) * few_rows, :]
+            out_ref[d, v * few_rows : (v + 1) * few_rows, :] = source_ref[skip + v, rows, :]
         if len(refs) == 2:
             out_ref[d, count * few_rows :, :] = refs[0][...]
 
 
 def pack(ci_vectors, heads, first, count, ring):
-    _, rows, strip = ci_vectors.shape
+    vectors, rows, strip = ci_vectors.shape
     few_rows = rows // ring
+    taken, at = (count, first // count) if first % count == 0 else (vectors, 0)
     depth = count * few_rows + (0 if heads is None else TILE)
     each = 4
-    in_specs = [pl.BlockSpec((count, each * few_rows, strip), lambda d: (first // count, d, 0))]
+    in_specs = [pl.BlockSpec((taken, each * few_rows, strip), lambda d: (at, d, 0))]
     args = [ci_vectors]
     if heads is not None:
         in_specs.append(pl.BlockSpec((TILE, strip), lambda d: (0, 0)))
         args.append(heads)
     return pl.pallas_call(
-        pack_kernel,
+        functools.partial(pack_kernel, first - at * taken, count),
         grid=(ring // each,),
         in_specs=in_specs,
         out_specs=pl.BlockSpec((each, depth, strip), lambda d: (d, 0, 0)),
@@ -333,7 +334,8 @@
     parity = lax.rem(at_a, 2)
     place = jnp.stack([lax.rem(at_b, CORES), lax.rem(lax.div(at_b, CORES), xs), parity, at_a]).astype(jnp.int32)
     few = vectors // 4
-    cuts = [(0, vectors - few), (vectors - few, few)]
+    lead = 3 * vectors // 8
+    cuts = [(0, lead), (lead, vectors - lead)]
     back = [(0, few), (few, vectors - few)]
     shares = [(0, few), (few, few), (2 * few, vectors - 2 * few)]
     sent = [ci_vectors[first : first + count] for first, count in shares]
@@ -356,7 +358,6 @@
 
     heads = jnp.pad(beta_cols.reshape(1, -1).astype(jnp.bfloat16), ((0, TILE - 1), (0, strip - owned * slots)))
     packed = [pack(ci_vectors, heads if i == 0 else None, *cut, ring) for i, cut in enumerate(cuts)]
-    packed[0] = after(packed[0], mine)
 
     others = [exchange(after(sent[0], (packed[1], *sent[1:])))]
 
@@ -368,14 +369,13 @@
             carried = carried + [swap(m, bit) for m in carried]
             bit *= 2
         for m in carried:
-            messages += [m, across(m if messages else after(m, others[0][-1]))]
+            messages += [m, across(m)]
 
     turned = [lax.all_to_all(packed[0], "beta", split_axis=0, concat_axis=0, tiled=True)]
-    ahead = tuple(messages[1:-1])
-    second = after(packed[1], (turned[0], *ahead))
+    second = after(packed[1], (turned[0], messages[0], others[0][-1]))
     turned.append(lax.all_to_all(second, "beta", split_axis=0, concat_axis=0, tiled=True))
     columns = turned[0][:, cuts[0][1] * few_rows, : owned * slots].reshape(-1).astype(jnp.int32)
-    twins = [swap(after(turned[0], ahead), 1)]
+    twins = [swap(after(turned[0], tuple(messages[1:-1])), 1)]
     for value in sent[1:]:
         others.append(exchange(after(value, messages[-1])))
 
@@ -398,7 +398,7 @@
     words = [send_back(after(term, turned[1]))]
     parts = [
         (turned[0], twins[0], few * few_rows, rest * few_rows),
-        (turned[1], twins[1], 0, few * few_rows),
+        (turned[1], twins[1], 0, cuts[1][1] * few_rows),
     ]
     term = beta_term(slots, xs, columns, place, parts, messages, pieces, HINTS[1])
     words.append(send_back(after(term, (words[0], others[1][-1]))))

time: 487 us -> 480 us (0.986)
  waiting for transfers between devices: 268 us -> 254 us
  starting transfers between devices: 37.6 us -> 45.7 us
    all_gather x1, waiting for transfers between devices: 80.1 us -> 71.3 us  [shards(): lax.all_gather(mine, 'beta', axis=0, tiled=False, axis_index_groups=far)]
    ppermute x4, waiting for transfers between devices: 53.6 us -> 44.9 us  [across(): return lax.ppermute(value, 'alpha', [(i, i ^ 1) for i in range(ring_a)])]
    all_to_all x1, waiting for transfers between devices: 0.01 us -> 8.17 us  [shards(): lax.all_to_all(packed[0], 'beta', split_axis=0, concat_axis=0, tiled=True)]
    all_to_all x2, starting transfers between devices: 11.5 us -> 19 us  [send_back(): lax.all_to_all(term, 'beta', split_axis=0, concat_axis=0, tiled=True, axi...]
    all_to_all x1, waiting for transfers between devices: 5.39 us -> 0.01 us  [shards(): lax.all_to_all(second, 'beta', split_axis=0, concat_axis=0, tiled=True)]
  transfers between devices with their start and end apart: 16 -> 16, of which waited for: 10 -> 10; matrix products, arithmetic and copies ran while one was open for 3% -> 3% of each run, Pallas kernels for 26% -> 27%
where the time goes in v9:
time: 480 us; the launch traced here: 475 us
  waiting for transfers between devices  254 us (53%)
  Pallas kernels  146 us (30%)
  starting transfers between devices  45.7 us (10%)
  local copies, waits for them, and re-layouts  15.4 us (3%)
  between operations  13.5 us (3%)
    all_gather x1, waiting for transfers between devices, shards(): lax.all_gather(mine, 'beta', axis=0, tiled=False, axis_index_groups=far)  71.3 us
    ppermute x3, waiting for transfers between devices, exchange(): lax.ppermute(value, 'alpha', [((i + s) % ring_a, i) for i in range(ring_a)])  62 us
    pallas_call x3, Pallas kernels, alpha_term(): pl.pallas_call(functools.partial(alpha_kernel, pieces), grid_spec=pltpu.P...  61.2 us
    pallas_call x2, Pallas kernels, beta_term(): pl.pallas_call(functools.partial(beta_kernel, slots, xs, segments, pieces...  56 us
    ppermute x4, waiting for transfers between devices, swap(): return lax.ppermute(value, 'beta', [(i, i ^ bit) for i in range(ring)])  54.2 us
    ppermute x4, waiting for transfers between devices, across(): return lax.ppermute(value, 'alpha', [(i, i ^ 1) for i in range(ring_a)])  44.9 us
    all_to_all x2, starting transfers between devices, send_back(): lax.all_to_all(term, 'beta', split_axis=0, concat_axis=0, tiled=True, axi...  19 us
    pallas_call x2, Pallas kernels, join(): pl.pallas_call(functools.partial(join_kernel, few_rows), grid=(count,), i...  15.3 us
  transfers between devices with their start and end apart: 16, of which 10 were waited for; matrix products, arithmetic and copies ran while one was open for 3% of the time, Pallas kernels for 27%

profile of v9, /device:TPU:11, one launch (start us, length us, event | category | flops | bytes accessed | tf_op | source)
XLA Modules:
  0.0 475.4 jit_solution(1745922544697475839)
XLA Ops:
  12.2 6.6 %all-to-all-start = ((bf16[16,400,256]{2,1,0:T(8,128)(2,1)}), bf16[16,400,256]{2,1,0:T(8,128)(2,1)S(1)}, u32[]{:S(2)}, u32[]{:S(2)}) async-start(bf16[16,400,256]{2,1,0:T(8,128)(2,1)} %pack_pieces.2), calls=%async_computation | async-start | bytes 6553600 | tf_op jit(solution)/shard_map/all_to_all | solution.py:374
  22.2 4.4 slice.12
  26.6 6.2 %pack_pieces.3 = bf16[16,640,256]{2,1,0:T(8,128)(2,1)} custom-call(bf16[8,2048,256]{2,1,0:T(8,128)(2,1)} %refs_0_.5), custom_call_target="tpu_custom_call" | custom-call | bytes 10485760 | tf_op jit(solution)/shard_map/pack_pieces/pallas_call | solution.py:79
  32.8 4.5 fusion.1
  38.6 71.3 %all-gather.3.cloned.1.call-done = bf16[8192,128]{1,0:T(8,128)(2,1)} async-done(((bf16[2048,128]{1,0:T(8,128)(2,1)}), bf16[8192,128]{1,0:T(8,128)(2,1)}) %all-gather.3.cloned.1.call-update) | async-done | bytes 2097168 | tf_op jit(solution)/shard_map/all_gather | solution.py:357
  112.9 4.5 collective-permute-start
  117.4 8.2 %all-to-all-done.refs_0_ = bf16[16,400,256]{2,1,0:T(8,128)(2,1)S(1)} async-done(((bf16[16,400,256]{2,1,0:T(8,128)(2,1)}), bf16[16,400,256]{2,1,0:T(8,128)(2,1)S(1)}, u32[]{:S(2)}, u32[]{:S(2)}) %all-to-all-start) | async-done | bytes 3276832 | tf_op jit(solution)/shard_map/all_to_all | solution.py:374
  125.6 4.6 all-to-all-start.1
  131.4 20.8 %collective-permute-done.refs_4_.refs_6_ = bf16[2,2048,128]{2,1,0:T(8,128)(2,1)} collective-permute-done((bf16[2,2048,128]{2,1,0:T(8,128)(2,1)}, bf16[2,2048,128]{2,1,0:T(8,128)(2,1)}, u32[]{:S(2)}, u32[]{:S(2)}) %collective-permute-start) | collective-permute-done | bytes 1048608 | tf_op jit(solution)/shard_map/ppermute | solution.py:345
  154.9 21.6 %collective-permute-done.7.refs_7_.refs_9_ = bf16[2,2048,128]{2,1,0:T(8,128)(2,1)S(1)} collective-permute-done((bf16[2,2048,128]{2,1,0:T(8,128)(2,1)}, bf16[2,2048,128]{2,1,0:T(8,128)(2,1)S(1)}, u32[]{:S(2)}, u32[]{:S(2)}) %collective-permute-start.7) | collective-permute-done | bytes 1048608 | tf_op jit(solution)/shard_map/ppermute | solution.py:348
  176.5 33.3 %collective-permute-done.1.refs_8_.refs_10_ = bf16[2,2048,128]{2,1,0:T(8,128)(2,1)} collective-permute-done((bf16[2,2048,128]{2,1,0:T(8,128)(2,1)}, bf16[2,2048,128]{2,1,0:T(8,128)(2,1)}, u32[]{:S(2)}, u32[]{:S(2)}) %collective-permute-start.1) | collective-permute-done | bytes 1048608 | tf_op jit(solution)/shard_map/ppermute | solution.py:345
  213.3 22.1 %collective-permute-done.2.refs_9_.refs_11_ = bf16[2,2048,128]{2,1,0:T(8,128)(2,1)} collective-permute-done((bf16[2,2048,128]{2,1,0:T(8,128)(2,1)}, bf16[2,2048,128]{2,1,0:T(8,128)(2,1)}, u32[]{:S(2)}, u32[]{:S(2)}) %collective-permute-start.2) | collective-permute-done | bytes 1048608 | tf_op jit(solution)/shard_map/ppermute | solution.py:348
  235.4 17.4 %beta_term.2 = s16[8,512,256]{2,1,0:T(8,128)(2,1)} custom-call(s32[512]{0:T(512)} %reshape.30.cols_ref, s32[4]{0:T(128)} %pad_add_fusion.place_ref, bf16[16,400,256]{2,1,0:T(8,128)(2,1)} %copy-done.1, bf16[16,400,256]{2,1,0:T(8,128)(2,1)} %collective-permute-done.8.refs_1_, bf16[2,2048,128]{2,1,0:T(8,128)(2,1)} %bitcast.5.refs_2_.refs_4_, ...), custom_call_target="tpu_custom_call" | custom-call | flops 55834574848 | bytes 16777216 | tf_op jit(solution)/shard_map/beta_term/pallas_call | solution.py:194
  254.8 13.2 %all-to-all-start.2 = ((s16[8,512,256]{2,1,0:T(8,128)(2,1)}), s16[8,512,256]{2,1,0:T(8,128)(2,1)S(1)}, u32[]{:S(2)}, u32[]{:S(2)}) async-start(s16[8,512,256]{2,1,0:T(8,128)(2,1)} %beta_term.2), calls=%async_computation.2 | async-start | bytes 4194304 | tf_op jit(solution)/shard_map/all_to_all | solution.py:392
  269.2 38.6 %beta_term.3 = s16[8,1536,256]{2,1,0:T(8,128)(2,1)} custom-call(s32[512]{0:T(512)} %reshape.30.cols_ref, s32[4]{0:T(128)} %pad_add_fusion.place_ref, bf16[16,400,256]{2,1,0:T(8,128)(2,1)} %copy-done.1, bf16[16,400,256]{2,1,0:T(8,128)(2,1)} %collective-permute-done.8.refs_1_, bf16[16,640,256]{2,1,0:T(8,128)(2,1)} %all-to-all-done.1.refs_2_, ...), custom_call_target="tpu_custom_call" | custom-call | flops 25769803776 | bytes 33554432 | tf_op jit(solution)/shard_map/beta_term/pallas_call | solution.py:194
  307.8 7.1 %collective-permute-done.4.refs_1_ = bf16[2,2048,256]{2,1,0:T(8,128)(2,1)} collective-permute-done((bf16[2,2048,256]{2,1,0:T(8,128)(2,1)}, bf16[2,2048,256]{2,1,0:T(8,128)(2,1)}, u32[]{:S(2)}, u32[]{:S(2)}) %collective-permute-start.4) | collective-permute-done | bytes 2097184 | tf_op jit(solution)/shard_map/ppermute | solution.py:352
  316.3 5.8 %all-to-all-start.3 = ((s16[8,1536,256]{2,1,0:T(8,128)(2,1)}), s16[8,1536,256]{2,1,0:T(8,128)(2,1)}, u32[]{:S(2)}, u32[]{:S(2)}) async-start(s16[8,1536,256]{2,1,0:T(8,128)(2,1)} %beta_term.3), calls=%async_computation.3 | async-start | bytes 12582912 | tf_op jit(solution)/shard_map/all_to_all | solution.py:392
  324.0 16.9 %alpha_term.5.acc_ref = f32[2,2048,256]{2,1,0:T(8,128)} custom-call(s32[256]{0:T(256)} %reshape.27.cols_ref, s32[4]{0:T(128)} %pad_add_fusion.place_ref, bf16[8,2048,256]{2,1,0:T(8,128)(2,1)} %refs_0_.5, bf16[2,2048,256]{2,1,0:T(8,128)(2,1)} %collective-permute-done.9.refs_1_, bf16[16,16,128,128]{3,2,1,0:T(8,128)(2,1)} %refs_2_.5, f32[2048,256]{1,0:T(8,128)} %refs_3_.5), custom_call_target="tpu_custom_call" | custom-call | flops 12884901888 | bytes 18874368 | tf_op jit(solution)/shard_map/alpha_term/pallas_call | solution.py:262
  340.9 17.0 %alpha_term.3.refs_4_ = f32[6,2048,256]{2,1,0:T(8,128)} custom-call(s32[256]{0:T(256)} %reshape.27.cols_ref, s32[4]{0:T(128)} %pad_add_fusion.place_ref, bf16[8,2048,256]{2,1,0:T(8,128)(2,1)} %refs_0_.5, bf16[2,2048,256]{2,1,0:T(8,128)(2,1)} %collective-permute-done.4.refs_1_, bf16[16,16,128,128]{3,2,1,0:T(8,128)(2,1)} %refs_2_.5, f32[2048,256]{1,0:T(8,128)} %refs_3_.5), custom_call_target="tpu_custom_call" | custom-call | flops 12884901888 | bytes 18874368 | tf_op jit(solution)/shard_map/alpha_term/pallas_call | solution.py:262
  357.9 54.9 %collective-permute-done.3.refs_1_ = bf16[4,2048,256]{2,1,0:T(8,128)(2,1)} collective-permute-done((bf16[4,2048,256]{2,1,0:T(8,128)(2,1)}, bf16[4,2048,256]{2,1,0:T(8,128)(2,1)}, u32[]{:S(2)}, u32[]{:S(2)}) %collective-permute-start.3) | collective-permute-done | bytes 4194336 | tf_op jit(solution)/shard_map/ppermute | solution.py:352
  412.8 27.3 %alpha_term.4.acc_ref = f32[6,2048,256]{2,1,0:T(8,128)} custom-call(s32[256]{0:T(256)} %reshape.27.cols_ref, s32[4]{0:T(128)} %pad_add_fusion.place_ref, bf16[8,2048,256]{2,1,0:T(8,128)(2,1)} %refs_0_.5, bf16[4,2048,256]{2,1,0:T(8,128)(2,1)} %collective-permute-done.3.refs_1_, bf16[16,16,128,128]{3,2,1,0:T(8,128)(2,1)} %refs_2_.5, ...), custom_call_target="tpu_custom_call", output_to_operand_aliasing={{}: (6, {})} | custom-call | flops 25769803776 | bytes 27262976 | tf_op jit(solution)/shard_map/alpha_term/pallas_call | solution.py:262
  440.1 4.4 join_terms.2.rest_0_
  444.4 13.2 %all-to-all-done.3 = s16[8,1536,256]{2,1,0:T(8,128)(2,1)} async-done(((s16[8,1536,256]{2,1,0:T(8,128)(2,1)}), s16[8,1536,256]{2,1,0:T(8,128)(2,1)}, u32[]{:S(2)}, u32[]{:S(2)}) %all-to-all-start.3) | async-done | bytes 6291488 | tf_op jit(solution)/shard_map/all_to_all | solution.py:392
  457.6 10.9 %join_terms.3 = bf16[8,2048,256]{2,1,0:T(8,128)(2,1)} custom-call(f32[6,2048,256]{2,1,0:T(8,128)} %alpha_term.4.acc_ref, s16[8,2,6,128,256]{4,3,2,1,0:T(8,128)(2,1)} %bitcast.6.words_ref, bf16[8,2048,256]{2,1,0:T(8,128)(2,1)} %join_terms.2.rest_0_), custom_call_target="tpu_custom_call", output_to_operand_aliasing={{}: (2, {})} | custom-call | flops 25165824 | bytes 25165824 | tf_op jit(solution)/shard_map/join_terms/pallas_call | solution.py:307
  (41 shorter events, 27.1 us)
Async XLA Ops:
  12.2 113.3 %all-to-all-start = ((bf16[16,400,256]{2,1,0:T(8,128)(2,1)}), bf16[16,400,256]{2,1,0:T(8,128)(2,1)S(1)}, u32[]{:S(2)}, u32[]{:S(2)}) async-start(bf16[16,400,256]{2,1,0:T(8,128)(2,1)} %pack_pieces.2), calls=%async_computation | async-start | bytes 6553600 | tf_op jit(solution)/shard_map/all_to_all | solution.py:374
  18.8 91.1 %all-gather.3.cloned.1.call-start = ((), (), s32[]{:S(2)}) async-start(), calls=%async_computation.4 | async-start | bytes 2621440 | tf_op jit(solution)/shard_map/all_gather | solution.py:357
  37.3 80.0 %collective-permute-start.9 = (bf16[2,2048,256]{2,1,0:T(8,128)(2,1)}, bf16[2,2048,256]{2,1,0:T(8,128)(2,1)}, u32[]{:S(2)}, u32[]{:S(2)}) collective-permute-start(bf16[2,2048,256]{2,1,0:T(8,128)(2,1)} %get-tuple-element.18), channel_id=1, source_target_pairs={{16,0},{0,16},{17,1},{1,17},{18,2},{2,18},{19,3},{3,19},{20,4},{4,... | collective-permute-start | bytes 6291464 | tf_op jit(solution)/shard_map/ppermute | solution.py:352
  112.9 39.4 %collective-permute-start = (bf16[2,2048,128]{2,1,0:T(8,128)(2,1)}, bf16[2,2048,128]{2,1,0:T(8,128)(2,1)}, u32[]{:S(2)}, u32[]{:S(2)}) collective-permute-start(bf16[2,2048,128]{2,1,0:T(8,128)(2,1)} %bitcast.5.refs_2_.refs_4_), channel_id=1, source_target_pairs={{0,2},{1,3},{2,0},{3,1},{4,6},{5,7},{6,4},{7,5},{8,10},{9,11},{10,... | collective-permute-start | bytes 3145736 | tf_op jit(solution)/shard_map/ppermute | solution.py:345
  125.6 87.0 %copy-start.1 = (bf16[16,400,256]{2,1,0:T(8,128)(2,1)}, bf16[16,400,256]{2,1,0:T(8,128)(2,1)S(1)}, u32[]{:S(2)}) copy-start(bf16[16,400,256]{2,1,0:T(8,128)(2,1)S(1)} %all-to-all-done.refs_0_) | copy-start | bytes 9830404
  125.6 127.3 %all-to-all-start.1 = ((bf16[16,640,256]{2,1,0:T(8,128)(2,1)}), bf16[16,640,256]{2,1,0:T(8,128)(2,1)}, u32[]{:S(2)}, u32[]{:S(2)}) async-start(bf16[16,640,256]{2,1,0:T(8,128)(2,1)} %pack_pieces.3), calls=%async_computation.1 | async-start | bytes 10485760 | tf_op jit(solution)/shard_map/all_to_all | solution.py:376
  130.1 24.8 %collective-permute-start.5 = (bf16[2,2048,128]{2,1,0:T(8,128)(2,1)}, bf16[2,2048,128]{2,1,0:T(8,128)(2,1)S(1)}, u32[]{:S(2)}, u32[]{:S(2)}) collective-permute-start(bf16[2,2048,128]{2,1,0:T(8,128)(2,1)} %bitcast.5.refs_2_.refs_4_), channel_id=1, source_target_pairs={{0,16},{16,0},{1,17},{17,1},{2,18},{18,2},{3,19},{19,3},{4,20},{20... | collective-permute-start | bytes 3145736 | tf_op jit(solution)/shard_map/ppermute | solution.py:348
  152.3 24.3 %collective-permute-start.7 = (bf16[2,2048,128]{2,1,0:T(8,128)(2,1)}, bf16[2,2048,128]{2,1,0:T(8,128)(2,1)S(1)}, u32[]{:S(2)}, u32[]{:S(2)}) collective-permute-start(bf16[2,2048,128]{2,1,0:T(8,128)(2,1)} %bitcast.9), channel_id=1, source_target_pairs={{0,16},{16,0},{1,17},{17,1},{2,18},{18,2},{3,19},{19,3},{4,20},{20... | collective-permute-start | bytes 3145736 | tf_op jit(solution)/shard_map/ppermute | solution.py:348
  153.5 56.3 %collective-permute-start.1 = (bf16[2,2048,128]{2,1,0:T(8,128)(2,1)}, bf16[2,2048,128]{2,1,0:T(8,128)(2,1)}, u32[]{:S(2)}, u32[]{:S(2)}) collective-permute-start(bf16[2,2048,128]{2,1,0:T(8,128)(2,1)} %bitcast.10), channel_id=1, source_target_pairs={{0,2},{1,3},{2,0},{3,1},{4,6},{5,7},{6,4},{7,5},{8,10},{9,11},{10,... | collective-permute-start | bytes 3145736 | tf_op jit(solution)/shard_map/ppermute | solution.py:345
  153.5 56.3 %collective-permute-start.6 = (bf16[2,2048,128]{2,1,0:T(8,128)(2,1)}, bf16[2,2048,128]{2,1,0:T(8,128)(2,1)S(1)}, u32[]{:S(2)}, u32[]{:S(2)}) collective-permute-start(bf16[2,2048,128]{2,1,0:T(8,128)(2,1)} %collective-permute-done.refs_4_.refs_6_), channel_id=1, source_target_pairs={{0,16},{16,0},{1,17},{17,1},{2,18},{18,2},{3,19},{19,3},{4,20},{20... | collective-permute-start | bytes 3145736 | tf_op jit(solution)/shard_map/ppermute | solution.py:348
  154.9 56.4 %copy-start.3 = (bf16[2,2048,128]{2,1,0:T(8,128)(2,1)}, bf16[2,2048,128]{2,1,0:T(8,128)(2,1)S(1)}, u32[]{:S(2)}) copy-start(bf16[2,2048,128]{2,1,0:T(8,128)(2,1)S(1)} %collective-permute-done.5.refs_3_.refs_5_) | copy-start | bytes 3145732
  176.5 34.8 %copy-start.4 = (bf16[2,2048,128]{2,1,0:T(8,128)(2,1)}, bf16[2,2048,128]{2,1,0:T(8,128)(2,1)S(1)}, u32[]{:S(2)}) copy-start(bf16[2,2048,128]{2,1,0:T(8,128)(2,1)S(1)} %collective-permute-done.7.refs_7_.refs_9_) | copy-start | bytes 3145732
  209.9 1.4 copy-start.5
  209.9 25.6 %collective-permute-start.8 = (bf16[16,400,256]{2,1,0:T(8,128)(2,1)S(1)}, bf16[16,400,256]{2,1,0:T(8,128)(2,1)}, u32[]{:S(2)}, u32[]{:S(2)}) collective-permute-start(bf16[16,400,256]{2,1,0:T(8,128)(2,1)S(1)} %all-to-all-done.refs_0_), channel_id=1, source_target_pairs={{0,1},{1,0},{2,3},{3,2},{4,5},{5,4},{6,7},{7,6},{8,9},{9,8},{10,11... | collective-permute-start | bytes 9830408 | tf_op jit(solution)/shard_map/ppermute | solution.py:345
  211.3 24.1 %collective-permute-start.2 = (bf16[2,2048,128]{2,1,0:T(8,128)(2,1)}, bf16[2,2048,128]{2,1,0:T(8,128)(2,1)}, u32[]{:S(2)}, u32[]{:S(2)}) collective-permute-start(bf16[2,2048,128]{2,1,0:T(8,128)(2,1)} %collective-permute-done.1.refs_8_.refs_10_), channel_id=1, source_target_pairs={{0,16},{16,0},{1,17},{17,1},{2,18},{18,2},{3,19},{19,3},{4,20},{20... | collective-permute-start | bytes 3145736 | tf_op jit(solution)/shard_map/ppermute | solution.py:348
  252.9 16.3 %collective-permute-start.10 = (bf16[16,640,256]{2,1,0:T(8,128)(2,1)}, bf16[16,640,256]{2,1,0:T(8,128)(2,1)}, u32[]{:S(2)}, u32[]{:S(2)}) collective-permute-start(bf16[16,640,256]{2,1,0:T(8,128)(2,1)} %all-to-all-done.1.refs_2_), channel_id=1, source_target_pairs={{0,1},{1,0},{2,3},{3,2},{4,5},{5,4},{6,7},{7,6},{8,9},{9,8},{10,11... | collective-permute-start | bytes 15728648 | tf_op jit(solution)/shard_map/ppermute | solution.py:345
  254.8 60.1 %all-to-all-start.2 = ((s16[8,512,256]{2,1,0:T(8,128)(2,1)}), s16[8,512,256]{2,1,0:T(8,128)(2,1)S(1)}, u32[]{:S(2)}, u32[]{:S(2)}) async-start(s16[8,512,256]{2,1,0:T(8,128)(2,1)} %beta_term.2), calls=%async_computation.2 | async-start | bytes 4194304 | tf_op jit(solution)/shard_map/all_to_all | solution.py:392
  267.9 46.9 %collective-permute-start.4 = (bf16[2,2048,256]{2,1,0:T(8,128)(2,1)}, bf16[2,2048,256]{2,1,0:T(8,128)(2,1)}, u32[]{:S(2)}, u32[]{:S(2)}) collective-permute-start(bf16[2,2048,256]{2,1,0:T(8,128)(2,1)} %get-tuple-element.16), channel_id=1, source_target_pairs={{16,0},{0,16},{17,1},{1,17},{18,2},{2,18},{19,3},{3,19},{20,4},{4,... | collective-permute-start | bytes 6291464 | tf_op jit(solution)/shard_map/ppermute | solution.py:352
  307.8 15.5 %copy-start.2 = (s32[16,16]{1,0:T(8,128)S(1)}, s32[16,16]{1,0:T(8,128)}, u32[]{:S(2)}) copy-start(s32[16,16]{1,0:T(8,128)} %param.8) | copy-start | bytes 3076
  314.9 1.4 copy-start
  316.3 141.4 %all-to-all-start.3 = ((s16[8,1536,256]{2,1,0:T(8,128)(2,1)}), s16[8,1536,256]{2,1,0:T(8,128)(2,1)}, u32[]{:S(2)}, u32[]{:S(2)}) async-start(s16[8,1536,256]{2,1,0:T(8,128)(2,1)} %beta_term.3), calls=%async_computation.3 | async-start | bytes 12582912 | tf_op jit(solution)/shard_map/all_to_all | solution.py:392
  322.1 90.7 %collective-permute-start.3 = (bf16[4,2048,256]{2,1,0:T(8,128)(2,1)}, bf16[4,2048,256]{2,1,0:T(8,128)(2,1)}, u32[]{:S(2)}, u32[]{:S(2)}) collective-permute-start(bf16[4,2048,256]{2,1,0:T(8,128)(2,1)} %slice.12), channel_id=1, source_target_pairs={{16,0},{0,16},{17,1},{1,17},{18,2},{2,18},{19,3},{3,19},{20,4},{4,... | collective-permute-start | bytes 12582920 | tf_op jit(solution)/shard_map/ppermute | solution.py:352
Sparse Core Ops, SparseCore 0:
  22.3 87.4 all-gather.2

commit v10 on v9

--- a/solution.py
+++ b/solution.py
@@ -14,7 +14,7 @@
 CODE_BITS = 11
 LARGEST = 32767.0
 TILE = 16
-HINTS = (26, 4)
+HINTS = (42, 4)
 VMEM = 60 * MIB
 CORES = 2
 ANYWHERE = pl.BlockSpec(memory_space=pl.ANY)
@@ -290,12 +290,13 @@
 
 
 def join(acc, words, first, vectors, before):
-    count, rows, strip = acc.shape
+    _, rows, strip = acc.shape
     sources = words.shape[0]
     few_rows = rows // (sources * CORES)
-    words = words.reshape(sources, CORES, count, few_rows, strip)
+    words = words.reshape(sources, CORES, -1, few_rows, strip)
+    count = words.shape[2]
     in_specs = [
-        pl.BlockSpec((1, rows, strip), lambda v: (v, 0, 0)),
+        pl.BlockSpec((1, rows, strip), lambda v: (first + v, 0, 0)),
         pl.BlockSpec((sources, CORES, 1, few_rows, strip), lambda v: (0, 0, v, 0, 0)),
     ]
     args = [acc, words]
@@ -334,12 +335,11 @@
     parity = lax.rem(at_a, 2)
     place = jnp.stack([lax.rem(at_b, CORES), lax.rem(lax.div(at_b, CORES), xs), parity, at_a]).astype(jnp.int32)
     few = vectors // 4
-    lead = 3 * vectors // 8
-    cuts = [(0, lead), (lead, vectors - lead)]
-    back = [(0, few), (few, vectors - few)]
-    shares = [(0, few), (few, few), (2 * few, vectors - 2 * few)]
+    cuts = [(vectors - few, few), (0, vectors - few)]
+    early = 3 * vectors // 8
+    shares = [(0, early), (early, vectors // 2 - early), (vectors // 2, vectors - vectors // 2)]
     sent = [ci_vectors[first : first + count] for first, count in shares]
-    pieces = 2
+    pieces = 1
 
     def swap(value, bit):
         return lax.ppermute(value, "beta", [(i, i ^ bit) for i in range(ring)])
@@ -361,51 +361,51 @@
 
     others = [exchange(after(sent[0], (packed[1], *sent[1:])))]
 
-    messages = []
+    carried = []
     for g in jnp.split(gathered, pieces):
-        carried = [after(g, messages[-2]) if messages else g]
-        bit = CORES
+        group, bit = [g], CORES
         while bit < inner:
-            carried = carried + [swap(m, bit) for m in carried]
+            group = group + [swap(m, bit) for m in group]
             bit *= 2
-        for m in carried:
-            messages += [m, across(m)]
+        carried += group
 
     turned = [lax.all_to_all(packed[0], "beta", split_axis=0, concat_axis=0, tiled=True)]
-    second = after(packed[1], (turned[0], messages[0], others[0][-1]))
+    second = after(packed[1], (turned[0], gathered, others[0][-1]))
     turned.append(lax.all_to_all(second, "beta", split_axis=0, concat_axis=0, tiled=True))
     columns = turned[0][:, cuts[0][1] * few_rows, : owned * slots].reshape(-1).astype(jnp.int32)
-    twins = [swap(after(turned[0], tuple(messages[1:-1])), 1)]
+    twins = [swap(turned[0], 1)]
+
+    messages = []
+    for i, m in enumerate(carried):
+        if i == len(carried) - 1:
+            m = after(m, (*messages[1::2], twins[0]))
+        messages += [m, across(m)]
     for value in sent[1:]:
         others.append(exchange(after(value, messages[-1])))
 
-    def alpha(i, base, total, before):
-        return alpha_term(
-            alpha_cols.reshape(-1), place, ci_vectors, others[i], alpha_blocks, diagonal, *shares[i], base, total, before
+    acc = None
+    for i, share in enumerate(shares):
+        acc = alpha_term(
+            alpha_cols.reshape(-1), place, ci_vectors, others[i], alpha_blocks, diagonal, *share, 0, vectors, acc
         )
-
-    acc = [alpha(0, 0, few, None), alpha(2, few, vectors - few, alpha(1, few, vectors - few, None))]
 
     near = [[j * CORES + c for j in range(ring // CORES)] for c in range(CORES)]
 
     def send_back(term):
         return lax.all_to_all(term, "beta", split_axis=0, concat_axis=0, tiled=True, axis_index_groups=near)
 
-    rest = cuts[0][1] - few
-    parts = [(turned[0], twins[0], 0, few * few_rows)]
-    term = beta_term(slots, xs, columns, place, parts, messages, pieces, HINTS[0])
+    def term_of(i):
+        parts = [(turned[i], twins[i], 0, cuts[i][1] * few_rows)]
+        return beta_term(slots, xs, columns, place, parts, messages, pieces, HINTS[i])
+
+    term = term_of(0)
     twins.append(swap(after(turned[1], term), 1))
     words = [send_back(after(term, turned[1]))]
-    parts = [
-        (turned[0], twins[0], few * few_rows, rest * few_rows),
-        (turned[1], twins[1], 0, cuts[1][1] * few_rows),
-    ]
-    term = beta_term(slots, xs, columns, place, parts, messages, pieces, HINTS[1])
-    words.append(send_back(after(term, (words[0], others[1][-1]))))
+    words.append(send_back(after(term_of(1), (words[0], others[1][-1]))))
 
     total = None
-    for i, (first, _) in enumerate(back):
-        total = join(acc[i], words[i], first, vectors, total)
+    for i, (first, _) in enumerate(cuts):
+        total = join(acc, words[i], first, vectors, total)
     return total
 
 

time: 480 us -> 468 us (0.975)
  starting transfers between devices: 45.7 us -> 30.8 us
    all_gather x1, waiting for transfers between devices: 71.3 us -> 0.01 us  [shards(): lax.all_gather(mine, 'beta', axis=0, tiled=False, axis_index_groups=far)]
    all_to_all x1, waiting for transfers between devices: 8.17 us -> 64.9 us  [shards(): lax.all_to_all(packed[0], 'beta', split_axis=0, concat_axis=0, tiled=True)]
    ppermute x4 -> x2, waiting for transfers between devices: 44.9 us -> 80.1 us  [across(): return lax.ppermute(value, 'alpha', [(i, i ^ 1) for i in range(ring_a)])]
    ppermute x4 -> x3, waiting for transfers between devices: 54.2 us -> 21.2 us  [swap(): return lax.ppermute(value, 'beta', [(i, i ^ bit) for i in range(ring)])]
    all_to_all x1, waiting for transfers between devices: 0.01 us -> 20.4 us  [shards(): lax.all_to_all(second, 'beta', split_axis=0, concat_axis=0, tiled=True)]
    all_to_all x2, starting transfers between devices: 19 us -> 11.2 us  [send_back(): lax.all_to_all(term, 'beta', split_axis=0, concat_axis=0, tiled=True, axi...]
    ppermute x4 -> x3, starting transfers between devices: 7.83 us -> 0.22 us  [swap(): return lax.ppermute(value, 'beta', [(i, i ^ bit) for i in range(ring)])]
    ppermute x3, waiting for transfers between devices: 62 us -> 56.9 us  [exchange(): lax.ppermute(value, 'alpha', [((i + s) % ring_a, i) for i in range(ring_a)])]
  transfers between devices with their start and end apart: 16 -> 13, of which waited for: 10 -> 10; matrix products, arithmetic and copies ran while one was open for 3% -> 2% of each run, Pallas kernels for 27% -> 28%
where the time goes in v10:
time: 468 us; the launch traced here: 463 us
  waiting for transfers between devices  258 us (55%)
  Pallas kernels  145 us (31%)
  starting transfers between devices  30.8 us (7%)
  local copies, waits for them, and re-layouts  13.5 us (3%)
  between operations  13.5 us (3%)
    ppermute x2, waiting for transfers between devices, across(): return lax.ppermute(value, 'alpha', [(i, i ^ 1) for i in range(ring_a)])  80.1 us
    all_to_all x1, waiting for transfers between devices, shards(): lax.all_to_all(packed[0], 'beta', split_axis=0, concat_axis=0, tiled=True)  64.9 us
    pallas_call x3, Pallas kernels, alpha_term(): pl.pallas_call(functools.partial(alpha_kernel, pieces), grid_spec=pltpu.P...  61.2 us
    ppermute x3, waiting for transfers between devices, exchange(): lax.ppermute(value, 'alpha', [((i + s) % ring_a, i) for i in range(ring_a)])  56.9 us
    pallas_call x2, Pallas kernels, beta_term(): pl.pallas_call(functools.partial(beta_kernel, slots, xs, segments, pieces...  55.9 us
    ppermute x3, waiting for transfers between devices, swap(): return lax.ppermute(value, 'beta', [(i, i ^ bit) for i in range(ring)])  21.2 us
    all_to_all x1, waiting for transfers between devices, shards(): lax.all_to_all(second, 'beta', split_axis=0, concat_axis=0, tiled=True)  20.4 us
    pallas_call x2, Pallas kernels, join(): pl.pallas_call(functools.partial(join_kernel, few_rows), grid=(count,), i...  15.3 us
  transfers between devices with their start and end apart: 13, of which 10 were waited for; matrix products, arithmetic and copies ran while one was open for 2% of the time, Pallas kernels for 28%

profile of v10, /device:TPU:11, one launch (start us, length us, event | category | flops | bytes accessed | tf_op | source)
XLA Modules:
  0.0 462.9 jit_solution(11818117202517975794)
XLA Ops:
  7.9 3.8 pack_pieces.2
  11.7 6.6 %all-to-all-start = ((bf16[16,272,256]{2,1,0:T(8,128)(2,1)}), bf16[16,272,256]{2,1,0:T(8,128)(2,1)}, u32[]{:S(2)}, u32[]{:S(2)}) async-start(bf16[16,272,256]{2,1,0:T(8,128)(2,1)} %pack_pieces.2), calls=%async_computation | async-start | bytes 4456448 | tf_op jit(solution)/shard_map/all_to_all | solution.py:372
  18.9 2.7 turn_blocks.1
  21.7 2.3 slice.13
  26.0 4.4 slice.12
  30.4 6.0 %pack_pieces.3 = bf16[16,768,256]{2,1,0:T(8,128)(2,1)} custom-call(bf16[8,2048,256]{2,1,0:T(8,128)(2,1)} %refs_0_.5), custom_call_target="tpu_custom_call" | custom-call | bytes 12582912 | tf_op jit(solution)/shard_map/pack_pieces/pallas_call | solution.py:79
  37.7 64.9 %all-to-all-done.refs_0_ = bf16[16,272,256]{2,1,0:T(8,128)(2,1)} async-done(((bf16[16,272,256]{2,1,0:T(8,128)(2,1)}), bf16[16,272,256]{2,1,0:T(8,128)(2,1)}, u32[]{:S(2)}, u32[]{:S(2)}) %all-to-all-start) | async-done | bytes 2228256 | tf_op jit(solution)/shard_map/all_to_all | solution.py:372
  105.9 7.6 %all-to-all-start.1 = ((bf16[16,768,256]{2,1,0:T(8,128)(2,1)}), bf16[16,768,256]{2,1,0:T(8,128)(2,1)}, u32[]{:S(2)}, u32[]{:S(2)}) async-start(bf16[16,768,256]{2,1,0:T(8,128)(2,1)} %pack_pieces.3), calls=%async_computation.1 | async-start | bytes 12582912 | tf_op jit(solution)/shard_map/all_to_all | solution.py:374
  113.5 37.3 %collective-permute-done.1.refs_3_ = bf16[4,2048,128]{2,1,0:T(8,128)(2,1)} collective-permute-done((bf16[4,2048,128]{2,1,0:T(8,128)(2,1)}, bf16[4,2048,128]{2,1,0:T(8,128)(2,1)}, u32[]{:S(2)}, u32[]{:S(2)}) %collective-permute-start.1) | collective-permute-done | bytes 2097184 | tf_op jit(solution)/shard_map/ppermute | solution.py:348
  150.8 16.6 %collective-permute-done.refs_4_ = bf16[4,2048,128]{2,1,0:T(8,128)(2,1)} collective-permute-done((bf16[4,2048,128]{2,1,0:T(8,128)(2,1)}, bf16[4,2048,128]{2,1,0:T(8,128)(2,1)}, u32[]{:S(2)}, u32[]{:S(2)}) %collective-permute-start) | collective-permute-done | bytes 2097184 | tf_op jit(solution)/shard_map/ppermute | solution.py:345
  169.1 42.8 %collective-permute-done.3.refs_5_ = bf16[4,2048,128]{2,1,0:T(8,128)(2,1)S(1)} collective-permute-done((bf16[4,2048,128]{2,1,0:T(8,128)(2,1)}, bf16[4,2048,128]{2,1,0:T(8,128)(2,1)S(1)}, u32[]{:S(2)}, u32[]{:S(2)}) %collective-permute-start.3) | collective-permute-done | bytes 2097184 | tf_op jit(solution)/shard_map/ppermute | solution.py:348
  213.2 17.4 %beta_term.2 = s16[8,512,256]{2,1,0:T(8,128)(2,1)} custom-call(s32[512]{0:T(512)} %reshape.30.cols_ref, s32[4]{0:T(128)} %pad_add_fusion.place_ref, bf16[16,272,256]{2,1,0:T(8,128)(2,1)} %all-to-all-done.refs_0_, bf16[16,272,256]{2,1,0:T(8,128)(2,1)} %collective-permute-done.2.refs_1_, bf16[4,2048,128]{2,1,0:T(8,128)(2,1)} %bitcast.10, ...), custom_call_target="tpu_custom_call" | custom-call | flops 90194313216 | bytes 16777216 | tf_op jit(solution)/shard_map/beta_term/pallas_call | solution.py:194
  230.6 20.4 %all-to-all-done.1.refs_0_ = bf16[16,768,256]{2,1,0:T(8,128)(2,1)} async-done(((bf16[16,768,256]{2,1,0:T(8,128)(2,1)}), bf16[16,768,256]{2,1,0:T(8,128)(2,1)}, u32[]{:S(2)}, u32[]{:S(2)}) %all-to-all-start.1) | async-done | bytes 6291488 | tf_op jit(solution)/shard_map/all_to_all | solution.py:374
  251.2 4.4 all-to-all-start.2
  256.9 4.6 collective-permute-done.7.refs_1_
  261.5 38.4 %beta_term.3 = s16[8,1536,256]{2,1,0:T(8,128)(2,1)} custom-call(s32[512]{0:T(512)} %reshape.30.cols_ref, s32[4]{0:T(128)} %pad_add_fusion.place_ref, bf16[16,768,256]{2,1,0:T(8,128)(2,1)} %all-to-all-done.1.refs_0_, bf16[16,768,256]{2,1,0:T(8,128)(2,1)} %collective-permute-done.7.refs_1_, bf16[4,2048,128]{2,1,0:T(8,128)(2,1)} %bitcast.11, ...), custom_call_target="tpu_custom_call" | custom-call | flops 25769803776 | bytes 33554432 | tf_op jit(solution)/shard_map/beta_term/pallas_call | solution.py:194
  302.7 6.8 %all-to-all-start.3 = ((s16[8,1536,256]{2,1,0:T(8,128)(2,1)}), s16[8,1536,256]{2,1,0:T(8,128)(2,1)}, u32[]{:S(2)}, u32[]{:S(2)}) async-start(s16[8,1536,256]{2,1,0:T(8,128)(2,1)} %beta_term.3), calls=%async_computation.3 | async-start | bytes 12582912 | tf_op jit(solution)/shard_map/all_to_all | solution.py:395
  311.4 22.1 %alpha_term.3.refs_4_ = f32[8,2048,256]{2,1,0:T(8,128)} custom-call(s32[256]{0:T(256)} %reshape.27.cols_ref, s32[4]{0:T(128)} %pad_add_fusion.place_ref, bf16[8,2048,256]{2,1,0:T(8,128)(2,1)} %refs_0_.5, bf16[3,2048,256]{2,1,0:T(8,128)(2,1)} %collective-permute-done.6.refs_1_, bf16[16,16,128,128]{3,2,1,0:T(8,128)(2,1)} %refs_2_.5, f32[2048,256]{1,0:T(8,128)} %refs_3_.5), custom_call_target="tpu_custom_call" | custom-call | flops 19327352832 | bytes 23068672 | tf_op jit(solution)/shard_map/alpha_term/pallas_call | solution.py:262
  333.6 11.8 %alpha_term.4.refs_4_ = f32[8,2048,256]{2,1,0:T(8,128)} custom-call(s32[256]{0:T(256)} %reshape.27.cols_ref, s32[4]{0:T(128)} %pad_add_fusion.place_ref, bf16[8,2048,256]{2,1,0:T(8,128)(2,1)} %refs_0_.5, bf16[1,2048,256]{2,1,0:T(8,128)(2,1)} %copy-done.1, bf16[16,16,128,128]{3,2,1,0:T(8,128)(2,1)} %refs_2_.5, ...), custom_call_target="tpu_custom_call", output_to_operand_aliasing={{}: (6, {})} | custom-call | flops 6442450944 | bytes 14680064 | tf_op jit(solution)/shard_map/alpha_term/pallas_call | solution.py:262
  345.3 54.9 %collective-permute-done.4.refs_1_ = bf16[4,2048,256]{2,1,0:T(8,128)(2,1)} collective-permute-done((bf16[4,2048,256]{2,1,0:T(8,128)(2,1)}, bf16[4,2048,256]{2,1,0:T(8,128)(2,1)}, u32[]{:S(2)}, u32[]{:S(2)}) %collective-permute-start.4) | collective-permute-done | bytes 4194336 | tf_op jit(solution)/shard_map/ppermute | solution.py:352
  400.2 27.3 %alpha_term.5.acc_ref = f32[8,2048,256]{2,1,0:T(8,128)} custom-call(s32[256]{0:T(256)} %reshape.27.cols_ref, s32[4]{0:T(128)} %pad_add_fusion.place_ref, bf16[8,2048,256]{2,1,0:T(8,128)(2,1)} %refs_0_.5, bf16[4,2048,256]{2,1,0:T(8,128)(2,1)} %collective-permute-done.4.refs_1_, bf16[16,16,128,128]{3,2,1,0:T(8,128)(2,1)} %refs_2_.5, ...), custom_call_target="tpu_custom_call", output_to_operand_aliasing={{}: (6, {})} | custom-call | flops 25769803776 | bytes 27262976 | tf_op jit(solution)/shard_map/alpha_term/pallas_call | solution.py:262
  427.5 4.4 join_terms.2.rest_0_
  431.9 13.2 %all-to-all-done.3 = s16[8,1536,256]{2,1,0:T(8,128)(2,1)} async-done(((s16[8,1536,256]{2,1,0:T(8,128)(2,1)}), s16[8,1536,256]{2,1,0:T(8,128)(2,1)}, u32[]{:S(2)}, u32[]{:S(2)}) %all-to-all-start.3) | async-done | bytes 6291488 | tf_op jit(solution)/shard_map/all_to_all | solution.py:395
  445.1 10.9 %join_terms.3 = bf16[8,2048,256]{2,1,0:T(8,128)(2,1)} custom-call(f32[8,2048,256]{2,1,0:T(8,128)} %alpha_term.5.acc_ref, s16[8,2,6,128,256]{4,3,2,1,0:T(8,128)(2,1)} %bitcast.5.words_ref, bf16[8,2048,256]{2,1,0:T(8,128)(2,1)} %join_terms.2.rest_0_), custom_call_target="tpu_custom_call", output_to_operand_aliasing={{}: (2, {})} | custom-call | flops 25165824 | bytes 25165824 | tf_op jit(solution)/shard_map/join_terms/pallas_call | solution.py:308
  (31 shorter events, 17.7 us)
Async XLA Ops:
  11.7 90.9 %all-to-all-start = ((bf16[16,272,256]{2,1,0:T(8,128)(2,1)}), bf16[16,272,256]{2,1,0:T(8,128)(2,1)}, u32[]{:S(2)}, u32[]{:S(2)}) async-start(bf16[16,272,256]{2,1,0:T(8,128)(2,1)} %pack_pieces.2), calls=%async_computation | async-start | bytes 4456448 | tf_op jit(solution)/shard_map/all_to_all | solution.py:372
  18.3 84.3 %all-gather.3.cloned.1.call-start = ((), (), s32[]{:S(2)}) async-start(), calls=%async_computation.4 | async-start | bytes 2621440 | tf_op jit(solution)/shard_map/all_gather | solution.py:357
  36.4 69.4 %collective-permute-start.6 = (bf16[3,2048,256]{2,1,0:T(8,128)(2,1)S(1)}, bf16[3,2048,256]{2,1,0:T(8,128)(2,1)}, u32[]{:S(2)}, u32[]{:S(2)}) collective-permute-start(bf16[3,2048,256]{2,1,0:T(8,128)(2,1)S(1)} %slice.14), channel_id=1, source_target_pairs={{16,0},{0,16},{17,1},{1,17},{18,2},{2,18},{19,3},{3,19},{20,4},{4,... | collective-permute-start | bytes 9437192 | tf_op jit(solution)/shard_map/ppermute | solution.py:352
  102.6 64.8 %collective-permute-start.2 = (bf16[16,272,256]{2,1,0:T(8,128)(2,1)}, bf16[16,272,256]{2,1,0:T(8,128)(2,1)}, u32[]{:S(2)}, u32[]{:S(2)}) collective-permute-start(bf16[16,272,256]{2,1,0:T(8,128)(2,1)} %all-to-all-done.refs_0_), channel_id=1, source_target_pairs={{0,1},{1,0},{2,3},{3,2},{4,5},{5,4},{6,7},{7,6},{8,9},{9,8},{10,11... | collective-permute-start | bytes 6684680 | tf_op jit(solution)/shard_map/ppermute | solution.py:345
  102.6 48.2 %collective-permute-start.1 = (bf16[4,2048,128]{2,1,0:T(8,128)(2,1)}, bf16[4,2048,128]{2,1,0:T(8,128)(2,1)}, u32[]{:S(2)}, u32[]{:S(2)}) collective-permute-start(bf16[4,2048,128]{2,1,0:T(8,128)(2,1)} %bitcast.8), channel_id=1, source_target_pairs={{0,16},{16,0},{1,17},{17,1},{2,18},{18,2},{3,19},{19,3},{4,20},{20... | collective-permute-start | bytes 6291464 | tf_op jit(solution)/shard_map/ppermute | solution.py:348
  103.9 63.5 %collective-permute-start = (bf16[4,2048,128]{2,1,0:T(8,128)(2,1)}, bf16[4,2048,128]{2,1,0:T(8,128)(2,1)}, u32[]{:S(2)}, u32[]{:S(2)}) collective-permute-start(bf16[4,2048,128]{2,1,0:T(8,128)(2,1)} %bitcast.9), channel_id=1, source_target_pairs={{0,2},{1,3},{2,0},{3,1},{4,6},{5,7},{6,4},{7,5},{8,10},{9,11},{10,... | collective-permute-start | bytes 6291464 | tf_op jit(solution)/shard_map/ppermute | solution.py:345
  105.9 145.2 %all-to-all-start.1 = ((bf16[16,768,256]{2,1,0:T(8,128)(2,1)}), bf16[16,768,256]{2,1,0:T(8,128)(2,1)}, u32[]{:S(2)}, u32[]{:S(2)}) async-start(bf16[16,768,256]{2,1,0:T(8,128)(2,1)} %pack_pieces.3), calls=%async_computation.1 | async-start | bytes 12582912 | tf_op jit(solution)/shard_map/all_to_all | solution.py:374
  167.4 44.5 %collective-permute-start.3 = (bf16[4,2048,128]{2,1,0:T(8,128)(2,1)}, bf16[4,2048,128]{2,1,0:T(8,128)(2,1)S(1)}, u32[]{:S(2)}, u32[]{:S(2)}) collective-permute-start(bf16[4,2048,128]{2,1,0:T(8,128)(2,1)} %collective-permute-done.refs_4_), channel_id=1, source_target_pairs={{0,16},{16,0},{1,17},{17,1},{2,18},{18,2},{3,19},{19,3},{4,20},{20... | collective-permute-start | bytes 6291464 | tf_op jit(solution)/shard_map/ppermute | solution.py:348
  211.9 1.3 copy-start.3
  251.0 10.5 %collective-permute-start.7 = (bf16[16,768,256]{2,1,0:T(8,128)(2,1)}, bf16[16,768,256]{2,1,0:T(8,128)(2,1)}, u32[]{:S(2)}, u32[]{:S(2)}) collective-permute-start(bf16[16,768,256]{2,1,0:T(8,128)(2,1)} %all-to-all-done.1.refs_0_), channel_id=1, source_target_pairs={{0,1},{1,0},{2,3},{3,2},{4,5},{5,4},{6,7},{7,6},{8,9},{9,8},{10,11... | collective-permute-start | bytes 18874376 | tf_op jit(solution)/shard_map/ppermute | solution.py:345
  251.2 50.2 %all-to-all-start.2 = ((s16[8,512,256]{2,1,0:T(8,128)(2,1)}), s16[8,512,256]{2,1,0:T(8,128)(2,1)S(1)}, u32[]{:S(2)}, u32[]{:S(2)}) async-start(s16[8,512,256]{2,1,0:T(8,128)(2,1)} %beta_term.2), calls=%async_computation.2 | async-start | bytes 4194304 | tf_op jit(solution)/shard_map/all_to_all | solution.py:395
  255.7 44.3 %collective-permute-start.5 = (bf16[1,2048,256]{2,1,0:T(8,128)(2,1)}, bf16[1,2048,256]{2,1,0:T(8,128)(2,1)S(1)}, u32[]{:S(2)}, u32[]{:S(2)}) collective-permute-start(bf16[1,2048,256]{2,1,0:T(8,128)(2,1)} %slice.13), channel_id=1, source_target_pairs={{16,0},{0,16},{17,1},{1,17},{18,2},{2,18},{19,3},{3,19},{20,4},{4,... | collective-permute-start | bytes 3145736 | tf_op jit(solution)/shard_map/ppermute | solution.py:352
  300.0 10.7 %copy-start.2 = (s32[16,16]{1,0:T(8,128)S(1)}, s32[16,16]{1,0:T(8,128)}, u32[]{:S(2)}) copy-start(s32[16,16]{1,0:T(8,128)} %param.8) | copy-start | bytes 3076
  300.0 1.4 copy-start.1
  301.4 1.3 copy-start
  302.7 142.3 %all-to-all-start.3 = ((s16[8,1536,256]{2,1,0:T(8,128)(2,1)}), s16[8,1536,256]{2,1,0:T(8,128)(2,1)}, u32[]{:S(2)}, u32[]{:S(2)}) async-start(s16[8,1536,256]{2,1,0:T(8,128)(2,1)} %beta_term.3), calls=%async_computation.3 | async-start | bytes 12582912 | tf_op jit(solution)/shard_map/all_to_all | solution.py:395
  309.5 90.7 %collective-permute-start.4 = (bf16[4,2048,256]{2,1,0:T(8,128)(2,1)}, bf16[4,2048,256]{2,1,0:T(8,128)(2,1)}, u32[]{:S(2)}, u32[]{:S(2)}) collective-permute-start(bf16[4,2048,256]{2,1,0:T(8,128)(2,1)} %slice.12), channel_id=1, source_target_pairs={{16,0},{0,16},{17,1},{1,17},{18,2},{2,18},{19,3},{3,19},{20,4},{4,... | collective-permute-start | bytes 12582920 | tf_op jit(solution)/shard_map/ppermute | solution.py:352
Sparse Core Ops, SparseCore 0:
  21.8 74.9 all-gather.2

commit v11 on v10

--- a/solution.py
+++ b/solution.py
@@ -359,7 +359,7 @@
     heads = jnp.pad(beta_cols.reshape(1, -1).astype(jnp.bfloat16), ((0, TILE - 1), (0, strip - owned * slots)))
     packed = [pack(ci_vectors, heads if i == 0 else None, *cut, ring) for i, cut in enumerate(cuts)]
 
-    others = [exchange(after(sent[0], (packed[1], *sent[1:])))]
+    others = [exchange(after(sent[0], packed[1]))]
 
     carried = []
     for g in jnp.split(gathered, pieces):

time: 468 us -> 468 us (level)
    all_to_all x1, waiting for transfers between devices: 64.9 us -> 71.3 us  [shards(): lax.all_to_all(packed[0], 'beta', split_axis=0, concat_axis=0, tiled=True)]
  transfers between devices with their start and end apart: 13 -> 13, of which waited for: 10 -> 8; matrix products, arithmetic and copies ran while one was open for 2% -> 2% of each run, Pallas kernels for 28% -> 28%
where the time goes in v11:
time: 468 us; the launch traced here: 463 us
  waiting for transfers between devices  258 us (55%)
  Pallas kernels  145 us (31%)
  starting transfers between devices  31.4 us (7%)
  local copies, waits for them, and re-layouts  13.5 us (3%)
  between operations  13.5 us (3%)
    ppermute x2, waiting for transfers between devices, across(): return lax.ppermute(value, 'alpha', [(i, i ^ 1) for i in range(ring_a)])  83.3 us
    all_to_all x1, waiting for transfers between devices, shards(): lax.all_to_all(packed[0], 'beta', split_axis=0, concat_axis=0, tiled=True)  71.3 us
    pallas_call x3, Pallas kernels, alpha_term(): pl.pallas_call(functools.partial(alpha_kernel, pieces), grid_spec=pltpu.P...  61.2 us
    ppermute x3, waiting for transfers between devices, exchange(): lax.ppermute(value, 'alpha', [((i + s) % ring_a, i) for i in range(ring_a)])  56.2 us
    pallas_call x2, Pallas kernels, beta_term(): pl.pallas_call(functools.partial(beta_kernel, slots, xs, segments, pieces...  55.9 us
    ppermute x3, waiting for transfers between devices, swap(): return lax.ppermute(value, 'beta', [(i, i ^ bit) for i in range(ring)])  17.8 us
    all_to_all x1, waiting for transfers between devices, shards(): lax.all_to_all(second, 'beta', split_axis=0, concat_axis=0, tiled=True)  15.9 us
    pallas_call x2, Pallas kernels, join(): pl.pallas_call(functools.partial(join_kernel, few_rows), grid=(count,), i...  15.3 us
  transfers between devices with their start and end apart: 13, of which 8 were waited for; matrix products, arithmetic and copies ran while one was open for 2% of the time, Pallas kernels for 28%

profile of v11, /device:TPU:11, one launch (start us, length us, event | category | flops | bytes accessed | tf_op | source)
XLA Modules:
  0.0 463.1 jit_solution(484157273002930105)
XLA Ops:
  7.9 3.8 pack_pieces.2
  11.7 6.6 %all-to-all-start = ((bf16[16,272,256]{2,1,0:T(8,128)(2,1)}), bf16[16,272,256]{2,1,0:T(8,128)(2,1)}, u32[]{:S(2)}, u32[]{:S(2)}) async-start(bf16[16,272,256]{2,1,0:T(8,128)(2,1)} %pack_pieces.2), calls=%async_computation | async-start | bytes 4456448 | tf_op jit(solution)/shard_map/all_to_all | solution.py:372
  19.0 2.7 turn_blocks.1
  23.8 5.9 %pack_pieces.3 = bf16[16,768,256]{2,1,0:T(8,128)(2,1)} custom-call(bf16[8,2048,256]{2,1,0:T(8,128)(2,1)} %refs_0_.5), custom_call_target="tpu_custom_call" | custom-call | bytes 12582912 | tf_op jit(solution)/shard_map/pack_pieces/pallas_call | solution.py:79
  31.0 71.3 %all-to-all-done.refs_0_ = bf16[16,272,256]{2,1,0:T(8,128)(2,1)} async-done(((bf16[16,272,256]{2,1,0:T(8,128)(2,1)}), bf16[16,272,256]{2,1,0:T(8,128)(2,1)}, u32[]{:S(2)}, u32[]{:S(2)}) %all-to-all-start) | async-done | bytes 2228256 | tf_op jit(solution)/shard_map/all_to_all | solution.py:372
  103.8 6.0 %all-to-all-start.1 = ((bf16[16,768,256]{2,1,0:T(8,128)(2,1)}), bf16[16,768,256]{2,1,0:T(8,128)(2,1)}, u32[]{:S(2)}, u32[]{:S(2)}) async-start(bf16[16,768,256]{2,1,0:T(8,128)(2,1)} %pack_pieces.3), calls=%async_computation.1 | async-start | bytes 12582912 | tf_op jit(solution)/shard_map/all_to_all | solution.py:374
  109.8 40.0 %collective-permute-done.1.refs_3_ = bf16[4,2048,128]{2,1,0:T(8,128)(2,1)} collective-permute-done((bf16[4,2048,128]{2,1,0:T(8,128)(2,1)}, bf16[4,2048,128]{2,1,0:T(8,128)(2,1)}, u32[]{:S(2)}, u32[]{:S(2)}) %collective-permute-start.1) | collective-permute-done | bytes 2097184 | tf_op jit(solution)/shard_map/ppermute | solution.py:348
  149.8 17.8 %collective-permute-done.refs_4_ = bf16[4,2048,128]{2,1,0:T(8,128)(2,1)} collective-permute-done((bf16[4,2048,128]{2,1,0:T(8,128)(2,1)}, bf16[4,2048,128]{2,1,0:T(8,128)(2,1)}, u32[]{:S(2)}, u32[]{:S(2)}) %collective-permute-start) | collective-permute-done | bytes 2097184 | tf_op jit(solution)/shard_map/ppermute | solution.py:345
  169.2 43.3 %collective-permute-done.3.refs_5_ = bf16[4,2048,128]{2,1,0:T(8,128)(2,1)S(1)} collective-permute-done((bf16[4,2048,128]{2,1,0:T(8,128)(2,1)}, bf16[4,2048,128]{2,1,0:T(8,128)(2,1)S(1)}, u32[]{:S(2)}, u32[]{:S(2)}) %collective-permute-start.3) | collective-permute-done | bytes 2097184 | tf_op jit(solution)/shard_map/ppermute | solution.py:348
  213.8 17.5 %beta_term.2 = s16[8,512,256]{2,1,0:T(8,128)(2,1)} custom-call(s32[512]{0:T(512)} %reshape.30.cols_ref, s32[4]{0:T(128)} %pad_add_fusion.place_ref, bf16[16,272,256]{2,1,0:T(8,128)(2,1)} %all-to-all-done.refs_0_, bf16[16,272,256]{2,1,0:T(8,128)(2,1)} %collective-permute-done.2.refs_1_, bf16[4,2048,128]{2,1,0:T(8,128)(2,1)} %bitcast.10, ...), custom_call_target="tpu_custom_call" | custom-call | flops 90194313216 | bytes 16777216 | tf_op jit(solution)/shard_map/beta_term/pallas_call | solution.py:194
  231.3 15.9 %all-to-all-done.1.refs_0_ = bf16[16,768,256]{2,1,0:T(8,128)(2,1)} async-done(((bf16[16,768,256]{2,1,0:T(8,128)(2,1)}), bf16[16,768,256]{2,1,0:T(8,128)(2,1)}, u32[]{:S(2)}, u32[]{:S(2)}) %all-to-all-start.1) | async-done | bytes 6291488 | tf_op jit(solution)/shard_map/all_to_all | solution.py:374
  247.5 8.2 %all-to-all-start.2 = ((s16[8,512,256]{2,1,0:T(8,128)(2,1)}), s16[8,512,256]{2,1,0:T(8,128)(2,1)S(1)}, u32[]{:S(2)}, u32[]{:S(2)}) async-start(s16[8,512,256]{2,1,0:T(8,128)(2,1)} %beta_term.2), calls=%async_computation.2 | async-start | bytes 4194304 | tf_op jit(solution)/shard_map/all_to_all | solution.py:395
  255.7 2.3 slice.13
  258.2 38.4 %beta_term.3 = s16[8,1536,256]{2,1,0:T(8,128)(2,1)} custom-call(s32[512]{0:T(512)} %reshape.30.cols_ref, s32[4]{0:T(128)} %pad_add_fusion.place_ref, bf16[16,768,256]{2,1,0:T(8,128)(2,1)} %all-to-all-done.1.refs_0_, bf16[16,768,256]{2,1,0:T(8,128)(2,1)} %collective-permute-done.7.refs_1_, bf16[4,2048,128]{2,1,0:T(8,128)(2,1)} %bitcast.11, ...), custom_call_target="tpu_custom_call" | custom-call | flops 25769803776 | bytes 33554432 | tf_op jit(solution)/shard_map/beta_term/pallas_call | solution.py:194
  296.7 4.8 %all-to-all-done.2 = s16[8,512,256]{2,1,0:T(8,128)(2,1)S(1)} async-done(((s16[8,512,256]{2,1,0:T(8,128)(2,1)}), s16[8,512,256]{2,1,0:T(8,128)(2,1)S(1)}, u32[]{:S(2)}, u32[]{:S(2)}) %all-to-all-start.2) | async-done | bytes 2097184 | tf_op jit(solution)/shard_map/all_to_all | solution.py:395
  302.8 7.0 %all-to-all-start.3 = ((s16[8,1536,256]{2,1,0:T(8,128)(2,1)}), s16[8,1536,256]{2,1,0:T(8,128)(2,1)}, u32[]{:S(2)}, u32[]{:S(2)}) async-start(s16[8,1536,256]{2,1,0:T(8,128)(2,1)} %beta_term.3), calls=%async_computation.3 | async-start | bytes 12582912 | tf_op jit(solution)/shard_map/all_to_all | solution.py:395
  309.8 4.5 slice.12
  315.1 22.1 %alpha_term.3.refs_4_ = f32[8,2048,256]{2,1,0:T(8,128)} custom-call(s32[256]{0:T(256)} %reshape.27.cols_ref, s32[4]{0:T(128)} %pad_add_fusion.place_ref, bf16[8,2048,256]{2,1,0:T(8,128)(2,1)} %refs_0_.5, bf16[3,2048,256]{2,1,0:T(8,128)(2,1)} %collective-permute-done.6.refs_1_, bf16[16,16,128,128]{3,2,1,0:T(8,128)(2,1)} %refs_2_.5, f32[2048,256]{1,0:T(8,128)} %refs_3_.5), custom_call_target="tpu_custom_call" | custom-call | flops 19327352832 | bytes 23068672 | tf_op jit(solution)/shard_map/alpha_term/pallas_call | solution.py:262
  337.3 11.8 %alpha_term.4.refs_4_ = f32[8,2048,256]{2,1,0:T(8,128)} custom-call(s32[256]{0:T(256)} %reshape.27.cols_ref, s32[4]{0:T(128)} %pad_add_fusion.place_ref, bf16[8,2048,256]{2,1,0:T(8,128)(2,1)} %refs_0_.5, bf16[1,2048,256]{2,1,0:T(8,128)(2,1)} %copy-done.1, bf16[16,16,128,128]{3,2,1,0:T(8,128)(2,1)} %refs_2_.5, ...), custom_call_target="tpu_custom_call", output_to_operand_aliasing={{}: (6, {})} | custom-call | flops 6442450944 | bytes 14680064 | tf_op jit(solution)/shard_map/alpha_term/pallas_call | solution.py:262
  349.0 56.2 %collective-permute-done.4.refs_1_ = bf16[4,2048,256]{2,1,0:T(8,128)(2,1)} collective-permute-done((bf16[4,2048,256]{2,1,0:T(8,128)(2,1)}, bf16[4,2048,256]{2,1,0:T(8,128)(2,1)}, u32[]{:S(2)}, u32[]{:S(2)}) %collective-permute-start.4) | collective-permute-done | bytes 4194336 | tf_op jit(solution)/shard_map/ppermute | solution.py:352
  405.2 27.2 %alpha_term.5.acc_ref = f32[8,2048,256]{2,1,0:T(8,128)} custom-call(s32[256]{0:T(256)} %reshape.27.cols_ref, s32[4]{0:T(128)} %pad_add_fusion.place_ref, bf16[8,2048,256]{2,1,0:T(8,128)(2,1)} %refs_0_.5, bf16[4,2048,256]{2,1,0:T(8,128)(2,1)} %collective-permute-done.4.refs_1_, bf16[16,16,128,128]{3,2,1,0:T(8,128)(2,1)} %refs_2_.5, ...), custom_call_target="tpu_custom_call", output_to_operand_aliasing={{}: (6, {})} | custom-call | flops 25769803776 | bytes 27262976 | tf_op jit(solution)/shard_map/alpha_term/pallas_call | solution.py:262
  432.5 4.4 join_terms.2.rest_0_
  436.8 8.5 %all-to-all-done.3 = s16[8,1536,256]{2,1,0:T(8,128)(2,1)} async-done(((s16[8,1536,256]{2,1,0:T(8,128)(2,1)}), s16[8,1536,256]{2,1,0:T(8,128)(2,1)}, u32[]{:S(2)}, u32[]{:S(2)}) %all-to-all-start.3) | async-done | bytes 6291488 | tf_op jit(solution)/shard_map/all_to_all | solution.py:395
  445.4 10.9 %join_terms.3 = bf16[8,2048,256]{2,1,0:T(8,128)(2,1)} custom-call(f32[8,2048,256]{2,1,0:T(8,128)} %alpha_term.5.acc_ref, s16[8,2,6,128,256]{4,3,2,1,0:T(8,128)(2,1)} %bitcast.5.words_ref, bf16[8,2048,256]{2,1,0:T(8,128)(2,1)} %join_terms.2.rest_0_), custom_call_target="tpu_custom_call", output_to_operand_aliasing={{}: (2, {})} | custom-call | flops 25165824 | bytes 25165824 | tf_op jit(solution)/shard_map/join_terms/pallas_call | solution.py:308
  (31 shorter events, 12.5 us)
Async XLA Ops:
  11.7 90.6 %all-to-all-start = ((bf16[16,272,256]{2,1,0:T(8,128)(2,1)}), bf16[16,272,256]{2,1,0:T(8,128)(2,1)}, u32[]{:S(2)}, u32[]{:S(2)}) async-start(bf16[16,272,256]{2,1,0:T(8,128)(2,1)} %pack_pieces.2), calls=%async_computation | async-start | bytes 4456448 | tf_op jit(solution)/shard_map/all_to_all | solution.py:372
  18.3 84.3 %all-gather.3.cloned.1.call-start = ((), (), s32[]{:S(2)}) async-start(), calls=%async_computation.4 | async-start | bytes 2621440 | tf_op jit(solution)/shard_map/all_gather | solution.py:357
  29.7 74.0 %collective-permute-start.6 = (bf16[3,2048,256]{2,1,0:T(8,128)(2,1)S(1)}, bf16[3,2048,256]{2,1,0:T(8,128)(2,1)}, u32[]{:S(2)}, u32[]{:S(2)}) collective-permute-start(bf16[3,2048,256]{2,1,0:T(8,128)(2,1)S(1)} %slice.14), channel_id=1, source_target_pairs={{16,0},{0,16},{17,1},{1,17},{18,2},{2,18},{19,3},{3,19},{20,4},{4,... | collective-permute-start | bytes 9437192 | tf_op jit(solution)/shard_map/ppermute | solution.py:352
  102.3 65.2 %collective-permute-start.2 = (bf16[16,272,256]{2,1,0:T(8,128)(2,1)}, bf16[16,272,256]{2,1,0:T(8,128)(2,1)}, u32[]{:S(2)}, u32[]{:S(2)}) collective-permute-start(bf16[16,272,256]{2,1,0:T(8,128)(2,1)} %all-to-all-done.refs_0_), channel_id=1, source_target_pairs={{0,1},{1,0},{2,3},{3,2},{4,5},{5,4},{6,7},{7,6},{8,9},{9,8},{10,11... | collective-permute-start | bytes 6684680 | tf_op jit(solution)/shard_map/ppermute | solution.py:345
  102.5 47.2 %collective-permute-start.1 = (bf16[4,2048,128]{2,1,0:T(8,128)(2,1)}, bf16[4,2048,128]{2,1,0:T(8,128)(2,1)}, u32[]{:S(2)}, u32[]{:S(2)}) collective-permute-start(bf16[4,2048,128]{2,1,0:T(8,128)(2,1)} %bitcast.8), channel_id=1, source_target_pairs={{0,16},{16,0},{1,17},{17,1},{2,18},{18,2},{3,19},{19,3},{4,20},{20... | collective-permute-start | bytes 6291464 | tf_op jit(solution)/shard_map/ppermute | solution.py:348
  103.8 63.8 %collective-permute-start = (bf16[4,2048,128]{2,1,0:T(8,128)(2,1)}, bf16[4,2048,128]{2,1,0:T(8,128)(2,1)}, u32[]{:S(2)}, u32[]{:S(2)}) collective-permute-start(bf16[4,2048,128]{2,1,0:T(8,128)(2,1)} %bitcast.9), channel_id=1, source_target_pairs={{0,2},{1,3},{2,0},{3,1},{4,6},{5,7},{6,4},{7,5},{8,10},{9,11},{10,... | collective-permute-start | bytes 6291464 | tf_op jit(solution)/shard_map/ppermute | solution.py:345
  103.8 143.5 %all-to-all-start.1 = ((bf16[16,768,256]{2,1,0:T(8,128)(2,1)}), bf16[16,768,256]{2,1,0:T(8,128)(2,1)}, u32[]{:S(2)}, u32[]{:S(2)}) async-start(bf16[16,768,256]{2,1,0:T(8,128)(2,1)} %pack_pieces.3), calls=%async_computation.1 | async-start | bytes 12582912 | tf_op jit(solution)/shard_map/all_to_all | solution.py:374
  167.5 45.0 %collective-permute-start.3 = (bf16[4,2048,128]{2,1,0:T(8,128)(2,1)}, bf16[4,2048,128]{2,1,0:T(8,128)(2,1)S(1)}, u32[]{:S(2)}, u32[]{:S(2)}) collective-permute-start(bf16[4,2048,128]{2,1,0:T(8,128)(2,1)} %collective-permute-done.refs_4_), channel_id=1, source_target_pairs={{0,16},{16,0},{1,17},{17,1},{2,18},{18,2},{3,19},{19,3},{4,20},{20... | collective-permute-start | bytes 6291464 | tf_op jit(solution)/shard_map/ppermute | solution.py:348
  212.5 1.3 copy-start.3
  247.3 10.9 %collective-permute-start.7 = (bf16[16,768,256]{2,1,0:T(8,128)(2,1)}, bf16[16,768,256]{2,1,0:T(8,128)(2,1)}, u32[]{:S(2)}, u32[]{:S(2)}) collective-permute-start(bf16[16,768,256]{2,1,0:T(8,128)(2,1)} %all-to-all-done.1.refs_0_), channel_id=1, source_target_pairs={{0,1},{1,0},{2,3},{3,2},{4,5},{5,4},{6,7},{7,6},{8,9},{9,8},{10,11... | collective-permute-start | bytes 18874376 | tf_op jit(solution)/shard_map/ppermute | solution.py:345
  247.5 54.0 %all-to-all-start.2 = ((s16[8,512,256]{2,1,0:T(8,128)(2,1)}), s16[8,512,256]{2,1,0:T(8,128)(2,1)S(1)}, u32[]{:S(2)}, u32[]{:S(2)}) async-start(s16[8,512,256]{2,1,0:T(8,128)(2,1)} %beta_term.2), calls=%async_computation.2 | async-start | bytes 4194304 | tf_op jit(solution)/shard_map/all_to_all | solution.py:395
  258.0 38.7 %collective-permute-start.5 = (bf16[1,2048,256]{2,1,0:T(8,128)(2,1)}, bf16[1,2048,256]{2,1,0:T(8,128)(2,1)S(1)}, u32[]{:S(2)}, u32[]{:S(2)}) collective-permute-start(bf16[1,2048,256]{2,1,0:T(8,128)(2,1)} %slice.13), channel_id=1, source_target_pairs={{16,0},{0,16},{17,1},{1,17},{18,2},{2,18},{19,3},{3,19},{20,4},{4,... | collective-permute-start | bytes 3145736 | tf_op jit(solution)/shard_map/ppermute | solution.py:352
  296.7 4.8 %copy-start.1 = (bf16[1,2048,256]{2,1,0:T(8,128)(2,1)}, bf16[1,2048,256]{2,1,0:T(8,128)(2,1)S(1)}, u32[]{:S(2)}) copy-start(bf16[1,2048,256]{2,1,0:T(8,128)(2,1)S(1)} %collective-permute-done.5.refs_1_) | copy-start | bytes 3145732
  301.5 1.3 copy-start
  302.8 142.6 %all-to-all-start.3 = ((s16[8,1536,256]{2,1,0:T(8,128)(2,1)}), s16[8,1536,256]{2,1,0:T(8,128)(2,1)}, u32[]{:S(2)}, u32[]{:S(2)}) async-start(s16[8,1536,256]{2,1,0:T(8,128)(2,1)} %beta_term.3), calls=%async_computation.3 | async-start | bytes 12582912 | tf_op jit(solution)/shard_map/all_to_all | solution.py:395
  309.8 4.7 %copy-start.2 = (s32[16,16]{1,0:T(8,128)S(1)}, s32[16,16]{1,0:T(8,128)}, u32[]{:S(2)}) copy-start(s32[16,16]{1,0:T(8,128)} %param.8) | copy-start | bytes 3076
  314.3 91.0 %collective-permute-start.4 = (bf16[4,2048,256]{2,1,0:T(8,128)(2,1)}, bf16[4,2048,256]{2,1,0:T(8,128)(2,1)}, u32[]{:S(2)}, u32[]{:S(2)}) collective-permute-start(bf16[4,2048,256]{2,1,0:T(8,128)(2,1)} %slice.12), channel_id=1, source_target_pairs={{16,0},{0,16},{17,1},{1,17},{18,2},{2,18},{19,3},{3,19},{20,4},{4,... | collective-permute-start | bytes 12582920 | tf_op jit(solution)/shard_map/ppermute | solution.py:352
Sparse Core Ops, SparseCore 0:
  21.8 74.8 all-gather.2

commit v12 on v10

--- a/solution.py
+++ b/solution.py
@@ -286,7 +286,9 @@
     for j in range(words_ref.shape[0]):
         for c in range(CORES):
             here = pl.ds((j * CORES + c) * few_rows, few_rows)
-            out_ref[0, here, :] = (acc_ref[0, here, :] + from_words(words_ref[j, c, 0], weights)).astype(jnp.bfloat16)
+            for v in range(out_ref.shape[0]):
+                part = from_words(words_ref[j, c, v], weights)
+                out_ref[v, here, :] = (acc_ref[v, here, :] + part).astype(jnp.bfloat16)
 
 
 def join(acc, words, first, vectors, before):
@@ -295,9 +297,10 @@
     few_rows = rows // (sources * CORES)
     words = words.reshape(sources, CORES, -1, few_rows, strip)
     count = words.shape[2]
+    step = 2 if first % 2 == 0 and count % 2 == 0 else 1
     in_specs = [
-        pl.BlockSpec((1, rows, strip), lambda v: (first + v, 0, 0)),
-        pl.BlockSpec((sources, CORES, 1, few_rows, strip), lambda v: (0, 0, v, 0, 0)),
+        pl.BlockSpec((step, rows, strip), lambda v: (first // step + v, 0, 0)),
+        pl.BlockSpec((sources, CORES, step, few_rows, strip), lambda v: (0, 0, v, 0, 0)),
     ]
     args = [acc, words]
     aliases = {}
@@ -307,9 +310,9 @@
         aliases = {2: 0}
     return pl.pallas_call(
         functools.partial(join_kernel, few_rows),
-        grid=(count,),
+        grid=(count // step,),
         in_specs=in_specs,
-        out_specs=pl.BlockSpec((1, rows, strip), lambda v: (first + v, 0, 0)),
+        out_specs=pl.BlockSpec((step, rows, strip), lambda v: (first // step + v, 0, 0)),
         out_shape=jax.ShapeDtypeStruct((vectors, rows, strip), jnp.bfloat16),
         input_output_aliases=aliases,
         compiler_params=pltpu.CompilerParams(vmem_limit_bytes=VMEM),

time: 468 us -> 468 us (level)
  no operation moved by 1% of the time
where the time goes in v12:
time: 468 us; the launch traced here: 463 us
  waiting for transfers between devices  257 us (55%)
  Pallas kernels  146 us (31%)
  starting transfers between devices  30.8 us (7%)
  local copies, waits for them, and re-layouts  13.5 us (3%)
  between operations  13.5 us (3%)
    ppermute x2, waiting for transfers between devices, across(): return lax.ppermute(value, 'alpha', [(i, i ^ 1) for i in range(ring_a)])  80.1 us
    all_to_all x1, waiting for transfers between devices, shards(): lax.all_to_all(packed[0], 'beta', split_axis=0, concat_axis=0, tiled=True)  64.9 us
    pallas_call x3, Pallas kernels, alpha_term(): pl.pallas_call(functools.partial(alpha_kernel, pieces), grid_spec=pltpu.P...  61.2 us
    ppermute x3, waiting for transfers between devices, exchange(): lax.ppermute(value, 'alpha', [((i + s) % ring_a, i) for i in range(ring_a)])  56.9 us
    pallas_call x2, Pallas kernels, beta_term(): pl.pallas_call(functools.partial(beta_kernel, slots, xs, segments, pieces...  55.9 us
    ppermute x3, waiting for transfers between devices, swap(): return lax.ppermute(value, 'beta', [(i, i ^ bit) for i in range(ring)])  21.2 us
    all_to_all x1, waiting for transfers between devices, shards(): lax.all_to_all(second, 'beta', split_axis=0, concat_axis=0, tiled=True)  20.4 us
    pallas_call x2, Pallas kernels, join(): pl.pallas_call(functools.partial(join_kernel, few_rows), grid=(count // s...  16.3 us
  transfers between devices with their start and end apart: 13, of which 10 were waited for; matrix products, arithmetic and copies ran while one was open for 2% of the time, Pallas kernels for 28%

profile of v12, /device:TPU:11, one launch (start us, length us, event | category | flops | bytes accessed | tf_op | source)
XLA Modules:
  0.0 462.9 jit_solution(18362903247387478335)
XLA Ops:
  7.9 3.8 pack_pieces.2
  11.7 6.6 %all-to-all-start = ((bf16[16,272,256]{2,1,0:T(8,128)(2,1)}), bf16[16,272,256]{2,1,0:T(8,128)(2,1)}, u32[]{:S(2)}, u32[]{:S(2)}) async-start(bf16[16,272,256]{2,1,0:T(8,128)(2,1)} %pack_pieces.2), calls=%async_computation | async-start | bytes 4456448 | tf_op jit(solution)/shard_map/all_to_all | solution.py:375
  18.9 2.7 turn_blocks.1
  21.7 2.3 slice.13
  26.0 4.4 slice.12
  30.4 6.0 %pack_pieces.3 = bf16[16,768,256]{2,1,0:T(8,128)(2,1)} custom-call(bf16[8,2048,256]{2,1,0:T(8,128)(2,1)} %refs_0_.5), custom_call_target="tpu_custom_call" | custom-call | bytes 12582912 | tf_op jit(solution)/shard_map/pack_pieces/pallas_call | solution.py:79
  37.7 64.9 %all-to-all-done.refs_0_ = bf16[16,272,256]{2,1,0:T(8,128)(2,1)} async-done(((bf16[16,272,256]{2,1,0:T(8,128)(2,1)}), bf16[16,272,256]{2,1,0:T(8,128)(2,1)}, u32[]{:S(2)}, u32[]{:S(2)}) %all-to-all-start) | async-done | bytes 2228256 | tf_op jit(solution)/shard_map/all_to_all | solution.py:375
  105.9 7.6 %all-to-all-start.1 = ((bf16[16,768,256]{2,1,0:T(8,128)(2,1)}), bf16[16,768,256]{2,1,0:T(8,128)(2,1)}, u32[]{:S(2)}, u32[]{:S(2)}) async-start(bf16[16,768,256]{2,1,0:T(8,128)(2,1)} %pack_pieces.3), calls=%async_computation.1 | async-start | bytes 12582912 | tf_op jit(solution)/shard_map/all_to_all | solution.py:377
  113.5 37.3 %collective-permute-done.1.refs_3_ = bf16[4,2048,128]{2,1,0:T(8,128)(2,1)} collective-permute-done((bf16[4,2048,128]{2,1,0:T(8,128)(2,1)}, bf16[4,2048,128]{2,1,0:T(8,128)(2,1)}, u32[]{:S(2)}, u32[]{:S(2)}) %collective-permute-start.1) | collective-permute-done | bytes 2097184 | tf_op jit(solution)/shard_map/ppermute | solution.py:351
  150.8 16.6 %collective-permute-done.refs_4_ = bf16[4,2048,128]{2,1,0:T(8,128)(2,1)} collective-permute-done((bf16[4,2048,128]{2,1,0:T(8,128)(2,1)}, bf16[4,2048,128]{2,1,0:T(8,128)(2,1)}, u32[]{:S(2)}, u32[]{:S(2)}) %collective-permute-start) | collective-permute-done | bytes 2097184 | tf_op jit(solution)/shard_map/ppermute | solution.py:348
  169.1 42.8 %collective-permute-done.3.refs_5_ = bf16[4,2048,128]{2,1,0:T(8,128)(2,1)S(1)} collective-permute-done((bf16[4,2048,128]{2,1,0:T(8,128)(2,1)}, bf16[4,2048,128]{2,1,0:T(8,128)(2,1)S(1)}, u32[]{:S(2)}, u32[]{:S(2)}) %collective-permute-start.3) | collective-permute-done | bytes 2097184 | tf_op jit(solution)/shard_map/ppermute | solution.py:351
  213.2 17.4 %beta_term.2 = s16[8,512,256]{2,1,0:T(8,128)(2,1)} custom-call(s32[512]{0:T(512)} %reshape.30.cols_ref, s32[4]{0:T(128)} %pad_add_fusion.place_ref, bf16[16,272,256]{2,1,0:T(8,128)(2,1)} %all-to-all-done.refs_0_, bf16[16,272,256]{2,1,0:T(8,128)(2,1)} %collective-permute-done.2.refs_1_, bf16[4,2048,128]{2,1,0:T(8,128)(2,1)} %bitcast.10, ...), custom_call_target="tpu_custom_call" | custom-call | flops 90194313216 | bytes 16777216 | tf_op jit(solution)/shard_map/beta_term/pallas_call | solution.py:194
  230.6 20.4 %all-to-all-done.1.refs_0_ = bf16[16,768,256]{2,1,0:T(8,128)(2,1)} async-done(((bf16[16,768,256]{2,1,0:T(8,128)(2,1)}), bf16[16,768,256]{2,1,0:T(8,128)(2,1)}, u32[]{:S(2)}, u32[]{:S(2)}) %all-to-all-start.1) | async-done | bytes 6291488 | tf_op jit(solution)/shard_map/all_to_all | solution.py:377
  251.2 4.4 all-to-all-start.2
  256.9 4.6 collective-permute-done.7.refs_1_
  261.5 38.4 %beta_term.3 = s16[8,1536,256]{2,1,0:T(8,128)(2,1)} custom-call(s32[512]{0:T(512)} %reshape.30.cols_ref, s32[4]{0:T(128)} %pad_add_fusion.place_ref, bf16[16,768,256]{2,1,0:T(8,128)(2,1)} %all-to-all-done.1.refs_0_, bf16[16,768,256]{2,1,0:T(8,128)(2,1)} %collective-permute-done.7.refs_1_, bf16[4,2048,128]{2,1,0:T(8,128)(2,1)} %bitcast.11, ...), custom_call_target="tpu_custom_call" | custom-call | flops 25769803776 | bytes 33554432 | tf_op jit(solution)/shard_map/beta_term/pallas_call | solution.py:194
  302.7 6.8 %all-to-all-start.3 = ((s16[8,1536,256]{2,1,0:T(8,128)(2,1)}), s16[8,1536,256]{2,1,0:T(8,128)(2,1)}, u32[]{:S(2)}, u32[]{:S(2)}) async-start(s16[8,1536,256]{2,1,0:T(8,128)(2,1)} %beta_term.3), calls=%async_computation.3 | async-start | bytes 12582912 | tf_op jit(solution)/shard_map/all_to_all | solution.py:398
  311.4 22.1 %alpha_term.3.refs_4_ = f32[8,2048,256]{2,1,0:T(8,128)} custom-call(s32[256]{0:T(256)} %reshape.27.cols_ref, s32[4]{0:T(128)} %pad_add_fusion.place_ref, bf16[8,2048,256]{2,1,0:T(8,128)(2,1)} %refs_0_.5, bf16[3,2048,256]{2,1,0:T(8,128)(2,1)} %collective-permute-done.6.refs_1_, bf16[16,16,128,128]{3,2,1,0:T(8,128)(2,1)} %refs_2_.5, f32[2048,256]{1,0:T(8,128)} %refs_3_.5), custom_call_target="tpu_custom_call" | custom-call | flops 19327352832 | bytes 23068672 | tf_op jit(solution)/shard_map/alpha_term/pallas_call | solution.py:262
  333.6 11.8 %alpha_term.4.refs_4_ = f32[8,2048,256]{2,1,0:T(8,128)} custom-call(s32[256]{0:T(256)} %reshape.27.cols_ref, s32[4]{0:T(128)} %pad_add_fusion.place_ref, bf16[8,2048,256]{2,1,0:T(8,128)(2,1)} %refs_0_.5, bf16[1,2048,256]{2,1,0:T(8,128)(2,1)} %copy-done.1, bf16[16,16,128,128]{3,2,1,0:T(8,128)(2,1)} %refs_2_.5, ...), custom_call_target="tpu_custom_call", output_to_operand_aliasing={{}: (6, {})} | custom-call | flops 6442450944 | bytes 14680064 | tf_op jit(solution)/shard_map/alpha_term/pallas_call | solution.py:262
  345.3 54.9 %collective-permute-done.4.refs_1_ = bf16[4,2048,256]{2,1,0:T(8,128)(2,1)} collective-permute-done((bf16[4,2048,256]{2,1,0:T(8,128)(2,1)}, bf16[4,2048,256]{2,1,0:T(8,128)(2,1)}, u32[]{:S(2)}, u32[]{:S(2)}) %collective-permute-start.4) | collective-permute-done | bytes 4194336 | tf_op jit(solution)/shard_map/ppermute | solution.py:355
  400.2 27.3 %alpha_term.5.acc_ref = f32[8,2048,256]{2,1,0:T(8,128)} custom-call(s32[256]{0:T(256)} %reshape.27.cols_ref, s32[4]{0:T(128)} %pad_add_fusion.place_ref, bf16[8,2048,256]{2,1,0:T(8,128)(2,1)} %refs_0_.5, bf16[4,2048,256]{2,1,0:T(8,128)(2,1)} %collective-permute-done.4.refs_1_, bf16[16,16,128,128]{3,2,1,0:T(8,128)(2,1)} %refs_2_.5, ...), custom_call_target="tpu_custom_call", output_to_operand_aliasing={{}: (6, {})} | custom-call | flops 25769803776 | bytes 27262976 | tf_op jit(solution)/shard_map/alpha_term/pallas_call | solution.py:262
  427.5 5.4 %join_terms.2.rest_0_ = bf16[8,2048,256]{2,1,0:T(8,128)(2,1)} custom-call(f32[8,2048,256]{2,1,0:T(8,128)} %alpha_term.5.acc_ref, s16[8,2,2,128,256]{4,3,2,1,0:T(8,128)(2,1)} %bitcast.7), custom_call_target="tpu_custom_call" | custom-call | flops 8388608 | bytes 8388608 | tf_op jit(solution)/shard_map/join_terms/pallas_call | solution.py:311
  432.8 12.3 %all-to-all-done.3 = s16[8,1536,256]{2,1,0:T(8,128)(2,1)} async-done(((s16[8,1536,256]{2,1,0:T(8,128)(2,1)}), s16[8,1536,256]{2,1,0:T(8,128)(2,1)}, u32[]{:S(2)}, u32[]{:S(2)}) %all-to-all-start.3) | async-done | bytes 6291488 | tf_op jit(solution)/shard_map/all_to_all | solution.py:398
  445.1 11.0 %join_terms.3 = bf16[8,2048,256]{2,1,0:T(8,128)(2,1)} custom-call(f32[8,2048,256]{2,1,0:T(8,128)} %alpha_term.5.acc_ref, s16[8,2,6,128,256]{4,3,2,1,0:T(8,128)(2,1)} %bitcast.5.words_ref, bf16[8,2048,256]{2,1,0:T(8,128)(2,1)} %join_terms.2.rest_0_), custom_call_target="tpu_custom_call", output_to_operand_aliasing={{}: (2, {})} | custom-call | flops 25165824 | bytes 25165824 | tf_op jit(solution)/shard_map/join_terms/pallas_call | solution.py:311
  (31 shorter events, 17.7 us)
Async XLA Ops:
  11.7 90.9 %all-to-all-start = ((bf16[16,272,256]{2,1,0:T(8,128)(2,1)}), bf16[16,272,256]{2,1,0:T(8,128)(2,1)}, u32[]{:S(2)}, u32[]{:S(2)}) async-start(bf16[16,272,256]{2,1,0:T(8,128)(2,1)} %pack_pieces.2), calls=%async_computation | async-start | bytes 4456448 | tf_op jit(solution)/shard_map/all_to_all | solution.py:375
  18.3 84.3 %all-gather.3.cloned.1.call-start = ((), (), s32[]{:S(2)}) async-start(), calls=%async_computation.4 | async-start | bytes 2621440 | tf_op jit(solution)/shard_map/all_gather | solution.py:360
  36.4 69.4 %collective-permute-start.6 = (bf16[3,2048,256]{2,1,0:T(8,128)(2,1)S(1)}, bf16[3,2048,256]{2,1,0:T(8,128)(2,1)}, u32[]{:S(2)}, u32[]{:S(2)}) collective-permute-start(bf16[3,2048,256]{2,1,0:T(8,128)(2,1)S(1)} %slice.14), channel_id=1, source_target_pairs={{16,0},{0,16},{17,1},{1,17},{18,2},{2,18},{19,3},{3,19},{20,4},{4,... | collective-permute-start | bytes 9437192 | tf_op jit(solution)/shard_map/ppermute | solution.py:355
  102.6 64.8 %collective-permute-start.2 = (bf16[16,272,256]{2,1,0:T(8,128)(2,1)}, bf16[16,272,256]{2,1,0:T(8,128)(2,1)}, u32[]{:S(2)}, u32[]{:S(2)}) collective-permute-start(bf16[16,272,256]{2,1,0:T(8,128)(2,1)} %all-to-all-done.refs_0_), channel_id=1, source_target_pairs={{0,1},{1,0},{2,3},{3,2},{4,5},{5,4},{6,7},{7,6},{8,9},{9,8},{10,11... | collective-permute-start | bytes 6684680 | tf_op jit(solution)/shard_map/ppermute | solution.py:348
  102.6 48.2 %collective-permute-start.1 = (bf16[4,2048,128]{2,1,0:T(8,128)(2,1)}, bf16[4,2048,128]{2,1,0:T(8,128)(2,1)}, u32[]{:S(2)}, u32[]{:S(2)}) collective-permute-start(bf16[4,2048,128]{2,1,0:T(8,128)(2,1)} %bitcast.8), channel_id=1, source_target_pairs={{0,16},{16,0},{1,17},{17,1},{2,18},{18,2},{3,19},{19,3},{4,20},{20... | collective-permute-start | bytes 6291464 | tf_op jit(solution)/shard_map/ppermute | solution.py:351
  103.9 63.5 %collective-permute-start = (bf16[4,2048,128]{2,1,0:T(8,128)(2,1)}, bf16[4,2048,128]{2,1,0:T(8,128)(2,1)}, u32[]{:S(2)}, u32[]{:S(2)}) collective-permute-start(bf16[4,2048,128]{2,1,0:T(8,128)(2,1)} %bitcast.9), channel_id=1, source_target_pairs={{0,2},{1,3},{2,0},{3,1},{4,6},{5,7},{6,4},{7,5},{8,10},{9,11},{10,... | collective-permute-start | bytes 6291464 | tf_op jit(solution)/shard_map/ppermute | solution.py:348
  105.9 145.2 %all-to-all-start.1 = ((bf16[16,768,256]{2,1,0:T(8,128)(2,1)}), bf16[16,768,256]{2,1,0:T(8,128)(2,1)}, u32[]{:S(2)}, u32[]{:S(2)}) async-start(bf16[16,768,256]{2,1,0:T(8,128)(2,1)} %pack_pieces.3), calls=%async_computation.1 | async-start | bytes 12582912 | tf_op jit(solution)/shard_map/all_to_all | solution.py:377
  167.4 44.5 %collective-permute-start.3 = (bf16[4,2048,128]{2,1,0:T(8,128)(2,1)}, bf16[4,2048,128]{2,1,0:T(8,128)(2,1)S(1)}, u32[]{:S(2)}, u32[]{:S(2)}) collective-permute-start(bf16[4,2048,128]{2,1,0:T(8,128)(2,1)} %collective-permute-done.refs_4_), channel_id=1, source_target_pairs={{0,16},{16,0},{1,17},{17,1},{2,18},{18,2},{3,19},{19,3},{4,20},{20... | collective-permute-start | bytes 6291464 | tf_op jit(solution)/shard_map/ppermute | solution.py:351
  211.9 1.3 copy-start.3
  251.0 10.5 %collective-permute-start.7 = (bf16[16,768,256]{2,1,0:T(8,128)(2,1)}, bf16[16,768,256]{2,1,0:T(8,128)(2,1)}, u32[]{:S(2)}, u32[]{:S(2)}) collective-permute-start(bf16[16,768,256]{2,1,0:T(8,128)(2,1)} %all-to-all-done.1.refs_0_), channel_id=1, source_target_pairs={{0,1},{1,0},{2,3},{3,2},{4,5},{5,4},{6,7},{7,6},{8,9},{9,8},{10,11... | collective-permute-start | bytes 18874376 | tf_op jit(solution)/shard_map/ppermute | solution.py:348
  251.2 50.2 %all-to-all-start.2 = ((s16[8,512,256]{2,1,0:T(8,128)(2,1)}), s16[8,512,256]{2,1,0:T(8,128)(2,1)S(1)}, u32[]{:S(2)}, u32[]{:S(2)}) async-start(s16[8,512,256]{2,1,0:T(8,128)(2,1)} %beta_term.2), calls=%async_computation.2 | async-start | bytes 4194304 | tf_op jit(solution)/shard_map/all_to_all | solution.py:398
  255.7 44.3 %collective-permute-start.5 = (bf16[1,2048,256]{2,1,0:T(8,128)(2,1)}, bf16[1,2048,256]{2,1,0:T(8,128)(2,1)S(1)}, u32[]{:S(2)}, u32[]{:S(2)}) collective-permute-start(bf16[1,2048,256]{2,1,0:T(8,128)(2,1)} %slice.13), channel_id=1, source_target_pairs={{16,0},{0,16},{17,1},{1,17},{18,2},{2,18},{19,3},{3,19},{20,4},{4,... | collective-permute-start | bytes 3145736 | tf_op jit(solution)/shard_map/ppermute | solution.py:355
  300.0 10.7 %copy-start.2 = (s32[16,16]{1,0:T(8,128)S(1)}, s32[16,16]{1,0:T(8,128)}, u32[]{:S(2)}) copy-start(s32[16,16]{1,0:T(8,128)} %param.8) | copy-start | bytes 3076
  300.0 1.4 copy-start.1
  301.4 1.3 copy-start
  302.7 142.3 %all-to-all-start.3 = ((s16[8,1536,256]{2,1,0:T(8,128)(2,1)}), s16[8,1536,256]{2,1,0:T(8,128)(2,1)}, u32[]{:S(2)}, u32[]{:S(2)}) async-start(s16[8,1536,256]{2,1,0:T(8,128)(2,1)} %beta_term.3), calls=%async_computation.3 | async-start | bytes 12582912 | tf_op jit(solution)/shard_map/all_to_all | solution.py:398
  309.5 90.7 %collective-permute-start.4 = (bf16[4,2048,256]{2,1,0:T(8,128)(2,1)}, bf16[4,2048,256]{2,1,0:T(8,128)(2,1)}, u32[]{:S(2)}, u32[]{:S(2)}) collective-permute-start(bf16[4,2048,256]{2,1,0:T(8,128)(2,1)} %slice.12), channel_id=1, source_target_pairs={{16,0},{0,16},{17,1},{1,17},{18,2},{2,18},{19,3},{3,19},{20,4},{4,... | collective-permute-start | bytes 12582920 | tf_op jit(solution)/shard_map/ppermute | solution.py:355
Sparse Core Ops, SparseCore 0:
  21.8 74.9 all-gather.2
